TPU v7x, 32 devices: a whole 2x2x4 slice. The times are simulated.
32 devices in a mesh: grp: 2 (over y), seq: 16 (over z, x, core).
Axes of the slice: x: 2, y: 2, z: 4, core: 2. Of those that a mesh axis runs over, the one named last changes fastest.
Arguments:
- queries: bfloat16 [4096, 4096], P(('grp', 'seq')), parts along dimension 0, may hold values from -4.5 to 4.5
- kv_pool: bfloat16 [288, 8, 1024], P(('grp', 'seq')), parts along dimension 0, may hold values from -4.5 to 4.5
- span_lengths: int32 [32], P('grp'), parts along dimension 0, may hold values from 0 to 128, as said below
- owner_branch: int32 [32], P('grp'), parts along dimension 0, may hold values from 0 to 15, as said below
- prefix_table: int32 [256], P('grp'), parts along dimension 0, may hold values from 0 to 143, as said below
- branch_table: int32 [32, 1], P('grp'), parts along dimension 0, may hold values from 0 to 143, as said below
Outputs:
- attended: bfloat16 [4096, 4096], P(('grp', 'seq')), parts along dimension 0
There are 2 independent parts, one for each index of `grp`. A program takes and returns all parts, laid end to end along the dimension named above; each array names one. Nothing has to cross between parts.
Inputs may be any that keep to these rules, and one draw needn't show every extreme that they name: `span_lengths`: the span lengths sum to 1024, and some branch has exactly 128 rows. `owner_branch`: A permutation of the branches. `prefix_table`: together with branch_table it names every page of the pool exactly once. `branch_table`: together with prefix_table it names every page of the pool exactly once.
All inputs are finite; a program needn't handle non-finite values.
Results may differ from a plain program's by a relative error of at most 0.008.
Values may be sent and summed in bfloat16 or wider, within the bound.
No kernel may reach another device: no remote copies, remote signals or barrier semaphores. Data moves between devices by JAX's collectives and lax.ppermute only.
A program may use at most 128 MiB of HBM per device.

v0:
```python
import math

import jax
import jax.numpy as jnp
from jax import lax
from jax.sharding import PartitionSpec as P

QH = 32
KVH = 4
HD = 128


def page_owners(prefix_table, branch_table, pool_size):
    page_ids = jnp.arange(pool_size, dtype=jnp.int32)
    is_prefix = jnp.any(prefix_table[:, None] == page_ids[None, :], 0)
    flat_table = branch_table.reshape(-1)
    table_branch = jnp.arange(flat_table.shape[0], dtype=jnp.int32) // branch_table.shape[1]
    owner_of = jnp.sum(
        jnp.where(flat_table[:, None] == page_ids[None, :], table_branch[:, None], 0), 0
    )
    return jnp.where(is_prefix, -1, owner_of)


def absorb(carry, query_heads, rows_branch, pages, block_owner):
    run_max, run_total, run_acc = carry
    page_tokens = pages.shape[1]
    token_count = pages.shape[0] * page_tokens
    kv_tokens = pages.reshape(token_count, 2, KVH, HD)
    keys = kv_tokens[:, 0]
    values = kv_tokens[:, 1]
    scores = jnp.einsum("rkgd,tkd->rkgt", query_heads, keys, preferred_element_type=jnp.float32) * (
        1.0 / math.sqrt(HD)
    )
    token_owner = jnp.repeat(block_owner, page_tokens)
    allowed = (token_owner[None, :] < 0) | (token_owner[None, :] == rows_branch[:, None])
    allowed = allowed[:, None, None, :]
    masked = jnp.where(allowed, scores, -1e30)
    new_max = jnp.maximum(run_max, jnp.max(masked, -1))
    weights = jnp.where(allowed, jnp.exp(scores - new_max[..., None]), 0.0).astype(jnp.bfloat16)
    factor = jnp.exp(run_max - new_max)
    new_total = run_total * factor + jnp.sum(weights.astype(jnp.float32), -1)
    new_acc = run_acc * factor[..., None] + jnp.einsum(
        "rkgt,tkd->rkgd", weights, values, preferred_element_type=jnp.float32
    )
    return (new_max, new_total, new_acc)


def fold_pages(carry, query_heads, rows_branch, pages, owners):
    row_count = query_heads.shape[0]
    page_tokens = pages.shape[1]
    piece_pages = pages.shape[0]
    block_pages = max(1, max(128, 32768 // row_count) // page_tokens)
    while piece_pages % block_pages:
        block_pages = block_pages - 1
    block_count = piece_pages // block_pages
    blocks = pages.reshape((block_count, block_pages) + pages.shape[1:])
    block_owners = owners.reshape(block_count, block_pages)

    def scan_step(state, inputs):
        block, owner_block = inputs
        return (absorb(state, query_heads, rows_branch, block, owner_block), None)

    result, unused = lax.scan(scan_step, carry, (blocks, block_owners))
    return result


def start_state(row_count):
    head_group = QH // KVH
    return (
        jnp.full((row_count, KVH, head_group), -1e30, jnp.float32),
        jnp.zeros((row_count, KVH, head_group), jnp.float32),
        jnp.zeros((row_count, KVH, head_group, HD), jnp.float32),
    )


def finish(state):
    run_max, run_total, run_acc = state
    mixed = run_acc / run_total[..., None]
    return mixed.reshape(mixed.shape[0], QH * HD).astype(jnp.bfloat16)


def heads_of(rows_query):
    return rows_query.reshape(rows_query.shape[0], KVH, QH // KVH, HD)


def fold_function(query_heads, rows_branch, slot_branch, carry, piece):
    return fold_pages(carry, query_heads, rows_branch, piece, slot_branch)


def prepare_send(queries, devices, my_base, my_used):
    capacity = queries.shape[0]
    device_count = devices.shape[0]
    per_peer = capacity // device_count
    slot_steps = jnp.arange(per_peer, dtype=jnp.int32)
    send_rows = (devices[:, None] - my_base) % device_count + slot_steps[None, :] * device_count
    send_live = send_rows < my_used
    outgoing = jnp.where(send_live[..., None], queries[jnp.minimum(send_rows, capacity - 1)], 0.0)
    return (outgoing, send_rows, send_live)


def place_received(incoming, self_index, dev_base, dev_used, dev_branch, capacity):
    device_count = dev_base.shape[0]
    features = incoming.shape[-1]
    per_peer = capacity // device_count
    rows_here = capacity // 2
    slot_steps = jnp.arange(per_peer, dtype=jnp.int32)
    recv_rows = (self_index - dev_base[:, None]) % device_count + slot_steps[None, :] * device_count
    recv_live = recv_rows < dev_used[:, None]
    dense_slot = jnp.where(recv_live, (dev_base[:, None] + recv_rows) // device_count, rows_here)
    flat_slot = dense_slot.reshape(-1)
    dense_query = (
        jnp.zeros((rows_here, features), jnp.bfloat16)
        .at[flat_slot]
        .set(incoming.reshape(-1, features), mode="drop")
    )
    source_branch = jnp.broadcast_to(dev_branch[:, None], dense_slot.shape).reshape(-1)
    dense_branch = jnp.zeros((rows_here,), jnp.int32).at[flat_slot].set(source_branch, mode="drop")
    return (dense_query, dense_branch, dense_slot, recv_live)


def pack_back(dense_out, dense_slot, recv_live):
    rows_here = dense_out.shape[0]
    return jnp.where(recv_live[..., None], dense_out[jnp.minimum(dense_slot, rows_here - 1)], 0.0)


def unpack_returned(returned, send_rows, send_live, capacity):
    features = returned.shape[-1]
    owner_slot = jnp.where(send_live, send_rows, capacity).reshape(-1)
    return (
        jnp.zeros((capacity, features), jnp.bfloat16)
        .at[owner_slot]
        .set(returned.reshape(-1, features), mode="drop")
    )


def per_device(queries, kv_pool, span_lengths, owner_branch, prefix_table, branch_table):
    device_count = lax.axis_size("seq")
    self_index = lax.axis_index("seq")
    capacity = queries.shape[0]
    branch_count = span_lengths.shape[0]
    owner_width = device_count // branch_count
    pages_dev = kv_pool.shape[0]
    pool_size = pages_dev * device_count
    slot_branch = page_owners(prefix_table, branch_table, pool_size)
    devices = jnp.arange(device_count, dtype=jnp.int32)
    branch_ids = jnp.arange(branch_count, dtype=jnp.int32)
    group_match = devices[:, None] // owner_width == branch_ids[None, :]
    dev_branch = jnp.sum(jnp.where(group_match, owner_branch[None, :], 0), 1)
    dev_length = jnp.sum(
        jnp.where(dev_branch[:, None] == branch_ids[None, :], span_lengths[None, :], 0), 1
    )
    dev_used = jnp.clip(dev_length - devices % owner_width * capacity, 0, capacity)
    dev_base = jnp.cumsum(dev_used) - dev_used
    is_self = devices == self_index
    my_used = jnp.sum(jnp.where(is_self, dev_used, 0))
    my_base = jnp.sum(jnp.where(is_self, dev_base, 0))
    outgoing, send_rows, send_live = prepare_send(queries, devices, my_base, my_used)
    incoming = lax.all_to_all(outgoing, "seq", split_axis=0, concat_axis=0, tiled=True)
    dense_query, dense_branch, dense_slot, recv_live = place_received(
        incoming, self_index, dev_base, dev_used, dev_branch, capacity
    )
    query_heads = heads_of(dense_query)
    state = fold_function(
        query_heads,
        dense_branch,
        slot_branch,
        start_state(dense_query.shape[0]),
        lax.all_gather(kv_pool, "seq", axis=0, tiled=True),
    )
    going_back = pack_back(finish(state), dense_slot, recv_live)
    returned = lax.all_to_all(going_back, "seq", split_axis=0, concat_axis=0, tiled=True)
    attended = unpack_returned(returned, send_rows, send_live, capacity)
    return attended


def solution(mesh):
    return jax.shard_map(
        per_device,
        mesh=mesh,
        in_specs=(
            P(("grp", "seq"), None),
            P(("grp", "seq"), None, None),
            P("grp"),
            P("grp"),
            P("grp"),
            P("grp", None),
        ),
        out_specs=P(("grp", "seq"), None),
        check_vma=False,
    )
```

profile of v0, /device:TPU:0, one launch (start us, length us, event | category | flops | bytes accessed | tf_op | source)
XLA Modules:
  0.0 122.9 jit_solution(575548253953638656)
XLA Ops:
  6.5 0.7 all-gather.2.cloned.1.call-update
  7.3 0.8 select_reduce_fusion.2
  8.0 0.8 select_reduce_fusion.1
  8.9 0.6 broadcast_clamp_fusion
  9.6 0.1 reduce
  9.8 0.6 fusion.26
  10.4 0.7 and_select_fusion.2
  11.3 1.2 gather_fusion
  12.5 0.6 broadcast_compare_fusion.1
  13.1 1.1 bitcast_select_fusion.2
  14.2 7.4 %all-to-all-start = ((bf16[16,8,4096]{2,1,0:T(8,128)(2,1)}), bf16[16,8,4096]{2,1,0:T(8,128)(2,1)S(1)}, u32[]{:S(2)}, u32[]{:S(2)}) async-start(bf16[16,8,4096]{2,1,0:T(8,128)(2,1)} %bitcast_select_fusion.2), calls=%async_computation | async-start | bytes 2097152 | tf_op jit(solution)/shard_map/all_to_all | solution.py:158
  21.6 0.1 fusion.16
  22.5 1.0 scatter_custom_fusion
  23.5 25.0 %all-to-all-done = bf16[16,8,4096]{2,1,0:T(8,128)(2,1)S(1)} async-done(((bf16[16,8,4096]{2,1,0:T(8,128)(2,1)}), bf16[16,8,4096]{2,1,0:T(8,128)(2,1)S(1)}, u32[]{:S(2)}, u32[]{:S(2)}) %all-to-all-start) | async-done | bytes 1048608 | tf_op jit(solution)/shard_map/all_to_all | solution.py:158
  48.5 2.1 %scatter_custom_fusion.1 = bf16[64,4096]{1,0:T(8,128)(2,1)S(1)} fusion(s32[128]{0:T(128)S(1)} %fusion.31, bf16[16,8,4096]{2,1,0:T(8,128)(2,1)S(1)} %all-to-all-done, bf16[]{:T(256)} %constant.114.clone.1), kind=kCustom, calls=%fused_computation.31 | custom fusion | bytes 1572866 | tf_op jit(solution)/shard_map/scatter | solution.py:114
  50.7 0.2 copy.22
  50.9 11.8 %all-gather.2.cloned.1.call-done = bf16[144,8,1024]{2,1,0:T(8,128)(2,1)} async-done(((bf16[9,8,1024]{2,1,0:T(8,128)(2,1)}), bf16[144,8,1024]{2,1,0:T(8,128)(2,1)}) %all-gather.2.cloned.1.call-update) | async-done | bytes 2359312 | tf_op jit(solution)/shard_map/all_gather | solution.py:168
  62.8 19.3 %while.15 = (s32[]{:T(128)}, f32[64,4,8]{0,2,1:T(8,128)S(1)}, f32[64,4,8]{0,2,1:T(8,128)S(1)}, f32[64,4,8,128]{3,0,2,1:T(8,128)}, s32[3,48]{1,0:T(4,128)S(1)}, /...) while((s32[]{:T(128)}, f32[64,4,8]{0,2,1:T(8,128)S(1)}, ...), condition=%wide.region_12.13_spmd.clone, body=%wide.region_9.12_spmd.clone.sunk | while | flops 413723008 | bytes 26191096 | solution.py:63
  63.0 1.2 constant_dynamic-slice_fusion.2
  64.2 0.6 reshape.651
  64.8 0.3 fusion.47
  65.1 0.7 fusion.48
  65.8 1.1 convert_reduce_fusion.2
  66.9 1.3 %fusion.50 = f32[64,4,8,128]{3,0,2,1:T(8,128)S(1)} fusion(f32[64,4,8,128]{3,0,2,1:T(8,128)S(1)} %copy-done.1, f32[64,4,8]{0,2,1:T(8,128)S(1)} %get-tuple-element.193, pred[]{:T(512)S(6)} %compare.37, bf16[384,1,4,128]{3,2,1,0:T(4,128)(2,1)S(1)} %get-tuple-element.194, f32[4,384,64,8]{1,2,3,0:T(8,128)S(1)} %get-tuple-element.191, ...), kind=kOutput, calls=%fused_computation.13.clone.1 | convolution fusion | flops 205258752 | bytes 5677057 | tf_op jit(solution)/shard_map/while/body/eval_jaxpr/rkgt,tkd->rkgd/dot_general | solution.py:42
  68.2 0.9 copy-done.2
  69.5 1.2 constant_dynamic-slice_fusion.2
  70.6 0.6 reshape.651
  71.2 0.3 fusion.47
  71.5 0.7 fusion.48
  72.2 1.1 convert_reduce_fusion.2
  73.3 1.3 %fusion.50 = f32[64,4,8,128]{3,0,2,1:T(8,128)S(1)} fusion(f32[64,4,8,128]{3,0,2,1:T(8,128)S(1)} %copy-done.1, f32[64,4,8]{0,2,1:T(8,128)S(1)} %get-tuple-element.193, pred[]{:T(512)S(6)} %compare.37, bf16[384,1,4,128]{3,2,1,0:T(4,128)(2,1)S(1)} %get-tuple-element.194, f32[4,384,64,8]{1,2,3,0:T(8,128)S(1)} %get-tuple-element.191, ...), kind=kOutput, calls=%fused_computation.13.clone.1 | convolution fusion | flops 205258752 | bytes 5677057 | tf_op jit(solution)/shard_map/while/body/eval_jaxpr/rkgt,tkd->rkgd/dot_general | solution.py:42
  74.6 0.9 copy-done.2
  75.9 1.2 constant_dynamic-slice_fusion.2
  77.1 0.6 reshape.651
  77.6 0.3 fusion.47
  77.9 0.7 fusion.48
  78.7 1.1 convert_reduce_fusion.2
  79.8 1.3 %fusion.50 = f32[64,4,8,128]{3,0,2,1:T(8,128)S(1)} fusion(f32[64,4,8,128]{3,0,2,1:T(8,128)S(1)} %copy-done.1, f32[64,4,8]{0,2,1:T(8,128)S(1)} %get-tuple-element.193, pred[]{:T(512)S(6)} %compare.37, bf16[384,1,4,128]{3,2,1,0:T(4,128)(2,1)S(1)} %get-tuple-element.194, f32[4,384,64,8]{1,2,3,0:T(8,128)S(1)} %get-tuple-element.191, ...), kind=kOutput, calls=%fused_computation.13.clone.1 | convolution fusion | flops 205258752 | bytes 5677057 | tf_op jit(solution)/shard_map/while/body/eval_jaxpr/rkgt,tkd->rkgd/dot_general | solution.py:42
  81.1 0.9 copy-done.2
  82.0 1.6 %divide_convert_fusion = bf16[64,4,8,128]{3,0,2,1:T(8,128)(2,1)S(1)} fusion(f32[64,4,8,128]{3,0,2,1:T(8,128)} %get-tuple-element.48, f32[64,4,8]{0,2,1:T(8,128)S(1)} %get-tuple-element.49), kind=kLoop, calls=%fused_computation.34 | loop fusion | flops 524288 | bytes 1581056 | tf_op jit(solution)/shard_map/convert_element_type | solution.py:79
  83.6 0.3 copy.23
  83.9 0.2 copy.37
  84.2 1.2 gather_fusion.1
  85.4 1.1 bitcast_select_fusion.1
  86.5 3.7 %all-to-all-start.1 = ((bf16[16,8,4096]{2,1,0:T(8,128)(2,1)}), bf16[16,8,4096]{2,1,0:T(8,128)(2,1)S(1)}, u32[]{:S(2)}, u32[]{:S(2)}) async-start(bf16[16,8,4096]{2,1,0:T(8,128)(2,1)} %bitcast_select_fusion.1), calls=%async_computation.1 | async-start | bytes 2097152 | tf_op jit(solution)/shard_map/all_to_all | solution.py:171
  90.2 0.6 fusion.30
  90.8 22.2 %all-to-all-done.1 = bf16[16,8,4096]{2,1,0:T(8,128)(2,1)S(1)} async-done(((bf16[16,8,4096]{2,1,0:T(8,128)(2,1)}), bf16[16,8,4096]{2,1,0:T(8,128)(2,1)S(1)}, u32[]{:S(2)}, u32[]{:S(2)}) %all-to-all-start.1) | async-done | bytes 1048608 | tf_op jit(solution)/shard_map/all_to_all | solution.py:171
  113.0 3.0 %scatter_custom_fusion.2 = bf16[128,4096]{1,0:T(8,128)(2,1)} fusion(s32[128]{0:T(128)S(1)} %fusion.30, bf16[16,8,4096]{2,1,0:T(8,128)(2,1)S(1)} %all-to-all-done.1, bf16[]{:T(256)} %constant.114.clone.1), kind=kCustom, calls=%fused_computation.28 | custom fusion | bytes 2097154 | tf_op jit(solution)/shard_map/scatter | solution.py:132
  (63 shorter events, 2.1 us)
Async XLA Ops:
  6.5 4.7 %copy-start = (bf16[128,4096]{1,0:T(8,128)(2,1)S(1)}, bf16[128,4096]{1,0:T(8,128)(2,1)}, u32[]{:S(2)}) copy-start(bf16[128,4096]{1,0:T(8,128)(2,1)} %param.8) | copy-start | bytes 3145732
  6.5 56.2 %all-gather.2.cloned.1.call-start = ((), (), s32[]{:S(2)}) async-start(), calls=%async_computation.2 | async-start | bytes 2506752 | tf_op jit(solution)/shard_map/all_gather | solution.py:168
  12.5 9.2 %copy-start.3 = (s32[128]{0:T(128)S(1)}, s32[128]{0:T(128)}, u32[]{:S(2)}) copy-start(s32[128]{0:T(128)} %param.12) | copy-start | bytes 1540
  12.5 9.3 %copy-start.4 = (s32[16,1]{0,1:T(1,128)S(1)}, s32[16,1]{0,1:T(1,128)}, u32[]{:S(2)}) copy-start(s32[16,1]{0,1:T(1,128)} %param.13) | copy-start | bytes 196
  14.2 34.3 %all-to-all-start = ((bf16[16,8,4096]{2,1,0:T(8,128)(2,1)}), bf16[16,8,4096]{2,1,0:T(8,128)(2,1)S(1)}, u32[]{:S(2)}, u32[]{:S(2)}) async-start(bf16[16,8,4096]{2,1,0:T(8,128)(2,1)} %bitcast_select_fusion.2), calls=%async_computation | async-start | bytes 2097152 | tf_op jit(solution)/shard_map/all_to_all | solution.py:158
  65.1 1.8 %copy-start.1 = (f32[64,4,8,128]{3,0,2,1:T(8,128)S(1)}, f32[64,4,8,128]{3,0,2,1:T(8,128)}, u32[]{:S(2)}) copy-start(f32[64,4,8,128]{3,0,2,1:T(8,128)} %get-tuple-element.208) | copy-start | bytes 3145732 | tf_op jit(solution)/shard_map/while
  68.2 1.0 copy-start.2
  71.5 1.8 %copy-start.1 = (f32[64,4,8,128]{3,0,2,1:T(8,128)S(1)}, f32[64,4,8,128]{3,0,2,1:T(8,128)}, u32[]{:S(2)}) copy-start(f32[64,4,8,128]{3,0,2,1:T(8,128)} %get-tuple-element.208) | copy-start | bytes 3145732 | tf_op jit(solution)/shard_map/while
  74.6 1.0 copy-start.2
  77.9 1.8 %copy-start.1 = (f32[64,4,8,128]{3,0,2,1:T(8,128)S(1)}, f32[64,4,8,128]{3,0,2,1:T(8,128)}, u32[]{:S(2)}) copy-start(f32[64,4,8,128]{3,0,2,1:T(8,128)} %get-tuple-element.208) | copy-start | bytes 3145732 | tf_op jit(solution)/shard_map/while
  81.0 1.0 copy-start.2
  86.5 26.6 %all-to-all-start.1 = ((bf16[16,8,4096]{2,1,0:T(8,128)(2,1)}), bf16[16,8,4096]{2,1,0:T(8,128)(2,1)S(1)}, u32[]{:S(2)}, u32[]{:S(2)}) async-start(bf16[16,8,4096]{2,1,0:T(8,128)(2,1)} %bitcast_select_fusion.1), calls=%async_computation.1 | async-start | bytes 2097152 | tf_op jit(solution)/shard_map/all_to_all | solution.py:171
Sparse Core Ops, SparseCore 0:
  9.6 53.0 all-gather.1
where the time goes:
time: 124 us; the launch traced here: 123 us
  waiting for transfers between devices  59.8 us (48%)
  local copies, waits for them, and re-layouts  19.6 us (16%)
  between operations  13.6 us (11%)
  other arithmetic  12.6 us (10%)
  starting transfers between devices  11 us (9%)
  matrix products  5.99 us (5%)
    all_to_all x1, waiting for transfers between devices, per_device(): lax.all_to_all(outgoing, 'seq', split_axis=0, concat_axis=0, tiled=True)  25 us
    all_to_all x1, waiting for transfers between devices, per_device(): lax.all_to_all(going_back, 'seq', split_axis=0, concat_axis=0, tiled=True)  22.2 us
    all_gather x1, waiting for transfers between devices, per_device(): lax.all_gather(kv_pool, 'seq', axis=0, tiled=True)  11.8 us
    all_to_all x1, starting transfers between devices, per_device(): lax.all_to_all(outgoing, 'seq', split_axis=0, concat_axis=0, tiled=True)  7.36 us
    dot_general x3, matrix products, absorb(): jnp.einsum('rkgt,tkd->rkgd', weights, values, preferred_element_type=jnp....  3.84 us
    all_to_all x1, starting transfers between devices, per_device(): lax.all_to_all(going_back, 'seq', split_axis=0, concat_axis=0, tiled=True)  3.66 us
    dynamic_slice x3, local copies, waits for them, and re-layouts, fold_pages(): result, unused = lax.scan(scan_step, carry, (blocks, block_owners))  3.57 us
    reduce_sum x3, other arithmetic, absorb(): new_total = run_total * factor + jnp.sum(weights.astype(jnp.float32), -1)  3.16 us
  transfers between devices with their start and end apart: 3, of which 3 were waited for; matrix products, arithmetic and copies ran while one was open for 10% of the time, Pallas kernels for 0%

commit v1 on v0

v1 whole, which is shorter than its diff:
```python
import functools
import math

import jax
import jax.numpy as jnp
from jax import lax
from jax.experimental import pallas as pl
from jax.experimental.pallas import tpu as pltpu
from jax.sharding import PartitionSpec as P

QH = 32
KVH = 4
HD = 128
GROUP = QH // KVH
EXP2_SCALE = math.log2(math.e) / math.sqrt(HD)
GATHER_DEVICES = 16


def page_owners(prefix_table, branch_table, pool_size):
    page_ids = jnp.arange(pool_size, dtype=jnp.int32)
    is_prefix = jnp.any(prefix_table[:, None] == page_ids[None, :], 0)
    flat_table = branch_table.reshape(-1)
    table_branch = jnp.arange(flat_table.shape[0], dtype=jnp.int32) // branch_table.shape[1]
    owner_of = jnp.sum(
        jnp.where(flat_table[:, None] == page_ids[None, :], table_branch[:, None], 0), 0
    )
    return jnp.where(is_prefix, -1, owner_of)


def absorb(carry, query_heads, pages, block_allowed):
    run_max, run_total, run_acc = carry
    page_tokens = pages.shape[1]
    token_count = pages.shape[0] * page_tokens
    kv_tokens = pages.reshape(token_count, 2, KVH, HD)
    keys = kv_tokens[:, 0]
    values = kv_tokens[:, 1]
    scores = jnp.einsum("rkgd,tkd->rkgt", query_heads, keys, preferred_element_type=jnp.float32) * (
        1.0 / math.sqrt(HD)
    )
    allowed = jnp.repeat(block_allowed, page_tokens)[None, None, None, :]
    masked = jnp.where(allowed, scores, -1e30)
    new_max = jnp.maximum(run_max, jnp.max(masked, -1))
    weights = jnp.where(allowed, jnp.exp(scores - new_max[..., None]), 0.0).astype(jnp.bfloat16)
    factor = jnp.exp(run_max - new_max)
    new_total = run_total * factor + jnp.sum(weights.astype(jnp.float32), -1)
    new_acc = run_acc * factor[..., None] + jnp.einsum(
        "rkgt,tkd->rkgd", weights, values, preferred_element_type=jnp.float32
    )
    return (new_max, new_total, new_acc)


def attend_general(queries, kv_pool, page_allowed, live_count):
    row_count = queries.shape[0]
    pages = lax.all_gather(kv_pool, "seq", axis=0, tiled=True)
    page_tokens = pages.shape[1]
    block_pages = max(1, max(128, 32768 // row_count) // page_tokens)
    while pages.shape[0] % block_pages:
        block_pages = block_pages - 1
    blocks = pages.reshape((-1, block_pages) + pages.shape[1:])
    block_allowed = page_allowed.reshape(-1, block_pages)
    query_heads = queries.reshape(row_count, KVH, GROUP, HD)
    start = (
        jnp.full((row_count, KVH, GROUP), -1e30, jnp.float32),
        jnp.zeros((row_count, KVH, GROUP), jnp.float32),
        jnp.zeros((row_count, KVH, GROUP, HD), jnp.float32),
    )

    def scan_step(state, inputs):
        block, allowed = inputs
        return (absorb(state, query_heads, block, allowed), None)

    (run_max, run_total, run_acc), unused = lax.scan(scan_step, start, (blocks, block_allowed))
    mixed = (run_acc / run_total[..., None]).reshape(row_count, QH * HD)
    live = jnp.arange(row_count, dtype=jnp.int32) < live_count
    return jnp.where(live[:, None], mixed, 0.0).astype(jnp.bfloat16)


def place(z, x, core):
    return z * 4 + x * 2 + core


def permute(block, target):
    pairs = []
    for index in range(GATHER_DEVICES):
        to = target(index // 4, index // 2 % 2, index % 2)
        if to is not None:
            pairs.append((index, place(*to)))
    return lax.ppermute(block, "seq", pairs)


def gather_pieces(shard):
    along_z = [
        shard,
        permute(shard, lambda z, x, c: (z ^ 1, x, c)),
        permute(shard, lambda z, x, c: (z ^ 2, x, c)),
        permute(shard, lambda z, x, c: (z ^ 3, x, c)),
    ]
    pieces = []
    for block in along_z:
        other = permute(block, lambda z, x, c: (z, 1 - x, c))
        for held in (block, other):
            pieces.append(held)
            pieces.append(permute(held, lambda z, x, c: (z, x, 1 - c)))
    return pieces


def attention_kernel(q_ref, bias_ref, live_ref, *refs, count):
    piece_refs = refs[:count]
    out_ref, keys, values = refs[count:]
    rows = q_ref.shape[0]
    tokens = keys.shape[1]
    piece = tokens // count
    values[:, :, HD:] = jnp.ones((KVH, tokens, HD), jnp.bfloat16)
    for i in range(count):
        block = piece_refs[i][...].reshape(piece, 2 * KVH * HD)
        span = slice(i * piece, (i + 1) * piece)
        for h in range(KVH):
            keys[h, span, :] = block[:, h * HD : (h + 1) * HD]
            values[h, span, :HD] = block[:, (KVH + h) * HD : (KVH + h + 1) * HD]
    live = lax.broadcasted_iota(jnp.int32, (rows, HD), 0) < live_ref[0]
    bias = bias_ref[...]
    for q_head in range(QH):
        h = q_head // GROUP
        lanes = slice(q_head * HD, (q_head + 1) * HD)
        scores = lax.dot_general(
            q_ref[:, lanes], keys[h], (((1,), (1,)), ((), ())), preferred_element_type=jnp.float32
        )
        scores = scores + bias
        row_max = jnp.max(scores, -1, keepdims=True)
        weights = jnp.exp2((scores - row_max) * EXP2_SCALE).astype(jnp.bfloat16)
        sums = jnp.dot(weights, values[h], preferred_element_type=jnp.float32)
        mixed = sums[:, :HD] / sums[:, HD:]
        out_ref[:, lanes] = jnp.where(live, mixed, 0.0).astype(jnp.bfloat16)


def attend_pieces(queries, pieces, bias, live_count):
    rows, features = queries.shape
    count = len(pieces)
    tokens = bias.shape[1]
    vmem = pl.BlockSpec(memory_space=pltpu.VMEM)
    return pl.pallas_call(
        functools.partial(attention_kernel, count=count),
        out_shape=jax.ShapeDtypeStruct((rows, features), jnp.bfloat16),
        in_specs=[vmem, vmem, pl.BlockSpec(memory_space=pltpu.SMEM)] + [vmem] * count,
        out_specs=vmem,
        scratch_shapes=[
            pltpu.VMEM((KVH, tokens, HD), jnp.bfloat16),
            pltpu.VMEM((KVH, tokens, 2 * HD), jnp.bfloat16),
        ],
        compiler_params=pltpu.CompilerParams(vmem_limit_bytes=40 << 20),
        cost_estimate=pl.CostEstimate(
            flops=4 * rows * features * tokens,
            bytes_accessed=4 * rows * features + 2 * tokens * KVH * HD * 2,
            transcendentals=rows * QH * tokens,
        ),
        name="attention",
    )(queries, bias, live_count.reshape(1), *pieces)


def per_device(queries, kv_pool, span_lengths, owner_branch, prefix_table, branch_table):
    device_count = lax.axis_size("seq")
    self_index = lax.axis_index("seq")
    capacity = queries.shape[0]
    branch_count = span_lengths.shape[0]
    owner_width = device_count // branch_count
    pages_dev, page_tokens = kv_pool.shape[:2]
    my_branch = owner_branch[self_index // owner_width]
    live_count = span_lengths[my_branch] - self_index % owner_width * capacity
    slot_branch = page_owners(prefix_table, branch_table, pages_dev * device_count)
    page_allowed = (slot_branch < 0) | (slot_branch == my_branch)
    if device_count != GATHER_DEVICES:
        return attend_general(queries, kv_pool, page_allowed, live_count)
    by_piece = page_allowed.reshape(device_count, pages_dev)[
        self_index ^ jnp.arange(device_count, dtype=jnp.int32)
    ]
    bias = jnp.where(jnp.repeat(by_piece.reshape(-1), page_tokens), 0.0, -1e30)[None, :]
    pieces = gather_pieces(kv_pool)
    return attend_pieces(queries, pieces, bias, live_count)


def solution(mesh):
    return jax.shard_map(
        per_device,
        mesh=mesh,
        in_specs=(
            P(("grp", "seq"), None),
            P(("grp", "seq"), None, None),
            P("grp"),
            P("grp"),
            P("grp"),
            P("grp", None),
        ),
        out_specs=P(("grp", "seq"), None),
        check_vma=False,
    )
```

time: 124 us -> 36.5 us (0.29)
  waiting for transfers between devices: 59.8 us -> 5.53 us
  local copies, waits for them, and re-layouts: 19.6 us -> 4.03 us
  between operations: 13.6 us -> 2.07 us
  other arithmetic: 12.6 us -> 2.18 us
  Pallas kernels: 0 us -> 8.88 us
  matrix products: 5.99 us -> 0 us
  starting transfers between devices: 11 us -> 13.5 us
    all_to_all x2 -> x0, waiting for transfers between devices: 47.3 us -> none  [the longest x1 25 us: per_device(): lax.all_to_all(outgoing, 'seq', split_axis=0, concat_axis=0, tiled=True)]
    ppermute x0 -> x15, starting transfers between devices: none -> 13.5 us  [permute(): return lax.ppermute(block, 'seq', pairs)]
    all_gather x1 -> x0, waiting for transfers between devices: 11.8 us -> none  [per_device(): lax.all_gather(kv_pool, 'seq', axis=0, tiled=True)]
    all_to_all x2 -> x0, starting transfers between devices: 11 us -> none  [the longest x1 7.36 us: per_device(): lax.all_to_all(outgoing, 'seq', split_axis=0, concat_axis=0, tiled=True)]
    pallas_call x0 -> x1, Pallas kernels: none -> 8.88 us  [attend_pieces(): pl.pallas_call(functools.partial(attention_kernel, count=count), out_shap...]
    scatter x3 -> x0, local copies, waits for them, and re-layouts: 6.1 us -> none  [the longest x1 3.03 us: unpack_returned(): return jnp.zeros((capacity, features), jnp.bfloat16).at[owner_slot].set(r...]
    dot_general x6 -> x0, matrix products: 5.99 us -> none  [the longest x3 3.84 us: absorb(): jnp.einsum('rkgt,tkd->rkgd', weights, values, preferred_element_type=jnp....]
    ppermute x0 -> x15, waiting for transfers between devices: none -> 5.53 us  [permute(): return lax.ppermute(block, 'seq', pairs)]
  transfers between devices with their start and end apart: 3 -> 15, of which waited for: 3 -> 3; matrix products, arithmetic and copies ran while one was open for 10% -> 14% of each run, Pallas kernels for 0% -> 0%
where the time goes in v1:
time: 36.5 us; the launch traced here: 36.2 us
  starting transfers between devices  13.5 us (37%)
  Pallas kernels  8.88 us (24%)
  waiting for transfers between devices  5.53 us (15%)
  local copies, waits for them, and re-layouts  4.03 us (11%)
  other arithmetic  2.18 us (6%)
  between operations  2.07 us (6%)
    ppermute x15, starting transfers between devices, permute(): return lax.ppermute(block, 'seq', pairs)  13.5 us
    pallas_call x1, Pallas kernels, attend_pieces(): pl.pallas_call(functools.partial(attention_kernel, count=count), out_shap...  8.88 us
    ppermute x15, waiting for transfers between devices, permute(): return lax.ppermute(block, 'seq', pairs)  5.53 us
    dynamic_slice x1, local copies, waits for them, and re-layouts, per_device(): my_branch = owner_branch[self_index // owner_width]  1.24 us
    unnamed x6, local copies, waits for them, and re-layouts  1.23 us
    reduce_or x1, other arithmetic, page_owners(): is_prefix = jnp.any(prefix_table[:, None] == page_ids[None, :], 0)  0.77 us
    reduce_sum x1, other arithmetic, page_owners(): jnp.sum(jnp.where(flat_table[:, None] == page_ids[None, :], table_branch[...  0.74 us
  transfers between devices with their start and end apart: 15, of which 3 were waited for; matrix products, arithmetic and copies ran while one was open for 14% of the time, Pallas kernels for 0%

profile of v1, /device:TPU:0, one launch (start us, length us, event | category | flops | bytes accessed | tf_op | source)
XLA Modules:
  0.0 36.2 jit_solution(11986496114291731748)
XLA Ops:
  0.0 0.0 copy-start.1
  0.0 4.0 %collective-permute-start.7 = (bf16[9,8,1024]{2,1,0:T(8,128)(2,1)}, bf16[9,8,1024]{2,1,0:T(8,128)(2,1)S(1)}, u32[]{:S(2)}, u32[]{:S(2)}) collective-permute-start(bf16[9,8,1024]{2,1,0:T(8,128)(2,1)} %refs_0_.1), channel_id=1, source_target_pairs={{0,8},{1,9},{2,10},{3,11},{4,12},{5,13},{6,14},{7,15},{8,0},{9,1},... | collective-permute-start | bytes 442376 | tf_op jit(solution)/shard_map/ppermute | solution.py:88
  4.0 1.6 %collective-permute-start.3 = (bf16[9,8,1024]{2,1,0:T(8,128)(2,1)}, bf16[9,8,1024]{2,1,0:T(8,128)(2,1)S(1)}, u32[]{:S(2)}, u32[]{:S(2)}) collective-permute-start(bf16[9,8,1024]{2,1,0:T(8,128)(2,1)} %refs_0_.1), channel_id=1, source_target_pairs={{0,4},{1,5},{2,6},{3,7},{4,0},{5,1},{6,2},{7,3},{8,12},{9,13},{10,... | collective-permute-start | bytes 442376 | tf_op jit(solution)/shard_map/ppermute | solution.py:88
  5.6 1.5 %collective-permute-start.1 = (bf16[9,8,1024]{2,1,0:T(8,128)(2,1)}, bf16[9,8,1024]{2,1,0:T(8,128)(2,1)S(1)}, u32[]{:S(2)}, u32[]{:S(2)}) collective-permute-start(bf16[9,8,1024]{2,1,0:T(8,128)(2,1)} %refs_0_.1), channel_id=1, source_target_pairs={{0,2},{1,3},{2,0},{3,1},{4,6},{5,7},{6,4},{7,5},{8,10},{9,11},{10,... | collective-permute-start | bytes 442376 | tf_op jit(solution)/shard_map/ppermute | solution.py:88
  7.1 0.0 collective-permute-start
  7.1 0.2 collective-permute-start.11
  7.3 0.8 %fusion = pred[144]{0:T(512)(128)(4,1)S(1)} fusion(s32[128]{0:T(128)} %param.10), kind=kLoop, calls=%fused_computation.2 | loop fusion | flops 36720 | bytes 656 | tf_op jit(solution)/shard_map/reduce_or | solution.py:21
  8.1 0.7 %select_reduce_fusion = s32[144]{0:T(256)S(1)} fusion(s32[16]{0:T(128)} %bitcast.4), kind=kLoop, calls=%fused_computation.3 | loop fusion | flops 6768 | bytes 640 | tf_op jit(solution)/shard_map/reduce_sum | solution.py:24
  8.8 1.2 %dynamic_slice.6 = s32[1]{0:T(128)} dynamic-slice(s32[16]{0:T(128)} %param.9, s32[]{:T(128)S(6)} %select_n.57), dynamic_slice_sizes={1} | dynamic-slice | bytes 12 | tf_op jit(solution)/shard_map/dynamic_slice | solution.py:167
  10.1 0.7 %compare_or_fusion = pred[144]{0:T(512)(128)(4,1)S(1)} fusion(pred[144]{0:T(512)(128)(4,1)S(1)} %fusion, s32[144]{0:T(256)S(1)} %select_reduce_fusion, s32[]{:T(128)} %bitcast.1), kind=kLoop, calls=%fused_computation.8 | loop fusion | flops 576 | bytes 868 | tf_op jit(solution)/shard_map/or | solution.py:170
  10.8 1.4 %collective-permute-done.7.refs_8_ = bf16[9,8,1024]{2,1,0:T(8,128)(2,1)S(1)} collective-permute-done((bf16[9,8,1024]{2,1,0:T(8,128)(2,1)}, bf16[9,8,1024]{2,1,0:T(8,128)(2,1)S(1)}, u32[]{:S(2)}, u32[]{:S(2)}) %collective-permute-start.7) | collective-permute-done | bytes 147488 | tf_op jit(solution)/shard_map/ppermute | solution.py:88
  12.2 2.9 %collective-permute-start.9 = (bf16[9,8,1024]{2,1,0:T(8,128)(2,1)S(1)}, bf16[9,8,1024]{2,1,0:T(8,128)(2,1)S(1)}, u32[]{:S(2)}, u32[]{:S(2)}) collective-permute-start(bf16[9,8,1024]{2,1,0:T(8,128)(2,1)S(1)} %collective-permute-done.7.refs_8_), channel_id=1, source_target_pairs={{0,2},{1,3},{2,0},{3,1},{4,6},{5,7},{6,4},{7,5},{8,10},{9,11},{10,... | collective-permute-start | bytes 442376 | tf_op jit(solution)/shard_map/ppermute | solution.py:88
  15.0 0.0 collective-permute-done.3.refs_4_
  15.0 0.0 collective-permute-start.8
  15.0 0.0 collective-permute-done.1.refs_2_
  15.0 0.1 collective-permute-start.5
  15.1 0.0 collective-permute-done.refs_1_
  15.1 0.5 %collective-permute-start.4 = (bf16[9,8,1024]{2,1,0:T(8,128)(2,1)S(1)}, bf16[9,8,1024]{2,1,0:T(8,128)(2,1)S(1)}, u32[]{:S(2)}, u32[]{:S(2)}) collective-permute-start(bf16[9,8,1024]{2,1,0:T(8,128)(2,1)S(1)} %collective-permute-done.3.refs_4_), channel_id=1, source_target_pairs={{0,1},{1,0},{2,3},{3,2},{4,5},{5,4},{6,7},{7,6},{8,9},{9,8},{10,11... | collective-permute-start | bytes 442376 | tf_op jit(solution)/shard_map/ppermute | solution.py:88
  15.6 0.0 collective-permute-done.11.refs_12_
  15.6 1.7 %collective-permute-start.13 = (bf16[9,8,1024]{2,1,0:T(8,128)(2,1)S(1)}, bf16[9,8,1024]{2,1,0:T(8,128)(2,1)S(1)}, u32[]{:S(2)}, u32[]{:S(2)}) collective-permute-start(bf16[9,8,1024]{2,1,0:T(8,128)(2,1)S(1)} %collective-permute-done.11.refs_12_), channel_id=1, source_target_pairs={{0,2},{1,3},{2,0},{3,1},{4,6},{5,7},{6,4},{7,5},{8,10},{9,11},{10,... | collective-permute-start | bytes 442376 | tf_op jit(solution)/shard_map/ppermute | solution.py:88
  18.6 0.1 or.8
  18.7 0.6 %gather_fusion = pred[16,9]{1,0:T(8,128)(4,1)S(1)} fusion(pred[16,9]{1,0:T(8,128)(4,1)S(1)} %or.8, s32[1024]{0:T(1024)S(1)} %pad_clamp_fusion), kind=kCustom, calls=%fused_computation | custom fusion | bytes 352 | tf_op jit(solution)/shard_map/gather | solution.py:173
  19.3 0.0 collective-permute-done.9.refs_10_
  19.3 0.1 collective-permute-start.12
  19.4 0.0 collective-permute-done.8.refs_9_
  19.4 0.4 %collective-permute-start.2 = (bf16[9,8,1024]{2,1,0:T(8,128)(2,1)S(1)}, bf16[9,8,1024]{2,1,0:T(8,128)(2,1)S(1)}, u32[]{:S(2)}, u32[]{:S(2)}) collective-permute-start(bf16[9,8,1024]{2,1,0:T(8,128)(2,1)S(1)} %collective-permute-done.1.refs_2_), channel_id=1, source_target_pairs={{0,1},{1,0},{2,3},{3,2},{4,5},{5,4},{6,7},{7,6},{8,9},{9,8},{10,11... | collective-permute-start | bytes 442376 | tf_op jit(solution)/shard_map/ppermute | solution.py:88
  19.9 2.4 %collective-permute-done.5.refs_6_ = bf16[9,8,1024]{2,1,0:T(8,128)(2,1)S(1)} collective-permute-done((bf16[9,8,1024]{2,1,0:T(8,128)(2,1)S(1)}, bf16[9,8,1024]{2,1,0:T(8,128)(2,1)S(1)}, u32[]{:S(2)}, u32[]{:S(2)}) %collective-permute-start.5) | collective-permute-done | bytes 147488 | tf_op jit(solution)/shard_map/ppermute | solution.py:88
  22.3 0.0 collective-permute-start.10
  22.3 0.0 collective-permute-done.4.refs_5_
  22.3 0.5 %collective-permute-start.6 = (bf16[9,8,1024]{2,1,0:T(8,128)(2,1)S(1)}, bf16[9,8,1024]{2,1,0:T(8,128)(2,1)S(1)}, u32[]{:S(2)}, u32[]{:S(2)}) collective-permute-start(bf16[9,8,1024]{2,1,0:T(8,128)(2,1)S(1)} %collective-permute-done.5.refs_6_), channel_id=1, source_target_pairs={{0,1},{1,0},{2,3},{3,2},{4,5},{5,4},{6,7},{7,6},{8,9},{9,8},{10,11... | collective-permute-start | bytes 442376 | tf_op jit(solution)/shard_map/ppermute | solution.py:88
  22.8 1.7 %collective-permute-done.13.refs_14_ = bf16[9,8,1024]{2,1,0:T(8,128)(2,1)S(1)} collective-permute-done((bf16[9,8,1024]{2,1,0:T(8,128)(2,1)S(1)}, bf16[9,8,1024]{2,1,0:T(8,128)(2,1)S(1)}, u32[]{:S(2)}, u32[]{:S(2)}) %collective-permute-start.13) | collective-permute-done | bytes 147488 | tf_op jit(solution)/shard_map/ppermute | solution.py:88
  24.5 0.0 collective-permute-start.14
  24.5 0.1 select_n.60
  24.6 0.1 broadcast_in_dim.38
  24.7 0.1 select_n.61.bias_ref
  24.8 0.0 copy-start.2
  25.4 0.0 copy-done.2
  25.5 0.6 %dynamic_slice.7.live_ref = s32[1]{0:T(128)} dynamic-slice(s32[16]{0:T(128)S(1)} %copy-done.2, s32[]{:T(128)S(6)} %select_n.62), dynamic_slice_sizes={1} | dynamic-slice | bytes 12 | tf_op jit(solution)/shard_map/dynamic_slice | solution.py:168
  26.1 0.0 collective-permute-done.2.refs_3_
  26.1 0.0 collective-permute-done.12.refs_13_
  26.1 0.0 collective-permute-done.10.refs_11_
  26.1 0.0 collective-permute-done.6.refs_7_
  26.1 0.0 collective-permute-done.14.refs_15_
  26.1 0.0 copy-done.1
  26.1 0.0 copy-start
  26.1 1.2 %copy-done = bf16[128,4096]{1,0:T(8,128)(2,1)S(1)} copy-done((bf16[128,4096]{1,0:T(8,128)(2,1)S(1)}, bf16[128,4096]{1,0:T(8,128)(2,1)}, u32[]{:S(2)}) %copy-start) | copy-done | bytes 1048600
  27.3 8.9 %attention.1 = bf16[128,4096]{1,0:T(8,128)(2,1)} custom-call(bf16[128,4096]{1,0:T(8,128)(2,1)S(1)} %copy-done, f32[1,1152]{1,0:T(1,128)S(1)} %select_n.61.bias_ref, s32[1]{0:T(128)} %dynamic_slice.7.live_ref, bf16[9,8,1024]{2,1,0:T(8,128)(2,1)S(1)} %copy-done.1, bf16[9,8,1024]{2,1,0:T(8,128)(2,1)S(1)} %collective-permute-done.refs_1_, ...), custom_call_target="tpu_custom_call" | custom-call | flops 2415919104 | bytes 4456448 | tf_op jit(solution)/shard_map/attention/pallas_call | solution.py:141
  (3 shorter events, 0.0 us)
Async XLA Ops:
  0.0 26.1 %copy-start.1 = (bf16[9,8,1024]{2,1,0:T(8,128)(2,1)S(1)}, bf16[9,8,1024]{2,1,0:T(8,128)(2,1)}, u32[]{:S(2)}) copy-start(bf16[9,8,1024]{2,1,0:T(8,128)(2,1)} %refs_0_.1) | copy-start | bytes 442372
  0.0 12.2 %collective-permute-start.7 = (bf16[9,8,1024]{2,1,0:T(8,128)(2,1)}, bf16[9,8,1024]{2,1,0:T(8,128)(2,1)S(1)}, u32[]{:S(2)}, u32[]{:S(2)}) collective-permute-start(bf16[9,8,1024]{2,1,0:T(8,128)(2,1)} %refs_0_.1), channel_id=1, source_target_pairs={{0,8},{1,9},{2,10},{3,11},{4,12},{5,13},{6,14},{7,15},{8,0},{9,1},... | collective-permute-start | bytes 442376 | tf_op jit(solution)/shard_map/ppermute | solution.py:88
  4.0 11.0 %collective-permute-start.3 = (bf16[9,8,1024]{2,1,0:T(8,128)(2,1)}, bf16[9,8,1024]{2,1,0:T(8,128)(2,1)S(1)}, u32[]{:S(2)}, u32[]{:S(2)}) collective-permute-start(bf16[9,8,1024]{2,1,0:T(8,128)(2,1)} %refs_0_.1), channel_id=1, source_target_pairs={{0,4},{1,5},{2,6},{3,7},{4,0},{5,1},{6,2},{7,3},{8,12},{9,13},{10,... | collective-permute-start | bytes 442376 | tf_op jit(solution)/shard_map/ppermute | solution.py:88
  5.6 9.4 %collective-permute-start.1 = (bf16[9,8,1024]{2,1,0:T(8,128)(2,1)}, bf16[9,8,1024]{2,1,0:T(8,128)(2,1)S(1)}, u32[]{:S(2)}, u32[]{:S(2)}) collective-permute-start(bf16[9,8,1024]{2,1,0:T(8,128)(2,1)} %refs_0_.1), channel_id=1, source_target_pairs={{0,2},{1,3},{2,0},{3,1},{4,6},{5,7},{6,4},{7,5},{8,10},{9,11},{10,... | collective-permute-start | bytes 442376 | tf_op jit(solution)/shard_map/ppermute | solution.py:88
  7.1 8.0 %collective-permute-start = (bf16[9,8,1024]{2,1,0:T(8,128)(2,1)}, bf16[9,8,1024]{2,1,0:T(8,128)(2,1)S(1)}, u32[]{:S(2)}, u32[]{:S(2)}) collective-permute-start(bf16[9,8,1024]{2,1,0:T(8,128)(2,1)} %refs_0_.1), channel_id=1, source_target_pairs={{0,1},{1,0},{2,3},{3,2},{4,5},{5,4},{6,7},{7,6},{8,9},{9,8},{10,11... | collective-permute-start | bytes 442376 | tf_op jit(solution)/shard_map/ppermute | solution.py:88
  7.1 8.5 %collective-permute-start.11 = (bf16[9,8,1024]{2,1,0:T(8,128)(2,1)}, bf16[9,8,1024]{2,1,0:T(8,128)(2,1)S(1)}, u32[]{:S(2)}, u32[]{:S(2)}) collective-permute-start(bf16[9,8,1024]{2,1,0:T(8,128)(2,1)} %refs_0_.1), channel_id=1, source_target_pairs={{0,12},{1,13},{2,14},{3,15},{4,8},{5,9},{6,10},{7,11},{8,4},{9,5},... | collective-permute-start | bytes 442376 | tf_op jit(solution)/shard_map/ppermute | solution.py:88
  12.2 7.1 %collective-permute-start.9 = (bf16[9,8,1024]{2,1,0:T(8,128)(2,1)S(1)}, bf16[9,8,1024]{2,1,0:T(8,128)(2,1)S(1)}, u32[]{:S(2)}, u32[]{:S(2)}) collective-permute-start(bf16[9,8,1024]{2,1,0:T(8,128)(2,1)S(1)} %collective-permute-done.7.refs_8_), channel_id=1, source_target_pairs={{0,2},{1,3},{2,0},{3,1},{4,6},{5,7},{6,4},{7,5},{8,10},{9,11},{10,... | collective-permute-start | bytes 442376 | tf_op jit(solution)/shard_map/ppermute | solution.py:88
  15.0 4.4 %collective-permute-start.8 = (bf16[9,8,1024]{2,1,0:T(8,128)(2,1)S(1)}, bf16[9,8,1024]{2,1,0:T(8,128)(2,1)S(1)}, u32[]{:S(2)}, u32[]{:S(2)}) collective-permute-start(bf16[9,8,1024]{2,1,0:T(8,128)(2,1)S(1)} %collective-permute-done.7.refs_8_), channel_id=1, source_target_pairs={{0,1},{1,0},{2,3},{3,2},{4,5},{5,4},{6,7},{7,6},{8,9},{9,8},{10,11... | collective-permute-start | bytes 442376 | tf_op jit(solution)/shard_map/ppermute | solution.py:88
  15.0 7.2 %collective-permute-start.5 = (bf16[9,8,1024]{2,1,0:T(8,128)(2,1)S(1)}, bf16[9,8,1024]{2,1,0:T(8,128)(2,1)S(1)}, u32[]{:S(2)}, u32[]{:S(2)}) collective-permute-start(bf16[9,8,1024]{2,1,0:T(8,128)(2,1)S(1)} %collective-permute-done.3.refs_4_), channel_id=1, source_target_pairs={{0,2},{1,3},{2,0},{3,1},{4,6},{5,7},{6,4},{7,5},{8,10},{9,11},{10,... | collective-permute-start | bytes 442376 | tf_op jit(solution)/shard_map/ppermute | solution.py:88
  15.1 7.1 %collective-permute-start.4 = (bf16[9,8,1024]{2,1,0:T(8,128)(2,1)S(1)}, bf16[9,8,1024]{2,1,0:T(8,128)(2,1)S(1)}, u32[]{:S(2)}, u32[]{:S(2)}) collective-permute-start(bf16[9,8,1024]{2,1,0:T(8,128)(2,1)S(1)} %collective-permute-done.3.refs_4_), channel_id=1, source_target_pairs={{0,1},{1,0},{2,3},{3,2},{4,5},{5,4},{6,7},{7,6},{8,9},{9,8},{10,11... | collective-permute-start | bytes 442376 | tf_op jit(solution)/shard_map/ppermute | solution.py:88
  15.6 8.8 %collective-permute-start.13 = (bf16[9,8,1024]{2,1,0:T(8,128)(2,1)S(1)}, bf16[9,8,1024]{2,1,0:T(8,128)(2,1)S(1)}, u32[]{:S(2)}, u32[]{:S(2)}) collective-permute-start(bf16[9,8,1024]{2,1,0:T(8,128)(2,1)S(1)} %collective-permute-done.11.refs_12_), channel_id=1, source_target_pairs={{0,2},{1,3},{2,0},{3,1},{4,6},{5,7},{6,4},{7,5},{8,10},{9,11},{10,... | collective-permute-start | bytes 442376 | tf_op jit(solution)/shard_map/ppermute | solution.py:88
  19.3 6.8 %collective-permute-start.12 = (bf16[9,8,1024]{2,1,0:T(8,128)(2,1)S(1)}, bf16[9,8,1024]{2,1,0:T(8,128)(2,1)S(1)}, u32[]{:S(2)}, u32[]{:S(2)}) collective-permute-start(bf16[9,8,1024]{2,1,0:T(8,128)(2,1)S(1)} %collective-permute-done.11.refs_12_), channel_id=1, source_target_pairs={{0,1},{1,0},{2,3},{3,2},{4,5},{5,4},{6,7},{7,6},{8,9},{9,8},{10,11... | collective-permute-start | bytes 442376 | tf_op jit(solution)/shard_map/ppermute | solution.py:88
  19.4 6.6 %collective-permute-start.2 = (bf16[9,8,1024]{2,1,0:T(8,128)(2,1)S(1)}, bf16[9,8,1024]{2,1,0:T(8,128)(2,1)S(1)}, u32[]{:S(2)}, u32[]{:S(2)}) collective-permute-start(bf16[9,8,1024]{2,1,0:T(8,128)(2,1)S(1)} %collective-permute-done.1.refs_2_), channel_id=1, source_target_pairs={{0,1},{1,0},{2,3},{3,2},{4,5},{5,4},{6,7},{7,6},{8,9},{9,8},{10,11... | collective-permute-start | bytes 442376 | tf_op jit(solution)/shard_map/ppermute | solution.py:88
  22.3 3.8 %collective-permute-start.10 = (bf16[9,8,1024]{2,1,0:T(8,128)(2,1)S(1)}, bf16[9,8,1024]{2,1,0:T(8,128)(2,1)S(1)}, u32[]{:S(2)}, u32[]{:S(2)}) collective-permute-start(bf16[9,8,1024]{2,1,0:T(8,128)(2,1)S(1)} %collective-permute-done.9.refs_10_), channel_id=1, source_target_pairs={{0,1},{1,0},{2,3},{3,2},{4,5},{5,4},{6,7},{7,6},{8,9},{9,8},{10,11... | collective-permute-start | bytes 442376 | tf_op jit(solution)/shard_map/ppermute | solution.py:88
  22.3 3.8 %collective-permute-start.6 = (bf16[9,8,1024]{2,1,0:T(8,128)(2,1)S(1)}, bf16[9,8,1024]{2,1,0:T(8,128)(2,1)S(1)}, u32[]{:S(2)}, u32[]{:S(2)}) collective-permute-start(bf16[9,8,1024]{2,1,0:T(8,128)(2,1)S(1)} %collective-permute-done.5.refs_6_), channel_id=1, source_target_pairs={{0,1},{1,0},{2,3},{3,2},{4,5},{5,4},{6,7},{7,6},{8,9},{9,8},{10,11... | collective-permute-start | bytes 442376 | tf_op jit(solution)/shard_map/ppermute | solution.py:88
  24.5 1.6 %collective-permute-start.14 = (bf16[9,8,1024]{2,1,0:T(8,128)(2,1)S(1)}, bf16[9,8,1024]{2,1,0:T(8,128)(2,1)S(1)}, u32[]{:S(2)}, u32[]{:S(2)}) collective-permute-start(bf16[9,8,1024]{2,1,0:T(8,128)(2,1)S(1)} %collective-permute-done.13.refs_14_), channel_id=1, source_target_pairs={{0,1},{1,0},{2,3},{3,2},{4,5},{5,4},{6,7},{7,6},{8,9},{9,8},{10,11... | collective-permute-start | bytes 442376 | tf_op jit(solution)/shard_map/ppermute | solution.py:88
  24.8 0.7 %copy-start.2 = (s32[16]{0:T(128)S(1)}, s32[16]{0:T(128)}, u32[]{:S(2)}) copy-start(s32[16]{0:T(128)} %param.8) | copy-start | bytes 196
  26.1 1.2 %copy-start = (bf16[128,4096]{1,0:T(8,128)(2,1)S(1)}, bf16[128,4096]{1,0:T(8,128)(2,1)}, u32[]{:S(2)}) copy-start(bf16[128,4096]{1,0:T(8,128)(2,1)} %q_ref.1) | copy-start | bytes 3145732

commit v2 on v1

v2 whole, which is shorter than its diff:
```python
import functools
import math

import jax
import jax.numpy as jnp
from jax import lax
from jax.experimental import pallas as pl
from jax.experimental.pallas import tpu as pltpu
from jax.sharding import PartitionSpec as P

QH = 32
KVH = 4
HD = 128
GROUP = QH // KVH
EXP2_SCALE = math.log2(math.e) / math.sqrt(HD)
GATHER_DEVICES = 16
MASKED = -1e30


def page_owners(prefix_table, branch_table, pool_size):
    page_ids = jnp.arange(pool_size, dtype=jnp.int32)
    is_prefix = jnp.any(prefix_table[:, None] == page_ids[None, :], 0)
    flat_table = branch_table.reshape(-1)
    table_branch = jnp.arange(flat_table.shape[0], dtype=jnp.int32) // branch_table.shape[1]
    owner_of = jnp.sum(
        jnp.where(flat_table[:, None] == page_ids[None, :], table_branch[:, None], 0), 0
    )
    return jnp.where(is_prefix, -1, owner_of)


def absorb(carry, query_heads, pages, block_allowed):
    run_max, run_total, run_acc = carry
    page_tokens = pages.shape[1]
    token_count = pages.shape[0] * page_tokens
    kv_tokens = pages.reshape(token_count, 2, KVH, HD)
    keys = kv_tokens[:, 0]
    values = kv_tokens[:, 1]
    scores = jnp.einsum("rkgd,tkd->rkgt", query_heads, keys, preferred_element_type=jnp.float32) * (
        1.0 / math.sqrt(HD)
    )
    allowed = jnp.repeat(block_allowed, page_tokens)[None, None, None, :]
    masked = jnp.where(allowed, scores, -1e30)
    new_max = jnp.maximum(run_max, jnp.max(masked, -1))
    weights = jnp.where(allowed, jnp.exp(scores - new_max[..., None]), 0.0).astype(jnp.bfloat16)
    factor = jnp.exp(run_max - new_max)
    new_total = run_total * factor + jnp.sum(weights.astype(jnp.float32), -1)
    new_acc = run_acc * factor[..., None] + jnp.einsum(
        "rkgt,tkd->rkgd", weights, values, preferred_element_type=jnp.float32
    )
    return (new_max, new_total, new_acc)


def attend_general(queries, kv_pool, page_allowed, live_count):
    row_count = queries.shape[0]
    pages = lax.all_gather(kv_pool, "seq", axis=0, tiled=True)
    page_tokens = pages.shape[1]
    block_pages = max(1, max(128, 32768 // row_count) // page_tokens)
    while pages.shape[0] % block_pages:
        block_pages = block_pages - 1
    blocks = pages.reshape((-1, block_pages) + pages.shape[1:])
    block_allowed = page_allowed.reshape(-1, block_pages)
    query_heads = queries.reshape(row_count, KVH, GROUP, HD)
    start = (
        jnp.full((row_count, KVH, GROUP), -1e30, jnp.float32),
        jnp.zeros((row_count, KVH, GROUP), jnp.float32),
        jnp.zeros((row_count, KVH, GROUP, HD), jnp.float32),
    )

    def scan_step(state, inputs):
        block, allowed = inputs
        return (absorb(state, query_heads, block, allowed), None)

    (run_max, run_total, run_acc), unused = lax.scan(scan_step, start, (blocks, block_allowed))
    mixed = (run_acc / run_total[..., None]).reshape(row_count, QH * HD)
    live = jnp.arange(row_count, dtype=jnp.int32) < live_count
    return jnp.where(live[:, None], mixed, 0.0).astype(jnp.bfloat16)


MOVES = {"core": 1, "x": 2, "z1": 4, "z2": 8}
PLAN = (
    ("z2", 0, ()),
    ("z1", 0, ()),
    ("x", 0, ()),
    ("core", 0, ()),
    ("prepare", ()),
    ("x", 4, ("prepare",)),
    ("z1", 8, ()),
    ("x", 8, ()),
    ("x", 12, ()),
    ("core", 2, ()),
    ("core", 4, ()),
    ("core", 6, ()),
    ("core", 8, ()),
    ("core", 10, ()),
    ("core", 12, ()),
    ("attend", (0, 1, 2, 3, 4, 5, 6, 7), ()),
    ("core", 14, ("attend1",)),
    ("attend", (8, 9, 10, 11, 12, 13, 14, 15), ()),
)


def permute(block, move):
    pairs = [(index, index ^ MOVES[move]) for index in range(GATHER_DEVICES)]
    return lax.ppermute(block, "seq", pairs)


def after(value, *earlier):
    return lax.optimization_barrier((value,) + earlier)[0] if earlier else value


def prepare_kernel(
    q_ref, shard_ref, lengths_in, owner_in, table_in, q_out, shard_out, live_ref, *rest, stages
):
    bias_refs, (lengths_ref, owner_ref, table_ref, sems) = rest[:-4], rest[-4:]
    ends = (
        (lengths_in, lengths_ref),
        (owner_in, owner_ref),
        (table_in, table_ref),
        (q_ref, q_out),
        (shard_ref, shard_out),
    )
    copies = [pltpu.make_async_copy(*pair, sems.at[i]) for i, pair in enumerate(ends)]
    for copy in copies:
        copy.start()
    for copy in copies[:3]:
        copy.wait()
    pages_dev, page_tokens = shard_ref.shape[:2]
    me = lax.axis_index("seq")
    rows = q_ref.shape[0]
    owner_width = GATHER_DEVICES // owner_ref.shape[0]
    branch = owner_ref[me // owner_width]
    live_count = lengths_ref[branch] - me % owner_width * rows
    live_ref[...] = jnp.where(
        lax.broadcasted_iota(jnp.int32, live_ref.shape, 0) < live_count, 1.0, 0.0
    )
    entries = table_ref.shape[0]
    history = entries // owner_ref.shape[0]
    piece_tokens = pages_dev * page_tokens
    for numbers, bias_ref in zip(stages, bias_refs):
        token = lax.broadcasted_iota(jnp.int32, bias_ref.shape, 1)
        page = jnp.full(bias_ref.shape, -1, jnp.int32)
        for i, number in enumerate(numbers):
            local = lax.shift_right_logical(
                token - i * piece_tokens, page_tokens.bit_length() - 1
            )
            page = jnp.where(token >= i * piece_tokens, (me ^ number) * pages_dev + local, page)
        masked = token >= len(numbers) * piece_tokens
        for e in range(entries):
            other = jnp.where(e // history == branch, -1, table_ref[e])
            masked = masked | (page == other)
        bias_ref[...] = jnp.where(masked, MASKED, 0.0)
    for copy in copies[3:]:
        copy.wait()


def prepare(queries, shard, span_lengths, owner_branch, branch_table, stages):
    vmem = pl.BlockSpec(memory_space=pltpu.VMEM)
    tables = (span_lengths, owner_branch, branch_table.reshape(-1))
    inputs = [
        pltpu.with_memory_space_constraint(value, pltpu.HBM) for value in (queries, shard) + tables
    ]
    shapes = [
        jax.ShapeDtypeStruct(queries.shape, queries.dtype),
        jax.ShapeDtypeStruct(shard.shape, shard.dtype),
        jax.ShapeDtypeStruct((queries.shape[0], HD), jnp.float32),
    ]
    for numbers in stages:
        held = len(numbers) * shard.shape[0] * shard.shape[1]
        shapes.append(jax.ShapeDtypeStruct((1, held + -held % HD), jnp.float32))
    return pl.pallas_call(
        functools.partial(prepare_kernel, stages=stages),
        out_shape=shapes,
        in_specs=[pl.BlockSpec(memory_space=pltpu.HBM)] * len(inputs),
        out_specs=[vmem] * len(shapes),
        scratch_shapes=[pltpu.SMEM(table.shape, table.dtype) for table in tables]
        + [pltpu.SemaphoreType.DMA((len(inputs),))],
        compiler_params=pltpu.CompilerParams(vmem_limit_bytes=4 << 20),
        name="prepare",
    )(*inputs)


def attention_kernel(*refs, count, first, last):
    q_ref, bias_ref, live_ref = refs[:3]
    piece_refs = refs[3 : 3 + count]
    rest = list(refs[3 + count :])
    old_sums, old_max = (None, None) if first else (rest.pop(0), rest.pop(0))
    out_ref, out_max = (rest.pop(0), None) if last else (rest.pop(0), rest.pop(0))
    keys, values = rest
    rows = q_ref.shape[0]
    tokens = keys.shape[1]
    piece_tokens = piece_refs[0].shape[0] * piece_refs[0].shape[1]
    values[:, :, HD:] = jnp.ones((KVH, tokens, HD), jnp.bfloat16)
    held = count * piece_tokens
    if held < tokens:
        keys[:, held:, :] = jnp.zeros((KVH, tokens - held, HD), jnp.bfloat16)
        values[:, held:, :HD] = jnp.zeros((KVH, tokens - held, HD), jnp.bfloat16)
    for i in range(count):
        block = piece_refs[i][...].reshape(piece_tokens, 2 * KVH * HD)
        span = slice(i * piece_tokens, (i + 1) * piece_tokens)
        for h in range(KVH):
            keys[h, span, :] = block[:, h * HD : (h + 1) * HD]
            values[h, span, :HD] = block[:, (KVH + h) * HD : (KVH + h + 1) * HD]
    bias = bias_ref[...]
    live = live_ref[...] > 0.0
    for q_head in range(QH):
        h = q_head // GROUP
        lanes = slice(q_head * HD, (q_head + 1) * HD)
        wide = slice(q_head * 2 * HD, (q_head + 1) * 2 * HD)
        scores = lax.dot_general(
            q_ref[:, lanes], keys[h], (((1,), (1,)), ((), ())), preferred_element_type=jnp.float32
        )
        scores = scores + bias
        row_max = jnp.broadcast_to(jnp.max(scores, -1, keepdims=True), (rows, HD))
        if not first:
            before = old_max[:, lanes]
            row_max = jnp.maximum(row_max, before)
        weights = jnp.concatenate(
            [
                jnp.exp2((scores[:, t : t + HD] - row_max) * EXP2_SCALE).astype(jnp.bfloat16)
                for t in range(0, tokens, HD)
            ],
            1,
        )
        sums = jnp.dot(weights, values[h], preferred_element_type=jnp.float32)
        mixed, totals = sums[:, :HD], sums[:, HD:]
        if not first:
            factor = jnp.exp2((before - row_max) * EXP2_SCALE)
            old = old_sums[:, wide]
            mixed, totals = mixed + old[:, :HD] * factor, totals + old[:, HD:] * factor
        if last:
            out_ref[:, lanes] = jnp.where(live, mixed / totals, 0.0).astype(jnp.bfloat16)
        else:
            out_ref[:, wide] = jnp.concatenate([mixed, totals], 1)
            out_max[:, lanes] = row_max


def attend_pieces(queries, bias, live, pieces, state, last):
    rows, features = queries.shape
    count = len(pieces)
    tokens = bias.shape[1]
    vmem = pl.BlockSpec(memory_space=pltpu.VMEM)
    state_shape = (
        jax.ShapeDtypeStruct((rows, 2 * features), jnp.float32),
        jax.ShapeDtypeStruct((rows, features), jnp.float32),
    )
    return pl.pallas_call(
        functools.partial(attention_kernel, count=count, first=not state, last=last),
        out_shape=jax.ShapeDtypeStruct((rows, features), jnp.bfloat16) if last else state_shape,
        in_specs=[vmem] * (3 + count + len(state)),
        out_specs=vmem if last else (vmem, vmem),
        scratch_shapes=[
            pltpu.VMEM((KVH, tokens, HD), jnp.bfloat16),
            pltpu.VMEM((KVH, tokens, 2 * HD), jnp.bfloat16),
        ],
        compiler_params=pltpu.CompilerParams(vmem_limit_bytes=32 << 20),
        cost_estimate=pl.CostEstimate(
            flops=4 * rows * features * tokens,
            bytes_accessed=4 * rows * features + 2 * tokens * KVH * HD * 2,
            transcendentals=rows * QH * tokens,
        ),
        name="attention_last" if last else "attention_stage",
    )(queries, bias, live, *pieces, *state)


def attend_staged(queries, kv_pool, span_lengths, owner_branch, branch_table):
    stages = [step[1] for step in PLAN if step[0] == "attend"]
    held = {0: kv_pool}
    marks = {}
    state, stage, biases = (), 0, None
    for step in PLAN:
        earlier = [marks[name] for name in step[-1]]
        if step[0] == "prepare":
            queries, own, live, *biases = prepare(
                after(queries, *earlier), kv_pool, span_lengths, owner_branch, branch_table, stages
            )
            marks["prepare"] = live
        elif step[0] == "attend":
            pieces = [own if number == 0 else held[number] for number in step[1]]
            bias = after(biases[stage], *earlier)
            stage += 1
            state = attend_pieces(queries, bias, live, pieces, state, stage == len(stages))
            if stage < len(stages):
                marks["attend%d" % stage] = state[1]
        else:
            number = step[1] ^ MOVES[step[0]]
            held[number] = permute(after(held[step[1]], *earlier), step[0])
            marks[number] = held[number]
    return state


def attend_anywhere(queries, kv_pool, span_lengths, owner_branch, prefix_table, branch_table):
    device_count = lax.axis_size("seq")
    self_index = lax.axis_index("seq")
    owner_width = device_count // span_lengths.shape[0]
    branch = owner_branch[self_index // owner_width]
    live_count = span_lengths[branch] - self_index % owner_width * queries.shape[0]
    slot_branch = page_owners(prefix_table, branch_table, kv_pool.shape[0] * device_count)
    page_allowed = (slot_branch < 0) | (slot_branch == branch)
    return attend_general(queries, kv_pool, page_allowed, live_count)


def per_device(queries, kv_pool, span_lengths, owner_branch, prefix_table, branch_table):
    if lax.axis_size("seq") == GATHER_DEVICES and kv_pool.shape[1] == 8:
        return attend_staged(queries, kv_pool, span_lengths, owner_branch, branch_table)
    return attend_anywhere(
        queries, kv_pool, span_lengths, owner_branch, prefix_table, branch_table
    )


def solution(mesh):
    return jax.shard_map(
        per_device,
        mesh=mesh,
        in_specs=(
            P(("grp", "seq"), None),
            P(("grp", "seq"), None, None),
            P("grp"),
            P("grp"),
            P("grp"),
            P("grp", None),
        ),
        out_specs=P(("grp", "seq"), None),
        check_vma=False,
    )
```

time: 36.5 us -> 32.2 us (0.88)
  local copies, waits for them, and re-layouts: 4.03 us -> 0 us
  Pallas kernels: 8.88 us -> 11.9 us
  other arithmetic: 2.18 us -> 0 us
  between operations: 2.07 us -> 0.05 us
  waiting for transfers between devices: 5.53 us -> 6.17 us
  starting transfers between devices: 13.5 us -> 13.9 us
    pallas_call x1 -> x3, Pallas kernels: 8.88 us -> 11.9 us  [the longest x2 10.7 us: attend_pieces(): pl.pallas_call(functools.partial(attention_kernel, count=count, first=not...]
    dynamic_slice x2 -> x0, local copies, waits for them, and re-layouts: 1.85 us -> none  [the longest x1 1.24 us: per_device(): my_branch = owner_branch[self_index // owner_width]]
    unnamed x6 -> x0, local copies, waits for them, and re-layouts: 1.23 us -> none
    reduce_or x1 -> x0, other arithmetic: 0.77 us -> none  [page_owners(): is_prefix = jnp.any(prefix_table[:, None] == page_ids[None, :], 0)]
    reduce_sum x1 -> x0, other arithmetic: 0.74 us -> none  [page_owners(): jnp.sum(jnp.where(flat_table[:, None] == page_ids[None, :], table_branch[...]
    or x1 -> x0, other arithmetic: 0.65 us -> none  [per_device(): page_allowed = (slot_branch < 0) | (slot_branch == my_branch)]
    ppermute x15, waiting for transfers between devices: 5.53 us -> 6.17 us  [permute(): return lax.ppermute(block, 'seq', pairs)]
    gather x1 -> x0, local copies, waits for them, and re-layouts: 0.58 us -> none  [per_device(): page_allowed.reshape(device_count, pages_dev)]
  transfers between devices with their start and end apart: 15 -> 15, of which waited for: 3 -> 5; matrix products, arithmetic and copies ran while one was open for 14% -> 0% of each run, Pallas kernels for 0% -> 18%
where the time goes in v2:
time: 32.2 us; the launch traced here: 32.1 us
  starting transfers between devices  13.9 us (43%)
  Pallas kernels  11.9 us (37%)
  waiting for transfers between devices  6.17 us (19%)
    ppermute x15, starting transfers between devices, permute(): return lax.ppermute(block, 'seq', pairs)  13.9 us
    pallas_call x2, Pallas kernels, attend_pieces(): pl.pallas_call(functools.partial(attention_kernel, count=count, first=not...  10.7 us
    ppermute x15, waiting for transfers between devices, permute(): return lax.ppermute(block, 'seq', pairs)  6.17 us
    pallas_call x1, Pallas kernels, prepare(): pl.pallas_call(functools.partial(prepare_kernel, stages=stages), out_shap...  1.27 us
  transfers between devices with their start and end apart: 15, of which 5 were waited for; matrix products, arithmetic and copies ran while one was open for 0% of the time, Pallas kernels for 18%

profile of v2, /device:TPU:0, one launch (start us, length us, event | category | flops | bytes accessed | tf_op | source)
XLA Modules:
  0.0 32.1 jit_solution(9857509460535802809)
XLA Ops:
  0.0 3.0 %collective-permute-start.10 = (bf16[9,8,1024]{2,1,0:T(8,128)(2,1)}, bf16[9,8,1024]{2,1,0:T(8,128)(2,1)S(1)}, u32[]{:S(2)}, u32[]{:S(2)}) collective-permute-start(bf16[9,8,1024]{2,1,0:T(8,128)(2,1)} %shard_ref.1), channel_id=1, source_target_pairs={{0,4},{1,5},{2,6},{3,7},{4,0},{5,1},{6,2},{7,3},{8,12},{9,13},{10,... | collective-permute-start | bytes 442376 | tf_op jit(solution)/shard_map/ppermute | solution.py:104
  3.0 2.6 %collective-permute-start = (bf16[9,8,1024]{2,1,0:T(8,128)(2,1)}, bf16[9,8,1024]{2,1,0:T(8,128)(2,1)S(1)}, u32[]{:S(2)}, u32[]{:S(2)}) collective-permute-start(bf16[9,8,1024]{2,1,0:T(8,128)(2,1)} %shard_ref.1), channel_id=1, source_target_pairs={{0,8},{1,9},{2,10},{3,11},{4,12},{5,13},{6,14},{7,15},{8,0},{9,1},... | collective-permute-start | bytes 442376 | tf_op jit(solution)/shard_map/ppermute | solution.py:104
  5.6 0.0 collective-permute-start.7
  5.6 1.5 %collective-permute-start.8 = (bf16[9,8,1024]{2,1,0:T(8,128)(2,1)}, bf16[9,8,1024]{2,1,0:T(8,128)(2,1)S(1)}, u32[]{:S(2)}, u32[]{:S(2)}) collective-permute-start(bf16[9,8,1024]{2,1,0:T(8,128)(2,1)} %shard_ref.1), channel_id=1, source_target_pairs={{0,2},{1,3},{2,0},{3,1},{4,6},{5,7},{6,4},{7,5},{8,10},{9,11},{10,... | collective-permute-start | bytes 442376 | tf_op jit(solution)/shard_map/ppermute | solution.py:104
  7.1 1.3 %prepare.1 = (bf16[128,4096]{1,0:T(8,128)(2,1)S(1)}, bf16[9,8,1024]{2,1,0:T(8,128)(2,1)S(1)}, f32[128,128]{1,0:T(8,128)S(1)}, f32[1,640]{1,0:T(1,128)S(1)}, f32[1,640]{1,0:T(1,128)S(1)}) custom-call(bf16[128,4096]{1,0:T(8,128)(2,1)} %q_ref.1, bf16[9,8,1024]{2,1,0:T(8,128)(2,1)} %shard_ref.1, s32[16]{0:T(128)} %lengths_in.1, s32[16]{0:T(128)} %owner_in.1, ...), custom_call_target="tpu_custom_call" | custom-call | tf_op jit(solution)/shard_map/prepare/pallas_call | solution.py:170
  8.4 1.2 %collective-permute-done.10.refs_7_ = bf16[9,8,1024]{2,1,0:T(8,128)(2,1)S(1)} collective-permute-done((bf16[9,8,1024]{2,1,0:T(8,128)(2,1)}, bf16[9,8,1024]{2,1,0:T(8,128)(2,1)S(1)}, u32[]{:S(2)}, u32[]{:S(2)}) %collective-permute-start.10) | collective-permute-done | bytes 147488 | tf_op jit(solution)/shard_map/ppermute | solution.py:104
  9.6 1.8 %collective-permute-start.12 = (bf16[9,8,1024]{2,1,0:T(8,128)(2,1)S(1)}, bf16[9,8,1024]{2,1,0:T(8,128)(2,1)S(1)}, u32[]{:S(2)}, u32[]{:S(2)}) collective-permute-start(bf16[9,8,1024]{2,1,0:T(8,128)(2,1)S(1)} %collective-permute-done.10.refs_7_), channel_id=1, source_target_pairs={{0,2},{1,3},{2,0},{3,1},{4,6},{5,7},{6,4},{7,5},{8,10},{9,11},{10,... | collective-permute-start | bytes 442376 | tf_op jit(solution)/shard_map/ppermute | solution.py:104
  11.4 1.2 %collective-permute-done.refs_3_ = bf16[9,8,1024]{2,1,0:T(8,128)(2,1)S(1)} collective-permute-done((bf16[9,8,1024]{2,1,0:T(8,128)(2,1)}, bf16[9,8,1024]{2,1,0:T(8,128)(2,1)S(1)}, u32[]{:S(2)}, u32[]{:S(2)}) %collective-permute-start) | collective-permute-done | bytes 147488 | tf_op jit(solution)/shard_map/ppermute | solution.py:104
  12.7 0.4 %collective-permute-start.4 = (bf16[9,8,1024]{2,1,0:T(8,128)(2,1)S(1)}, bf16[9,8,1024]{2,1,0:T(8,128)(2,1)S(1)}, u32[]{:S(2)}, u32[]{:S(2)}) collective-permute-start(bf16[9,8,1024]{2,1,0:T(8,128)(2,1)S(1)} %collective-permute-done.refs_3_), channel_id=1, source_target_pairs={{0,4},{1,5},{2,6},{3,7},{4,0},{5,1},{6,2},{7,3},{8,12},{9,13},{10,... | collective-permute-start | bytes 442376 | tf_op jit(solution)/shard_map/ppermute | solution.py:104
  13.1 1.5 %collective-permute-start.2 = (bf16[9,8,1024]{2,1,0:T(8,128)(2,1)S(1)}, bf16[9,8,1024]{2,1,0:T(8,128)(2,1)S(1)}, u32[]{:S(2)}, u32[]{:S(2)}) collective-permute-start(bf16[9,8,1024]{2,1,0:T(8,128)(2,1)S(1)} %collective-permute-done.refs_3_), channel_id=1, source_target_pairs={{0,2},{1,3},{2,0},{3,1},{4,6},{5,7},{6,4},{7,5},{8,10},{9,11},{10,... | collective-permute-start | bytes 442376 | tf_op jit(solution)/shard_map/ppermute | solution.py:104
  14.6 0.0 collective-permute-done.7.refs_4_
  14.6 0.0 collective-permute-start.11
  14.6 0.0 collective-permute-done.8.refs_5_
  14.6 0.5 %collective-permute-start.9 = (bf16[9,8,1024]{2,1,0:T(8,128)(2,1)S(1)}, bf16[9,8,1024]{2,1,0:T(8,128)(2,1)S(1)}, u32[]{:S(2)}, u32[]{:S(2)}) collective-permute-start(bf16[9,8,1024]{2,1,0:T(8,128)(2,1)S(1)} %collective-permute-done.8.refs_5_), channel_id=1, source_target_pairs={{0,1},{1,0},{2,3},{3,2},{4,5},{5,4},{6,7},{7,6},{8,9},{9,8},{10,11... | collective-permute-start | bytes 442376 | tf_op jit(solution)/shard_map/ppermute | solution.py:104
  15.1 1.1 %collective-permute-done.12.refs_9_ = bf16[9,8,1024]{2,1,0:T(8,128)(2,1)S(1)} collective-permute-done((bf16[9,8,1024]{2,1,0:T(8,128)(2,1)S(1)}, bf16[9,8,1024]{2,1,0:T(8,128)(2,1)S(1)}, u32[]{:S(2)}, u32[]{:S(2)}) %collective-permute-start.12) | collective-permute-done | bytes 147488 | tf_op jit(solution)/shard_map/ppermute | solution.py:104
  16.2 0.0 collective-permute-start.13
  16.2 1.6 %collective-permute-done.4.refs_7_ = bf16[9,8,1024]{2,1,0:T(8,128)(2,1)S(1)} collective-permute-done((bf16[9,8,1024]{2,1,0:T(8,128)(2,1)S(1)}, bf16[9,8,1024]{2,1,0:T(8,128)(2,1)S(1)}, u32[]{:S(2)}, u32[]{:S(2)}) %collective-permute-start.4) | collective-permute-done | bytes 147488 | tf_op jit(solution)/shard_map/ppermute | solution.py:104
  17.8 1.5 %collective-permute-start.6 = (bf16[9,8,1024]{2,1,0:T(8,128)(2,1)S(1)}, bf16[9,8,1024]{2,1,0:T(8,128)(2,1)S(1)}, u32[]{:S(2)}, u32[]{:S(2)}) collective-permute-start(bf16[9,8,1024]{2,1,0:T(8,128)(2,1)S(1)} %collective-permute-done.4.refs_7_), channel_id=1, source_target_pairs={{0,2},{1,3},{2,0},{3,1},{4,6},{5,7},{6,4},{7,5},{8,10},{9,11},{10,... | collective-permute-start | bytes 442376 | tf_op jit(solution)/shard_map/ppermute | solution.py:104
  19.3 0.0 collective-permute-done.2.refs_5_
  19.3 0.0 collective-permute-start.1
  19.3 0.0 collective-permute-done.11.refs_8_
  19.3 0.5 %collective-permute-start.5 = (bf16[9,8,1024]{2,1,0:T(8,128)(2,1)S(1)}, bf16[9,8,1024]{2,1,0:T(8,128)(2,1)S(1)}, u32[]{:S(2)}, u32[]{:S(2)}) collective-permute-start(bf16[9,8,1024]{2,1,0:T(8,128)(2,1)S(1)} %collective-permute-done.4.refs_7_), channel_id=1, source_target_pairs={{0,1},{1,0},{2,3},{3,2},{4,5},{5,4},{6,7},{7,6},{8,9},{9,8},{10,11... | collective-permute-start | bytes 442376 | tf_op jit(solution)/shard_map/ppermute | solution.py:104
  19.8 0.0 collective-permute-done.9.refs_6_
  19.8 0.1 collective-permute-start.3
  19.9 0.0 collective-permute-done.13.refs_10_
  19.9 4.6 %attention_stage.1 = (f32[128,8192]{1,0:T(8,128)S(1)}, f32[128,4096]{1,0:T(8,128)S(1)}) custom-call(bf16[128,4096]{1,0:T(8,128)(2,1)S(1)} %get-tuple-element.14.refs_0_, f32[1,640]{1,0:T(1,128)S(1)} %get-tuple-element.17.refs_1_, f32[128,128]{1,0:T(8,128)S(1)} %get-tuple-element.16.refs_2_, bf16[9,8,1024]{2,1,0:T(8,128)(2,1)S(1)} %get-tuple-element.18.refs_3_, ...), custom_call_target="tpu_custom_call" | custom-call | flops 1342177280 | bytes 3407872 | tf_op jit(solution)/shard_map/attention_stage/pallas_call | solution.py:246
  24.5 0.0 collective-permute-done.6.refs_9_
  24.5 0.5 %collective-permute-start.14 = (bf16[9,8,1024]{2,1,0:T(8,128)(2,1)S(1)}, bf16[9,8,1024]{2,1,0:T(8,128)(2,1)S(1)}, u32[]{:S(2)}, u32[]{:S(2)}) collective-permute-start(bf16[9,8,1024]{2,1,0:T(8,128)(2,1)S(1)} %collective-permute-done.6.refs_9_), channel_id=1, source_target_pairs={{0,1},{1,0},{2,3},{3,2},{4,5},{5,4},{6,7},{7,6},{8,9},{9,8},{10,11... | collective-permute-start | bytes 442376 | tf_op jit(solution)/shard_map/ppermute | solution.py:104
  25.0 0.0 collective-permute-done.1.refs_4_
  25.0 0.0 collective-permute-done.5.refs_8_
  25.0 0.0 collective-permute-done.3.refs_6_
  25.0 1.0 %collective-permute-done.14.refs_10_ = bf16[9,8,1024]{2,1,0:T(8,128)(2,1)S(1)} collective-permute-done((bf16[9,8,1024]{2,1,0:T(8,128)(2,1)S(1)}, bf16[9,8,1024]{2,1,0:T(8,128)(2,1)S(1)}, u32[]{:S(2)}, u32[]{:S(2)}) %collective-permute-start.14) | collective-permute-done | bytes 147488 | tf_op jit(solution)/shard_map/ppermute | solution.py:104
  26.0 6.1 %attention_last.1 = bf16[128,4096]{1,0:T(8,128)(2,1)} custom-call(bf16[128,4096]{1,0:T(8,128)(2,1)S(1)} %get-tuple-element.14.refs_0_, f32[1,640]{1,0:T(1,128)S(1)} %get-tuple-element.15.refs_1_, f32[128,128]{1,0:T(8,128)S(1)} %get-tuple-element.16.refs_2_, bf16[9,8,1024]{2,1,0:T(8,128)(2,1)S(1)} %collective-permute-done.refs_3_, ...), custom_call_target="tpu_custom_call" | custom-call | flops 1342177280 | bytes 3407872 | tf_op jit(solution)/shard_map/attention_last/pallas_call | solution.py:246
Async XLA Ops:
  0.0 9.6 %collective-permute-start.10 = (bf16[9,8,1024]{2,1,0:T(8,128)(2,1)}, bf16[9,8,1024]{2,1,0:T(8,128)(2,1)S(1)}, u32[]{:S(2)}, u32[]{:S(2)}) collective-permute-start(bf16[9,8,1024]{2,1,0:T(8,128)(2,1)} %shard_ref.1), channel_id=1, source_target_pairs={{0,4},{1,5},{2,6},{3,7},{4,0},{5,1},{6,2},{7,3},{8,12},{9,13},{10,... | collective-permute-start | bytes 442376 | tf_op jit(solution)/shard_map/ppermute | solution.py:104
  3.0 9.6 %collective-permute-start = (bf16[9,8,1024]{2,1,0:T(8,128)(2,1)}, bf16[9,8,1024]{2,1,0:T(8,128)(2,1)S(1)}, u32[]{:S(2)}, u32[]{:S(2)}) collective-permute-start(bf16[9,8,1024]{2,1,0:T(8,128)(2,1)} %shard_ref.1), channel_id=1, source_target_pairs={{0,8},{1,9},{2,10},{3,11},{4,12},{5,13},{6,14},{7,15},{8,0},{9,1},... | collective-permute-start | bytes 442376 | tf_op jit(solution)/shard_map/ppermute | solution.py:104
  5.6 9.0 %collective-permute-start.7 = (bf16[9,8,1024]{2,1,0:T(8,128)(2,1)}, bf16[9,8,1024]{2,1,0:T(8,128)(2,1)S(1)}, u32[]{:S(2)}, u32[]{:S(2)}) collective-permute-start(bf16[9,8,1024]{2,1,0:T(8,128)(2,1)} %shard_ref.1), channel_id=1, source_target_pairs={{0,1},{1,0},{2,3},{3,2},{4,5},{5,4},{6,7},{7,6},{8,9},{9,8},{10,11... | collective-permute-start | bytes 442376 | tf_op jit(solution)/shard_map/ppermute | solution.py:104
  5.6 9.0 %collective-permute-start.8 = (bf16[9,8,1024]{2,1,0:T(8,128)(2,1)}, bf16[9,8,1024]{2,1,0:T(8,128)(2,1)S(1)}, u32[]{:S(2)}, u32[]{:S(2)}) collective-permute-start(bf16[9,8,1024]{2,1,0:T(8,128)(2,1)} %shard_ref.1), channel_id=1, source_target_pairs={{0,2},{1,3},{2,0},{3,1},{4,6},{5,7},{6,4},{7,5},{8,10},{9,11},{10,... | collective-permute-start | bytes 442376 | tf_op jit(solution)/shard_map/ppermute | solution.py:104
  9.6 6.6 %collective-permute-start.12 = (bf16[9,8,1024]{2,1,0:T(8,128)(2,1)S(1)}, bf16[9,8,1024]{2,1,0:T(8,128)(2,1)S(1)}, u32[]{:S(2)}, u32[]{:S(2)}) collective-permute-start(bf16[9,8,1024]{2,1,0:T(8,128)(2,1)S(1)} %collective-permute-done.10.refs_7_), channel_id=1, source_target_pairs={{0,2},{1,3},{2,0},{3,1},{4,6},{5,7},{6,4},{7,5},{8,10},{9,11},{10,... | collective-permute-start | bytes 442376 | tf_op jit(solution)/shard_map/ppermute | solution.py:104
  12.7 5.1 %collective-permute-start.4 = (bf16[9,8,1024]{2,1,0:T(8,128)(2,1)S(1)}, bf16[9,8,1024]{2,1,0:T(8,128)(2,1)S(1)}, u32[]{:S(2)}, u32[]{:S(2)}) collective-permute-start(bf16[9,8,1024]{2,1,0:T(8,128)(2,1)S(1)} %collective-permute-done.refs_3_), channel_id=1, source_target_pairs={{0,4},{1,5},{2,6},{3,7},{4,0},{5,1},{6,2},{7,3},{8,12},{9,13},{10,... | collective-permute-start | bytes 442376 | tf_op jit(solution)/shard_map/ppermute | solution.py:104
  13.1 6.2 %collective-permute-start.2 = (bf16[9,8,1024]{2,1,0:T(8,128)(2,1)S(1)}, bf16[9,8,1024]{2,1,0:T(8,128)(2,1)S(1)}, u32[]{:S(2)}, u32[]{:S(2)}) collective-permute-start(bf16[9,8,1024]{2,1,0:T(8,128)(2,1)S(1)} %collective-permute-done.refs_3_), channel_id=1, source_target_pairs={{0,2},{1,3},{2,0},{3,1},{4,6},{5,7},{6,4},{7,5},{8,10},{9,11},{10,... | collective-permute-start | bytes 442376 | tf_op jit(solution)/shard_map/ppermute | solution.py:104
  14.6 4.7 %collective-permute-start.11 = (bf16[9,8,1024]{2,1,0:T(8,128)(2,1)S(1)}, bf16[9,8,1024]{2,1,0:T(8,128)(2,1)S(1)}, u32[]{:S(2)}, u32[]{:S(2)}) collective-permute-start(bf16[9,8,1024]{2,1,0:T(8,128)(2,1)S(1)} %collective-permute-done.10.refs_7_), channel_id=1, source_target_pairs={{0,1},{1,0},{2,3},{3,2},{4,5},{5,4},{6,7},{7,6},{8,9},{9,8},{10,11... | collective-permute-start | bytes 442376 | tf_op jit(solution)/shard_map/ppermute | solution.py:104
  14.6 5.2 %collective-permute-start.9 = (bf16[9,8,1024]{2,1,0:T(8,128)(2,1)S(1)}, bf16[9,8,1024]{2,1,0:T(8,128)(2,1)S(1)}, u32[]{:S(2)}, u32[]{:S(2)}) collective-permute-start(bf16[9,8,1024]{2,1,0:T(8,128)(2,1)S(1)} %collective-permute-done.8.refs_5_), channel_id=1, source_target_pairs={{0,1},{1,0},{2,3},{3,2},{4,5},{5,4},{6,7},{7,6},{8,9},{9,8},{10,11... | collective-permute-start | bytes 442376 | tf_op jit(solution)/shard_map/ppermute | solution.py:104
  16.2 3.7 %collective-permute-start.13 = (bf16[9,8,1024]{2,1,0:T(8,128)(2,1)S(1)}, bf16[9,8,1024]{2,1,0:T(8,128)(2,1)S(1)}, u32[]{:S(2)}, u32[]{:S(2)}) collective-permute-start(bf16[9,8,1024]{2,1,0:T(8,128)(2,1)S(1)} %collective-permute-done.12.refs_9_), channel_id=1, source_target_pairs={{0,1},{1,0},{2,3},{3,2},{4,5},{5,4},{6,7},{7,6},{8,9},{9,8},{10,11... | collective-permute-start | bytes 442376 | tf_op jit(solution)/shard_map/ppermute | solution.py:104
  17.8 6.7 %collective-permute-start.6 = (bf16[9,8,1024]{2,1,0:T(8,128)(2,1)S(1)}, bf16[9,8,1024]{2,1,0:T(8,128)(2,1)S(1)}, u32[]{:S(2)}, u32[]{:S(2)}) collective-permute-start(bf16[9,8,1024]{2,1,0:T(8,128)(2,1)S(1)} %collective-permute-done.4.refs_7_), channel_id=1, source_target_pairs={{0,2},{1,3},{2,0},{3,1},{4,6},{5,7},{6,4},{7,5},{8,10},{9,11},{10,... | collective-permute-start | bytes 442376 | tf_op jit(solution)/shard_map/ppermute | solution.py:104
  19.3 5.7 %collective-permute-start.1 = (bf16[9,8,1024]{2,1,0:T(8,128)(2,1)S(1)}, bf16[9,8,1024]{2,1,0:T(8,128)(2,1)S(1)}, u32[]{:S(2)}, u32[]{:S(2)}) collective-permute-start(bf16[9,8,1024]{2,1,0:T(8,128)(2,1)S(1)} %collective-permute-done.refs_3_), channel_id=1, source_target_pairs={{0,1},{1,0},{2,3},{3,2},{4,5},{5,4},{6,7},{7,6},{8,9},{9,8},{10,11... | collective-permute-start | bytes 442376 | tf_op jit(solution)/shard_map/ppermute | solution.py:104
  19.3 5.7 %collective-permute-start.5 = (bf16[9,8,1024]{2,1,0:T(8,128)(2,1)S(1)}, bf16[9,8,1024]{2,1,0:T(8,128)(2,1)S(1)}, u32[]{:S(2)}, u32[]{:S(2)}) collective-permute-start(bf16[9,8,1024]{2,1,0:T(8,128)(2,1)S(1)} %collective-permute-done.4.refs_7_), channel_id=1, source_target_pairs={{0,1},{1,0},{2,3},{3,2},{4,5},{5,4},{6,7},{7,6},{8,9},{9,8},{10,11... | collective-permute-start | bytes 442376 | tf_op jit(solution)/shard_map/ppermute | solution.py:104
  19.8 5.2 %collective-permute-start.3 = (bf16[9,8,1024]{2,1,0:T(8,128)(2,1)S(1)}, bf16[9,8,1024]{2,1,0:T(8,128)(2,1)S(1)}, u32[]{:S(2)}, u32[]{:S(2)}) collective-permute-start(bf16[9,8,1024]{2,1,0:T(8,128)(2,1)S(1)} %collective-permute-done.2.refs_5_), channel_id=1, source_target_pairs={{0,1},{1,0},{2,3},{3,2},{4,5},{5,4},{6,7},{7,6},{8,9},{9,8},{10,11... | collective-permute-start | bytes 442376 | tf_op jit(solution)/shard_map/ppermute | solution.py:104
  24.5 1.5 %collective-permute-start.14 = (bf16[9,8,1024]{2,1,0:T(8,128)(2,1)S(1)}, bf16[9,8,1024]{2,1,0:T(8,128)(2,1)S(1)}, u32[]{:S(2)}, u32[]{:S(2)}) collective-permute-start(bf16[9,8,1024]{2,1,0:T(8,128)(2,1)S(1)} %collective-permute-done.6.refs_9_), channel_id=1, source_target_pairs={{0,1},{1,0},{2,3},{3,2},{4,5},{5,4},{6,7},{7,6},{8,9},{9,8},{10,11... | collective-permute-start | bytes 442376 | tf_op jit(solution)/shard_map/ppermute | solution.py:104

commit v3 on v2

--- a/solution.py
+++ b/solution.py
@@ -14,6 +14,7 @@
 GROUP = QH // KVH
 EXP2_SCALE = math.log2(math.e) / math.sqrt(HD)
 GATHER_DEVICES = 16
+TOGETHER = 4
 MASKED = -1e30
 
 
@@ -109,9 +110,9 @@
 
 
 def prepare_kernel(
-    q_ref, shard_ref, lengths_in, owner_in, table_in, q_out, shard_out, live_ref, *rest, stages
+    q_ref, shard_ref, lengths_in, owner_in, table_in, q_out, shard_out, live_ref, keep_ref, bias_ref, *rest
 ):
-    bias_refs, (lengths_ref, owner_ref, table_ref, sems) = rest[:-4], rest[-4:]
+    lengths_ref, owner_ref, table_ref, sems = rest
     ends = (
         (lengths_in, lengths_ref),
         (owner_in, owner_ref),
@@ -122,9 +123,11 @@
     copies = [pltpu.make_async_copy(*pair, sems.at[i]) for i, pair in enumerate(ends)]
     for copy in copies:
         copy.start()
+    keep_ref[...] = jnp.ones(keep_ref.shape, jnp.float32)
     for copy in copies[:3]:
         copy.wait()
     pages_dev, page_tokens = shard_ref.shape[:2]
+    piece_tokens = pages_dev * page_tokens
     me = lax.axis_index("seq")
     rows = q_ref.shape[0]
     owner_width = GATHER_DEVICES // owner_ref.shape[0]
@@ -135,40 +138,38 @@
     )
     entries = table_ref.shape[0]
     history = entries // owner_ref.shape[0]
-    piece_tokens = pages_dev * page_tokens
-    for numbers, bias_ref in zip(stages, bias_refs):
-        token = lax.broadcasted_iota(jnp.int32, bias_ref.shape, 1)
-        page = jnp.full(bias_ref.shape, -1, jnp.int32)
-        for i, number in enumerate(numbers):
-            local = lax.shift_right_logical(
-                token - i * piece_tokens, page_tokens.bit_length() - 1
-            )
-            page = jnp.where(token >= i * piece_tokens, (me ^ number) * pages_dev + local, page)
-        masked = token >= len(numbers) * piece_tokens
-        for e in range(entries):
-            other = jnp.where(e // history == branch, -1, table_ref[e])
-            masked = masked | (page == other)
-        bias_ref[...] = jnp.where(masked, MASKED, 0.0)
+    token = lax.broadcasted_iota(jnp.int32, bias_ref.shape, 1)
+    bias = jnp.zeros(bias_ref.shape, jnp.float32)
+    for e in range(entries):
+        page = table_ref[e]
+        device = page // pages_dev
+        begin = (device ^ me) * piece_tokens + (page - device * pages_dev) * page_tokens
+        seen = jnp.where(branch == e // history, 1.0, 0.0)
+        rows_of_page = pl.ds(pl.multiple_of(begin, page_tokens), page_tokens)
+        keep_ref[rows_of_page, :] = jnp.full((page_tokens, HD), seen, jnp.float32)
+        in_page = (token >= begin) & (token < begin + page_tokens)
+        bias = jnp.where(in_page, (1.0 - seen) * MASKED, bias)
+    bias_ref[...] = bias
     for copy in copies[3:]:
         copy.wait()
 
 
-def prepare(queries, shard, span_lengths, owner_branch, branch_table, stages):
+def prepare(queries, shard, span_lengths, owner_branch, branch_table):
     vmem = pl.BlockSpec(memory_space=pltpu.VMEM)
     tables = (span_lengths, owner_branch, branch_table.reshape(-1))
     inputs = [
         pltpu.with_memory_space_constraint(value, pltpu.HBM) for value in (queries, shard) + tables
     ]
+    tokens = GATHER_DEVICES * shard.shape[0] * shard.shape[1]
     shapes = [
         jax.ShapeDtypeStruct(queries.shape, queries.dtype),
         jax.ShapeDtypeStruct(shard.shape, shard.dtype),
         jax.ShapeDtypeStruct((queries.shape[0], HD), jnp.float32),
+        jax.ShapeDtypeStruct((tokens, HD), jnp.float32),
+        jax.ShapeDtypeStruct((1, tokens), jnp.float32),
     ]
-    for numbers in stages:
-        held = len(numbers) * shard.shape[0] * shard.shape[1]
-        shapes.append(jax.ShapeDtypeStruct((1, held + -held % HD), jnp.float32))
     return pl.pallas_call(
-        functools.partial(prepare_kernel, stages=stages),
+        prepare_kernel,
         out_shape=shapes,
         in_specs=[pl.BlockSpec(memory_space=pltpu.HBM)] * len(inputs),
         out_specs=[vmem] * len(shapes),
@@ -179,113 +180,196 @@
     )(*inputs)
 
 
-def attention_kernel(*refs, count, first, last):
-    q_ref, bias_ref, live_ref = refs[:3]
-    piece_refs = refs[3 : 3 + count]
-    rest = list(refs[3 + count :])
-    old_sums, old_max = (None, None) if first else (rest.pop(0), rest.pop(0))
-    out_ref, out_max = (rest.pop(0), None) if last else (rest.pop(0), rest.pop(0))
-    keys, values = rest
-    rows = q_ref.shape[0]
+def lay_out(piece_ref, h, keep):
+    piece_tokens = piece_ref.shape[0] * piece_ref.shape[1]
+    keys = piece_ref[:, :, h * HD : (h + 1) * HD].reshape(piece_tokens, HD)
+    values = piece_ref[:, :, (KVH + h) * HD : (KVH + h + 1) * HD].reshape(piece_tokens, HD)
+    return keys, values * keep, keep
+
+
+def stage_sums(q_ref, keep_ref, piece_refs, numbers, keys, values, old_sums, give):
     tokens = keys.shape[1]
     piece_tokens = piece_refs[0].shape[0] * piece_refs[0].shape[1]
-    values[:, :, HD:] = jnp.ones((KVH, tokens, HD), jnp.bfloat16)
-    held = count * piece_tokens
+    held = len(numbers) * piece_tokens
     if held < tokens:
         keys[:, held:, :] = jnp.zeros((KVH, tokens - held, HD), jnp.bfloat16)
-        values[:, held:, :HD] = jnp.zeros((KVH, tokens - held, HD), jnp.bfloat16)
-    for i in range(count):
-        block = piece_refs[i][...].reshape(piece_tokens, 2 * KVH * HD)
+        values[:, held:, :] = jnp.zeros((KVH, tokens - held, 2 * HD), jnp.bfloat16)
+    for i, number in enumerate(numbers):
+        keep = keep_ref[number * piece_tokens : (number + 1) * piece_tokens, :].astype(jnp.bfloat16)
         span = slice(i * piece_tokens, (i + 1) * piece_tokens)
         for h in range(KVH):
-            keys[h, span, :] = block[:, h * HD : (h + 1) * HD]
-            values[h, span, :HD] = block[:, (KVH + h) * HD : (KVH + h + 1) * HD]
-    bias = bias_ref[...]
+            keys[h, span, :], values[h, span, :HD], values[h, span, HD:] = lay_out(
+                piece_refs[i], h, keep
+            )
+    rows = q_ref.shape[0]
+    for begin in range(0, QH, TOGETHER):
+        h = begin // GROUP
+        heads = range(begin, begin + TOGETHER)
+        q = jnp.concatenate([q_ref[:, n * HD : (n + 1) * HD] for n in heads], 0)
+        scores = lax.dot_general(
+            q, keys[h], (((1,), (1,)), ((), ())), preferred_element_type=jnp.float32
+        )
+        weights = jnp.exp2(scores * EXP2_SCALE).astype(jnp.bfloat16)
+        sums = jnp.dot(weights, values[h], preferred_element_type=jnp.float32)
+        for i, n in enumerate(heads):
+            part = sums[i * rows : (i + 1) * rows]
+            if old_sums is not None:
+                part = part + old_sums[:, n * 2 * HD : (n + 1) * 2 * HD]
+            give(n, part)
+
+
+def stage_kernel(*refs, numbers, first):
+    q_ref, keep_ref = refs[:2]
+    piece_refs = refs[2 : 2 + len(numbers)]
+    rest = list(refs[2 + len(numbers) :])
+    old_sums = None if first else rest.pop(0)
+    out_ref, keys, values = rest
+
+    def give(n, part):
+        out_ref[:, n * 2 * HD : (n + 1) * 2 * HD] = part
+
+    stage_sums(q_ref, keep_ref, piece_refs, numbers, keys, values, old_sums, give)
+
+
+def last_kernel(*refs, numbers):
+    q_ref, keep_ref, live_ref, bias_ref = refs[:4]
+    piece_refs = refs[4 : 4 + GATHER_DEVICES]
+    old_sums, out_ref, keys, values, out_vmem, all_keys, all_values, sems = refs[4 + GATHER_DEVICES :]
+    rows = q_ref.shape[0]
     live = live_ref[...] > 0.0
-    for q_head in range(QH):
-        h = q_head // GROUP
-        lanes = slice(q_head * HD, (q_head + 1) * HD)
-        wide = slice(q_head * 2 * HD, (q_head + 1) * 2 * HD)
-        scores = lax.dot_general(
-            q_ref[:, lanes], keys[h], (((1,), (1,)), ((), ())), preferred_element_type=jnp.float32
+    chunk = GROUP * HD
+    copies = [
+        pltpu.make_async_copy(
+            out_vmem.at[:, h * chunk : (h + 1) * chunk],
+            out_ref.at[:, h * chunk : (h + 1) * chunk],
+            sems.at[h],
         )
-        scores = scores + bias
-        row_max = jnp.broadcast_to(jnp.max(scores, -1, keepdims=True), (rows, HD))
-        if not first:
-            before = old_max[:, lanes]
-            row_max = jnp.maximum(row_max, before)
-        weights = jnp.concatenate(
-            [
-                jnp.exp2((scores[:, t : t + HD] - row_max) * EXP2_SCALE).astype(jnp.bfloat16)
-                for t in range(0, tokens, HD)
-            ],
-            1,
-        )
-        sums = jnp.dot(weights, values[h], preferred_element_type=jnp.float32)
-        mixed, totals = sums[:, :HD], sums[:, HD:]
-        if not first:
-            factor = jnp.exp2((before - row_max) * EXP2_SCALE)
-            old = old_sums[:, wide]
-            mixed, totals = mixed + old[:, :HD] * factor, totals + old[:, HD:] * factor
-        if last:
-            out_ref[:, lanes] = jnp.where(live, mixed / totals, 0.0).astype(jnp.bfloat16)
-        else:
-            out_ref[:, wide] = jnp.concatenate([mixed, totals], 1)
-            out_max[:, lanes] = row_max
-
-
-def attend_pieces(queries, bias, live, pieces, state, last):
+        for h in range(KVH)
+    ]
+    added = [jnp.zeros((rows, HD), jnp.float32), jnp.full((rows, HD), 1.0, jnp.float32)]
+
+    def give(n, part):
+        mixed, totals = part[:, :HD], part[:, HD:]
+        added[0] = added[0] + totals
+        added[1] = jnp.minimum(added[1], totals)
+        inverse = pl.reciprocal(totals, approx=True)
+        inverse = inverse * (2.0 - totals * inverse)
+        lanes = slice(n * HD, (n + 1) * HD)
+        out_vmem[:, lanes] = jnp.where(live, mixed * inverse, 0.0).astype(jnp.bfloat16)
+        if n % GROUP == GROUP - 1:
+            copies[n // GROUP].start()
+
+    new_refs = [piece_refs[number] for number in numbers]
+    stage_sums(q_ref, keep_ref, new_refs, numbers, keys, values, old_sums, give)
+    fits = (added[0] <= 2.0**100) & (added[1] >= 2.0**-100)
+    fits = jnp.min(jnp.where(fits, 1.0, 0.0).reshape(rows // 8, 8, HD), 0)
+    fits = jnp.min(fits)
+    for copy in copies:
+        copy.wait()
+
+    @pl.when(fits < 0.5)
+    def with_row_maxima():
+        bias = bias_ref[...]
+        piece_tokens = piece_refs[0].shape[0] * piece_refs[0].shape[1]
+        for h in range(KVH):
+            for number in range(GATHER_DEVICES):
+                span = slice(number * piece_tokens, (number + 1) * piece_tokens)
+                keep = keep_ref[span, :].astype(jnp.bfloat16)
+                all_keys[span, :], all_values[span, :HD], all_values[span, HD:] = lay_out(
+                    piece_refs[number], h, keep
+                )
+
+            def one_head(g, unused):
+                lanes = pl.ds(pl.multiple_of((h * GROUP + g) * HD, HD), HD)
+                scores = lax.dot_general(
+                    q_ref[:, lanes],
+                    all_keys[...],
+                    (((1,), (1,)), ((), ())),
+                    preferred_element_type=jnp.float32,
+                )
+                scores = scores + bias
+                row_max = jnp.max(scores, -1, keepdims=True)
+                weights = jnp.exp2((scores - row_max) * EXP2_SCALE).astype(jnp.bfloat16)
+                sums = jnp.dot(weights, all_values[...], preferred_element_type=jnp.float32)
+                mixed = jnp.where(live, sums[:, :HD] / sums[:, HD:], 0.0)
+                out_vmem[:, lanes] = mixed.astype(jnp.bfloat16)
+                return unused
+
+            lax.fori_loop(0, GROUP, one_head, 0)
+        for copy in copies:
+            copy.start()
+        for copy in copies:
+            copy.wait()
+
+
+def attend_pieces(queries, keep, live, bias, pieces, numbers, state, last):
     rows, features = queries.shape
-    count = len(pieces)
-    tokens = bias.shape[1]
+    piece_tokens = pieces[numbers[0]].shape[0] * pieces[numbers[0]].shape[1]
+    held = len(numbers) * piece_tokens
+    tokens = held + -held % HD
     vmem = pl.BlockSpec(memory_space=pltpu.VMEM)
-    state_shape = (
-        jax.ShapeDtypeStruct((rows, 2 * features), jnp.float32),
-        jax.ShapeDtypeStruct((rows, features), jnp.float32),
-    )
+    scratch = [
+        pltpu.VMEM((KVH, tokens, HD), jnp.bfloat16),
+        pltpu.VMEM((KVH, tokens, 2 * HD), jnp.bfloat16),
+    ]
+    if last:
+        everything = GATHER_DEVICES * piece_tokens
+        scratch += [
+            pltpu.VMEM((rows, features), jnp.bfloat16),
+            pltpu.VMEM((everything, HD), jnp.bfloat16),
+            pltpu.VMEM((everything, 2 * HD), jnp.bfloat16),
+            pltpu.SemaphoreType.DMA((KVH,)),
+        ]
+        kernel = functools.partial(last_kernel, numbers=numbers)
+        operands = [queries, keep, live, bias] + [pieces[n] for n in range(GATHER_DEVICES)]
+        out_shape = jax.ShapeDtypeStruct((rows, features), jnp.bfloat16)
+    else:
+        kernel = functools.partial(stage_kernel, numbers=numbers, first=not state)
+        operands = [queries, keep] + [pieces[n] for n in numbers]
+        out_shape = jax.ShapeDtypeStruct((rows, 2 * features), jnp.float32)
+    operands += state
     return pl.pallas_call(
-        functools.partial(attention_kernel, count=count, first=not state, last=last),
-        out_shape=jax.ShapeDtypeStruct((rows, features), jnp.bfloat16) if last else state_shape,
-        in_specs=[vmem] * (3 + count + len(state)),
-        out_specs=vmem if last else (vmem, vmem),
-        scratch_shapes=[
-            pltpu.VMEM((KVH, tokens, HD), jnp.bfloat16),
-            pltpu.VMEM((KVH, tokens, 2 * HD), jnp.bfloat16),
-        ],
-        compiler_params=pltpu.CompilerParams(vmem_limit_bytes=32 << 20),
+        kernel,
+        out_shape=out_shape,
+        in_specs=[vmem] * len(operands),
+        out_specs=pl.BlockSpec(memory_space=pltpu.HBM) if last else vmem,
+        scratch_shapes=scratch,
+        compiler_params=pltpu.CompilerParams(vmem_limit_bytes=24 << 20),
         cost_estimate=pl.CostEstimate(
             flops=4 * rows * features * tokens,
             bytes_accessed=4 * rows * features + 2 * tokens * KVH * HD * 2,
             transcendentals=rows * QH * tokens,
         ),
         name="attention_last" if last else "attention_stage",
-    )(queries, bias, live, *pieces, *state)
+    )(*operands)
 
 
 def attend_staged(queries, kv_pool, span_lengths, owner_branch, branch_table):
-    stages = [step[1] for step in PLAN if step[0] == "attend"]
     held = {0: kv_pool}
     marks = {}
-    state, stage, biases = (), 0, None
+    state, stage, stages = [], 0, sum(step[0] == "attend" for step in PLAN)
     for step in PLAN:
         earlier = [marks[name] for name in step[-1]]
         if step[0] == "prepare":
-            queries, own, live, *biases = prepare(
-                after(queries, *earlier), kv_pool, span_lengths, owner_branch, branch_table, stages
+            queries, own, live, keep, bias = prepare(
+                after(queries, *earlier), kv_pool, span_lengths, owner_branch, branch_table
             )
             marks["prepare"] = live
         elif step[0] == "attend":
-            pieces = [own if number == 0 else held[number] for number in step[1]]
-            bias = after(biases[stage], *earlier)
             stage += 1
-            state = attend_pieces(queries, bias, live, pieces, state, stage == len(stages))
-            if stage < len(stages):
-                marks["attend%d" % stage] = state[1]
+            pieces = held | {0: own}
+            state = [
+                attend_pieces(
+                    queries, after(keep, *earlier), live, bias, pieces, step[1], state, stage == stages
+                )
+            ]
+            if stage < stages:
+                marks["attend%d" % stage] = state[0]
         else:
             number = step[1] ^ MOVES[step[0]]
             held[number] = permute(after(held[step[1]], *earlier), step[0])
             marks[number] = held[number]
-    return state
+    return state[0]
 
 
 def attend_anywhere(queries, kv_pool, span_lengths, owner_branch, prefix_table, branch_table):

time: 32.2 us -> 53.1 us (1.65)
  Pallas kernels: 11.9 us -> 32.5 us
  waiting for transfers between devices: 6.17 us -> 6.89 us
    pallas_call x3, Pallas kernels: 11.9 us -> 32.5 us  [the longest x2 31.3 us: attend_pieces(): pl.pallas_call(kernel, out_shape=out_shape, in_specs=[vmem] * len(operand...]
    ppermute x15, waiting for transfers between devices: 6.17 us -> 6.89 us  [permute(): return lax.ppermute(block, 'seq', pairs)]
  transfers between devices with their start and end apart: 15 -> 15, of which waited for: 5 -> 5; matrix products, arithmetic and copies ran while one was open for 0% -> 0% of each run, Pallas kernels for 18% -> 9%
where the time goes in v3:
time: 53.1 us; the launch traced here: 53 us
  Pallas kernels  32.5 us (61%)
  starting transfers between devices  13.5 us (25%)
  waiting for transfers between devices  6.89 us (13%)
    pallas_call x2, Pallas kernels, attend_pieces(): pl.pallas_call(kernel, out_shape=out_shape, in_specs=[vmem] * len(operand...  31.3 us
    ppermute x15, starting transfers between devices, permute(): return lax.ppermute(block, 'seq', pairs)  13.5 us
    ppermute x15, waiting for transfers between devices, permute(): return lax.ppermute(block, 'seq', pairs)  6.89 us
    pallas_call x1, Pallas kernels, prepare(): pl.pallas_call(prepare_kernel, out_shape=shapes, in_specs=[pl.BlockSpec(m...  1.27 us
  transfers between devices with their start and end apart: 15, of which 5 were waited for; matrix products, arithmetic and copies ran while one was open for 0% of the time, Pallas kernels for 9%

profile of v3, /device:TPU:0, one launch (start us, length us, event | category | flops | bytes accessed | tf_op | source)
XLA Modules:
  0.0 53.0 jit_solution(5569652418130095279)
XLA Ops:
  0.0 3.0 %collective-permute-start.3 = (bf16[9,8,1024]{2,1,0:T(8,128)(2,1)}, bf16[9,8,1024]{2,1,0:T(8,128)(2,1)S(1)}, u32[]{:S(2)}, u32[]{:S(2)}) collective-permute-start(bf16[9,8,1024]{2,1,0:T(8,128)(2,1)} %shard_ref.1), channel_id=1, source_target_pairs={{0,4},{1,5},{2,6},{3,7},{4,0},{5,1},{6,2},{7,3},{8,12},{9,13},{10,... | collective-permute-start | bytes 442376 | tf_op jit(solution)/shard_map/ppermute | solution.py:105
  3.0 2.6 %collective-permute-start.7 = (bf16[9,8,1024]{2,1,0:T(8,128)(2,1)}, bf16[9,8,1024]{2,1,0:T(8,128)(2,1)S(1)}, u32[]{:S(2)}, u32[]{:S(2)}) collective-permute-start(bf16[9,8,1024]{2,1,0:T(8,128)(2,1)} %shard_ref.1), channel_id=1, source_target_pairs={{0,8},{1,9},{2,10},{3,11},{4,12},{5,13},{6,14},{7,15},{8,0},{9,1},... | collective-permute-start | bytes 442376 | tf_op jit(solution)/shard_map/ppermute | solution.py:105
  5.6 1.5 %collective-permute-start.1 = (bf16[9,8,1024]{2,1,0:T(8,128)(2,1)}, bf16[9,8,1024]{2,1,0:T(8,128)(2,1)S(1)}, u32[]{:S(2)}, u32[]{:S(2)}) collective-permute-start(bf16[9,8,1024]{2,1,0:T(8,128)(2,1)} %shard_ref.1), channel_id=1, source_target_pairs={{0,2},{1,3},{2,0},{3,1},{4,6},{5,7},{6,4},{7,5},{8,10},{9,11},{10,... | collective-permute-start | bytes 442376 | tf_op jit(solution)/shard_map/ppermute | solution.py:105
  7.1 0.0 collective-permute-start
  7.1 1.3 %prepare.1 = (bf16[128,4096]{1,0:T(8,128)(2,1)S(1)}, bf16[9,8,1024]{2,1,0:T(8,128)(2,1)S(1)}, f32[128,128]{1,0:T(8,128)S(1)}, f32[1152,128]{1,0:T(8,128)S(1)}, f32[1,1152]{1,0:T(1,128)S(1)}) custom-call(bf16[128,4096]{1,0:T(8,128)(2,1)} %q_ref.1, bf16[9,8,1024]{2,1,0:T(8,128)(2,1)} %shard_ref.1, s32[16]{0:T(128)} %lengths_in.1, s32[16]{0:T(128)} %owner_in.1, ...), custom_call_target="tpu_custom_call" | custom-call | tf_op jit(solution)/shard_map/prepare/pallas_call | solution.py:171
  8.4 1.2 %collective-permute-done.3.refs_6_.refs_8_ = bf16[9,8,1024]{2,1,0:T(8,128)(2,1)S(1)} collective-permute-done((bf16[9,8,1024]{2,1,0:T(8,128)(2,1)}, bf16[9,8,1024]{2,1,0:T(8,128)(2,1)S(1)}, u32[]{:S(2)}, u32[]{:S(2)}) %collective-permute-start.3) | collective-permute-done | bytes 147488 | tf_op jit(solution)/shard_map/ppermute | solution.py:105
  9.6 1.8 %collective-permute-start.5 = (bf16[9,8,1024]{2,1,0:T(8,128)(2,1)S(1)}, bf16[9,8,1024]{2,1,0:T(8,128)(2,1)S(1)}, u32[]{:S(2)}, u32[]{:S(2)}) collective-permute-start(bf16[9,8,1024]{2,1,0:T(8,128)(2,1)S(1)} %collective-permute-done.3.refs_6_.refs_8_), channel_id=1, source_target_pairs={{0,2},{1,3},{2,0},{3,1},{4,6},{5,7},{6,4},{7,5},{8,10},{9,11},{10,... | collective-permute-start | bytes 442376 | tf_op jit(solution)/shard_map/ppermute | solution.py:105
  11.4 1.2 %collective-permute-done.7.refs_12_ = bf16[9,8,1024]{2,1,0:T(8,128)(2,1)S(1)} collective-permute-done((bf16[9,8,1024]{2,1,0:T(8,128)(2,1)}, bf16[9,8,1024]{2,1,0:T(8,128)(2,1)S(1)}, u32[]{:S(2)}, u32[]{:S(2)}) %collective-permute-start.7) | collective-permute-done | bytes 147488 | tf_op jit(solution)/shard_map/ppermute | solution.py:105
  12.7 0.4 collective-permute-start.11
  13.1 0.0 collective-permute-done.1.refs_4_.refs_6_
  13.1 0.0 collective-permute-start.2
  13.1 1.5 %collective-permute-start.9 = (bf16[9,8,1024]{2,1,0:T(8,128)(2,1)S(1)}, bf16[9,8,1024]{2,1,0:T(8,128)(2,1)S(1)}, u32[]{:S(2)}, u32[]{:S(2)}) collective-permute-start(bf16[9,8,1024]{2,1,0:T(8,128)(2,1)S(1)} %collective-permute-done.7.refs_12_), channel_id=1, source_target_pairs={{0,2},{1,3},{2,0},{3,1},{4,6},{5,7},{6,4},{7,5},{8,10},{9,11},{10,... | collective-permute-start | bytes 442376 | tf_op jit(solution)/shard_map/ppermute | solution.py:105
  14.6 0.0 collective-permute-done.refs_3_.refs_5_
  14.6 0.2 collective-permute-start.4
  14.8 0.0 collective-permute-done.5.refs_8_.refs_10_
  14.8 0.3 collective-permute-start.6
  15.1 2.7 %collective-permute-done.11.refs_16_ = bf16[9,8,1024]{2,1,0:T(8,128)(2,1)S(1)} collective-permute-done((bf16[9,8,1024]{2,1,0:T(8,128)(2,1)S(1)}, bf16[9,8,1024]{2,1,0:T(8,128)(2,1)S(1)}, u32[]{:S(2)}, u32[]{:S(2)}) %collective-permute-start.11) | collective-permute-done | bytes 147488 | tf_op jit(solution)/shard_map/ppermute | solution.py:105
  17.8 1.5 %collective-permute-start.13 = (bf16[9,8,1024]{2,1,0:T(8,128)(2,1)S(1)}, bf16[9,8,1024]{2,1,0:T(8,128)(2,1)S(1)}, u32[]{:S(2)}, u32[]{:S(2)}) collective-permute-start(bf16[9,8,1024]{2,1,0:T(8,128)(2,1)S(1)} %collective-permute-done.11.refs_16_), channel_id=1, source_target_pairs={{0,2},{1,3},{2,0},{3,1},{4,6},{5,7},{6,4},{7,5},{8,10},{9,11},{10,... | collective-permute-start | bytes 442376 | tf_op jit(solution)/shard_map/ppermute | solution.py:105
  19.3 0.0 collective-permute-done.2.refs_5_.refs_7_
  19.3 0.0 collective-permute-start.8
  19.3 0.4 collective-permute-done.9.refs_14_
  19.7 0.1 collective-permute-start.12
  19.8 0.0 collective-permute-done.4.refs_7_.refs_9_
  19.8 0.4 collective-permute-start.10
  20.3 0.0 collective-permute-done.6.refs_9_.refs_11_
  20.3 3.4 %attention_stage.1.refs_20_ = f32[128,8192]{1,0:T(8,128)S(1)} custom-call(bf16[128,4096]{1,0:T(8,128)(2,1)S(1)} %get-tuple-element.12.refs_0_, f32[1152,128]{1,0:T(8,128)S(1)} %get-tuple-element.13.refs_1_, bf16[9,8,1024]{2,1,0:T(8,128)(2,1)S(1)} %get-tuple-element.16.refs_2_.refs_4_, bf16[9,8,1024]{2,1,0:T(8,128)(2,1)S(1)} %collective-permute-done.refs_3_.refs_5_, ...), custom_call_target="tpu_custom_call" | custom-call | flops 1342177280 | bytes 3407872 | tf_op jit(solution)/shard_map/attention_stage/pallas_call | solution.py:331
  23.6 0.0 collective-permute-done.13.refs_18_
  23.6 0.1 collective-permute-start.14
  23.8 0.0 collective-permute-done.8.refs_13_
  23.8 0.0 collective-permute-done.12.refs_17_
  23.8 0.0 collective-permute-done.10.refs_15_
  23.8 1.3 %collective-permute-done.14.refs_19_ = bf16[9,8,1024]{2,1,0:T(8,128)(2,1)S(1)} collective-permute-done((bf16[9,8,1024]{2,1,0:T(8,128)(2,1)S(1)}, bf16[9,8,1024]{2,1,0:T(8,128)(2,1)S(1)}, u32[]{:S(2)}, u32[]{:S(2)}) %collective-permute-start.14) | collective-permute-done | bytes 147488 | tf_op jit(solution)/shard_map/ppermute | solution.py:105
  25.1 27.9 %attention_last.1 = bf16[128,4096]{1,0:T(8,128)(2,1)} custom-call(bf16[128,4096]{1,0:T(8,128)(2,1)S(1)} %get-tuple-element.12.refs_0_, f32[1152,128]{1,0:T(8,128)S(1)} %get-tuple-element.13.refs_1_, f32[128,128]{1,0:T(8,128)S(1)} %get-tuple-element.14.refs_2_, f32[1,1152]{1,0:T(1,128)S(1)} %get-tuple-element.15.refs_3_, ...), custom_call_target="tpu_custom_call" | custom-call | flops 1342177280 | bytes 3407872 | tf_op jit(solution)/shard_map/attention_last/pallas_call | solution.py:331
Async XLA Ops:
  0.0 9.6 %collective-permute-start.3 = (bf16[9,8,1024]{2,1,0:T(8,128)(2,1)}, bf16[9,8,1024]{2,1,0:T(8,128)(2,1)S(1)}, u32[]{:S(2)}, u32[]{:S(2)}) collective-permute-start(bf16[9,8,1024]{2,1,0:T(8,128)(2,1)} %shard_ref.1), channel_id=1, source_target_pairs={{0,4},{1,5},{2,6},{3,7},{4,0},{5,1},{6,2},{7,3},{8,12},{9,13},{10,... | collective-permute-start | bytes 442376 | tf_op jit(solution)/shard_map/ppermute | solution.py:105
  3.0 9.6 %collective-permute-start.7 = (bf16[9,8,1024]{2,1,0:T(8,128)(2,1)}, bf16[9,8,1024]{2,1,0:T(8,128)(2,1)S(1)}, u32[]{:S(2)}, u32[]{:S(2)}) collective-permute-start(bf16[9,8,1024]{2,1,0:T(8,128)(2,1)} %shard_ref.1), channel_id=1, source_target_pairs={{0,8},{1,9},{2,10},{3,11},{4,12},{5,13},{6,14},{7,15},{8,0},{9,1},... | collective-permute-start | bytes 442376 | tf_op jit(solution)/shard_map/ppermute | solution.py:105
  5.6 7.5 %collective-permute-start.1 = (bf16[9,8,1024]{2,1,0:T(8,128)(2,1)}, bf16[9,8,1024]{2,1,0:T(8,128)(2,1)S(1)}, u32[]{:S(2)}, u32[]{:S(2)}) collective-permute-start(bf16[9,8,1024]{2,1,0:T(8,128)(2,1)} %shard_ref.1), channel_id=1, source_target_pairs={{0,2},{1,3},{2,0},{3,1},{4,6},{5,7},{6,4},{7,5},{8,10},{9,11},{10,... | collective-permute-start | bytes 442376 | tf_op jit(solution)/shard_map/ppermute | solution.py:105
  7.1 7.5 %collective-permute-start = (bf16[9,8,1024]{2,1,0:T(8,128)(2,1)}, bf16[9,8,1024]{2,1,0:T(8,128)(2,1)S(1)}, u32[]{:S(2)}, u32[]{:S(2)}) collective-permute-start(bf16[9,8,1024]{2,1,0:T(8,128)(2,1)} %shard_ref.1), channel_id=1, source_target_pairs={{0,1},{1,0},{2,3},{3,2},{4,5},{5,4},{6,7},{7,6},{8,9},{9,8},{10,11... | collective-permute-start | bytes 442376 | tf_op jit(solution)/shard_map/ppermute | solution.py:105
  9.6 5.2 %collective-permute-start.5 = (bf16[9,8,1024]{2,1,0:T(8,128)(2,1)S(1)}, bf16[9,8,1024]{2,1,0:T(8,128)(2,1)S(1)}, u32[]{:S(2)}, u32[]{:S(2)}) collective-permute-start(bf16[9,8,1024]{2,1,0:T(8,128)(2,1)S(1)} %collective-permute-done.3.refs_6_.refs_8_), channel_id=1, source_target_pairs={{0,2},{1,3},{2,0},{3,1},{4,6},{5,7},{6,4},{7,5},{8,10},{9,11},{10,... | collective-permute-start | bytes 442376 | tf_op jit(solution)/shard_map/ppermute | solution.py:105
  12.7 5.1 %collective-permute-start.11 = (bf16[9,8,1024]{2,1,0:T(8,128)(2,1)S(1)}, bf16[9,8,1024]{2,1,0:T(8,128)(2,1)S(1)}, u32[]{:S(2)}, u32[]{:S(2)}) collective-permute-start(bf16[9,8,1024]{2,1,0:T(8,128)(2,1)S(1)} %collective-permute-done.7.refs_12_), channel_id=1, source_target_pairs={{0,4},{1,5},{2,6},{3,7},{4,0},{5,1},{6,2},{7,3},{8,12},{9,13},{10,... | collective-permute-start | bytes 442376 | tf_op jit(solution)/shard_map/ppermute | solution.py:105
  13.1 6.2 %collective-permute-start.2 = (bf16[9,8,1024]{2,1,0:T(8,128)(2,1)S(1)}, bf16[9,8,1024]{2,1,0:T(8,128)(2,1)S(1)}, u32[]{:S(2)}, u32[]{:S(2)}) collective-permute-start(bf16[9,8,1024]{2,1,0:T(8,128)(2,1)S(1)} %collective-permute-done.1.refs_4_.refs_6_), channel_id=1, source_target_pairs={{0,1},{1,0},{2,3},{3,2},{4,5},{5,4},{6,7},{7,6},{8,9},{9,8},{10,11... | collective-permute-start | bytes 442376 | tf_op jit(solution)/shard_map/ppermute | solution.py:105
  13.1 6.6 %collective-permute-start.9 = (bf16[9,8,1024]{2,1,0:T(8,128)(2,1)S(1)}, bf16[9,8,1024]{2,1,0:T(8,128)(2,1)S(1)}, u32[]{:S(2)}, u32[]{:S(2)}) collective-permute-start(bf16[9,8,1024]{2,1,0:T(8,128)(2,1)S(1)} %collective-permute-done.7.refs_12_), channel_id=1, source_target_pairs={{0,2},{1,3},{2,0},{3,1},{4,6},{5,7},{6,4},{7,5},{8,10},{9,11},{10,... | collective-permute-start | bytes 442376 | tf_op jit(solution)/shard_map/ppermute | solution.py:105
  14.6 5.2 %collective-permute-start.4 = (bf16[9,8,1024]{2,1,0:T(8,128)(2,1)S(1)}, bf16[9,8,1024]{2,1,0:T(8,128)(2,1)S(1)}, u32[]{:S(2)}, u32[]{:S(2)}) collective-permute-start(bf16[9,8,1024]{2,1,0:T(8,128)(2,1)S(1)} %collective-permute-done.3.refs_6_.refs_8_), channel_id=1, source_target_pairs={{0,1},{1,0},{2,3},{3,2},{4,5},{5,4},{6,7},{7,6},{8,9},{9,8},{10,11... | collective-permute-start | bytes 442376 | tf_op jit(solution)/shard_map/ppermute | solution.py:105
  14.8 5.4 %collective-permute-start.6 = (bf16[9,8,1024]{2,1,0:T(8,128)(2,1)S(1)}, bf16[9,8,1024]{2,1,0:T(8,128)(2,1)S(1)}, u32[]{:S(2)}, u32[]{:S(2)}) collective-permute-start(bf16[9,8,1024]{2,1,0:T(8,128)(2,1)S(1)} %collective-permute-done.5.refs_8_.refs_10_), channel_id=1, source_target_pairs={{0,1},{1,0},{2,3},{3,2},{4,5},{5,4},{6,7},{7,6},{8,9},{9,8},{10,11... | collective-permute-start | bytes 442376 | tf_op jit(solution)/shard_map/ppermute | solution.py:105
  17.8 5.8 %collective-permute-start.13 = (bf16[9,8,1024]{2,1,0:T(8,128)(2,1)S(1)}, bf16[9,8,1024]{2,1,0:T(8,128)(2,1)S(1)}, u32[]{:S(2)}, u32[]{:S(2)}) collective-permute-start(bf16[9,8,1024]{2,1,0:T(8,128)(2,1)S(1)} %collective-permute-done.11.refs_16_), channel_id=1, source_target_pairs={{0,2},{1,3},{2,0},{3,1},{4,6},{5,7},{6,4},{7,5},{8,10},{9,11},{10,... | collective-permute-start | bytes 442376 | tf_op jit(solution)/shard_map/ppermute | solution.py:105
  19.3 4.5 %collective-permute-start.8 = (bf16[9,8,1024]{2,1,0:T(8,128)(2,1)S(1)}, bf16[9,8,1024]{2,1,0:T(8,128)(2,1)S(1)}, u32[]{:S(2)}, u32[]{:S(2)}) collective-permute-start(bf16[9,8,1024]{2,1,0:T(8,128)(2,1)S(1)} %collective-permute-done.7.refs_12_), channel_id=1, source_target_pairs={{0,1},{1,0},{2,3},{3,2},{4,5},{5,4},{6,7},{7,6},{8,9},{9,8},{10,11... | collective-permute-start | bytes 442376 | tf_op jit(solution)/shard_map/ppermute | solution.py:105
  19.7 4.0 %collective-permute-start.12 = (bf16[9,8,1024]{2,1,0:T(8,128)(2,1)S(1)}, bf16[9,8,1024]{2,1,0:T(8,128)(2,1)S(1)}, u32[]{:S(2)}, u32[]{:S(2)}) collective-permute-start(bf16[9,8,1024]{2,1,0:T(8,128)(2,1)S(1)} %collective-permute-done.11.refs_16_), channel_id=1, source_target_pairs={{0,1},{1,0},{2,3},{3,2},{4,5},{5,4},{6,7},{7,6},{8,9},{9,8},{10,11... | collective-permute-start | bytes 442376 | tf_op jit(solution)/shard_map/ppermute | solution.py:105
  19.8 4.0 %collective-permute-start.10 = (bf16[9,8,1024]{2,1,0:T(8,128)(2,1)S(1)}, bf16[9,8,1024]{2,1,0:T(8,128)(2,1)S(1)}, u32[]{:S(2)}, u32[]{:S(2)}) collective-permute-start(bf16[9,8,1024]{2,1,0:T(8,128)(2,1)S(1)} %collective-permute-done.9.refs_14_), channel_id=1, source_target_pairs={{0,1},{1,0},{2,3},{3,2},{4,5},{5,4},{6,7},{7,6},{8,9},{9,8},{10,11... | collective-permute-start | bytes 442376 | tf_op jit(solution)/shard_map/ppermute | solution.py:105
  23.6 1.4 %collective-permute-start.14 = (bf16[9,8,1024]{2,1,0:T(8,128)(2,1)S(1)}, bf16[9,8,1024]{2,1,0:T(8,128)(2,1)S(1)}, u32[]{:S(2)}, u32[]{:S(2)}) collective-permute-start(bf16[9,8,1024]{2,1,0:T(8,128)(2,1)S(1)} %collective-permute-done.13.refs_18_), channel_id=1, source_target_pairs={{0,1},{1,0},{2,3},{3,2},{4,5},{5,4},{6,7},{7,6},{8,9},{9,8},{10,11... | collective-permute-start | bytes 442376 | tf_op jit(solution)/shard_map/ppermute | solution.py:105

commit v4 on v3

--- a/solution.py
+++ b/solution.py
@@ -14,7 +14,7 @@
 GROUP = QH // KVH
 EXP2_SCALE = math.log2(math.e) / math.sqrt(HD)
 GATHER_DEVICES = 16
-TOGETHER = 4
+TOGETHER = 2
 MASKED = -1e30
 
 
@@ -94,9 +94,9 @@
     ("core", 8, ()),
     ("core", 10, ()),
     ("core", 12, ()),
-    ("attend", (0, 1, 2, 3, 4, 5, 6, 7), ()),
+    ("attend", (0, 1, 2, 3, 4, 5, 6, 7, 8), ()),
     ("core", 14, ("attend1",)),
-    ("attend", (8, 9, 10, 11, 12, 13, 14, 15), ()),
+    ("attend", (9, 10, 11, 12, 13, 14, 15), ()),
 )
 
 
@@ -335,11 +335,7 @@
         out_specs=pl.BlockSpec(memory_space=pltpu.HBM) if last else vmem,
         scratch_shapes=scratch,
         compiler_params=pltpu.CompilerParams(vmem_limit_bytes=24 << 20),
-        cost_estimate=pl.CostEstimate(
-            flops=4 * rows * features * tokens,
-            bytes_accessed=4 * rows * features + 2 * tokens * KVH * HD * 2,
-            transcendentals=rows * QH * tokens,
-        ),
+        cost_estimate=pl.CostEstimate(flops=0, bytes_accessed=0, transcendentals=0),
         name="attention_last" if last else "attention_stage",
     )(*operands)
 

time: 53.1 us -> 52.2 us (0.983)
  Pallas kernels: 32.5 us -> 31.6 us
    pallas_call x2, Pallas kernels: 31.3 us -> 30.4 us  [attend_pieces(): pl.pallas_call(kernel, out_shape=out_shape, in_specs=[vmem] * len(operand...]
where the time goes in v4:
time: 52.2 us; the launch traced here: 52.1 us
  Pallas kernels  31.6 us (61%)
  starting transfers between devices  13.5 us (26%)
  waiting for transfers between devices  6.9 us (13%)
    pallas_call x2, Pallas kernels, attend_pieces(): pl.pallas_call(kernel, out_shape=out_shape, in_specs=[vmem] * len(operand...  30.4 us
    ppermute x15, starting transfers between devices, permute(): return lax.ppermute(block, 'seq', pairs)  13.5 us
    ppermute x15, waiting for transfers between devices, permute(): return lax.ppermute(block, 'seq', pairs)  6.9 us
    pallas_call x1, Pallas kernels, prepare(): pl.pallas_call(prepare_kernel, out_shape=shapes, in_specs=[pl.BlockSpec(m...  1.27 us
  transfers between devices with their start and end apart: 15, of which 5 were waited for; matrix products, arithmetic and copies ran while one was open for 0% of the time, Pallas kernels for 9%

profile of v4, /device:TPU:0, one launch (start us, length us, event | category | flops | bytes accessed | tf_op | source)
XLA Modules:
  0.0 52.1 jit_solution(10541202506786863314)
XLA Ops:
  0.0 3.0 %collective-permute-start.3 = (bf16[9,8,1024]{2,1,0:T(8,128)(2,1)}, bf16[9,8,1024]{2,1,0:T(8,128)(2,1)S(1)}, u32[]{:S(2)}, u32[]{:S(2)}) collective-permute-start(bf16[9,8,1024]{2,1,0:T(8,128)(2,1)} %shard_ref.1), channel_id=1, source_target_pairs={{0,4},{1,5},{2,6},{3,7},{4,0},{5,1},{6,2},{7,3},{8,12},{9,13},{10,... | collective-permute-start | bytes 442376 | tf_op jit(solution)/shard_map/ppermute | solution.py:105
  3.0 2.6 %collective-permute-start.7 = (bf16[9,8,1024]{2,1,0:T(8,128)(2,1)}, bf16[9,8,1024]{2,1,0:T(8,128)(2,1)S(1)}, u32[]{:S(2)}, u32[]{:S(2)}) collective-permute-start(bf16[9,8,1024]{2,1,0:T(8,128)(2,1)} %shard_ref.1), channel_id=1, source_target_pairs={{0,8},{1,9},{2,10},{3,11},{4,12},{5,13},{6,14},{7,15},{8,0},{9,1},... | collective-permute-start | bytes 442376 | tf_op jit(solution)/shard_map/ppermute | solution.py:105
  5.6 1.5 %collective-permute-start.1 = (bf16[9,8,1024]{2,1,0:T(8,128)(2,1)}, bf16[9,8,1024]{2,1,0:T(8,128)(2,1)S(1)}, u32[]{:S(2)}, u32[]{:S(2)}) collective-permute-start(bf16[9,8,1024]{2,1,0:T(8,128)(2,1)} %shard_ref.1), channel_id=1, source_target_pairs={{0,2},{1,3},{2,0},{3,1},{4,6},{5,7},{6,4},{7,5},{8,10},{9,11},{10,... | collective-permute-start | bytes 442376 | tf_op jit(solution)/shard_map/ppermute | solution.py:105
  7.1 0.0 collective-permute-start
  7.1 1.3 %prepare.1 = (bf16[128,4096]{1,0:T(8,128)(2,1)S(1)}, bf16[9,8,1024]{2,1,0:T(8,128)(2,1)S(1)}, f32[128,128]{1,0:T(8,128)S(1)}, f32[1152,128]{1,0:T(8,128)S(1)}, f32[1,1152]{1,0:T(1,128)S(1)}) custom-call(bf16[128,4096]{1,0:T(8,128)(2,1)} %q_ref.1, bf16[9,8,1024]{2,1,0:T(8,128)(2,1)} %shard_ref.1, s32[16]{0:T(128)} %lengths_in.1, s32[16]{0:T(128)} %owner_in.1, ...), custom_call_target="tpu_custom_call" | custom-call | tf_op jit(solution)/shard_map/prepare/pallas_call | solution.py:171
  8.4 1.2 %collective-permute-done.3.refs_6_.refs_8_ = bf16[9,8,1024]{2,1,0:T(8,128)(2,1)S(1)} collective-permute-done((bf16[9,8,1024]{2,1,0:T(8,128)(2,1)}, bf16[9,8,1024]{2,1,0:T(8,128)(2,1)S(1)}, u32[]{:S(2)}, u32[]{:S(2)}) %collective-permute-start.3) | collective-permute-done | bytes 147488 | tf_op jit(solution)/shard_map/ppermute | solution.py:105
  9.6 1.8 %collective-permute-start.5 = (bf16[9,8,1024]{2,1,0:T(8,128)(2,1)S(1)}, bf16[9,8,1024]{2,1,0:T(8,128)(2,1)S(1)}, u32[]{:S(2)}, u32[]{:S(2)}) collective-permute-start(bf16[9,8,1024]{2,1,0:T(8,128)(2,1)S(1)} %collective-permute-done.3.refs_6_.refs_8_), channel_id=1, source_target_pairs={{0,2},{1,3},{2,0},{3,1},{4,6},{5,7},{6,4},{7,5},{8,10},{9,11},{10,... | collective-permute-start | bytes 442376 | tf_op jit(solution)/shard_map/ppermute | solution.py:105
  11.4 1.2 %collective-permute-done.7.refs_10_.refs_12_ = bf16[9,8,1024]{2,1,0:T(8,128)(2,1)S(1)} collective-permute-done((bf16[9,8,1024]{2,1,0:T(8,128)(2,1)}, bf16[9,8,1024]{2,1,0:T(8,128)(2,1)S(1)}, u32[]{:S(2)}, u32[]{:S(2)}) %collective-permute-start.7) | collective-permute-done | bytes 147488 | tf_op jit(solution)/shard_map/ppermute | solution.py:105
  12.7 0.4 collective-permute-start.11
  13.1 0.0 collective-permute-done.1.refs_4_.refs_6_
  13.1 0.0 collective-permute-start.2
  13.1 1.5 %collective-permute-start.9 = (bf16[9,8,1024]{2,1,0:T(8,128)(2,1)S(1)}, bf16[9,8,1024]{2,1,0:T(8,128)(2,1)S(1)}, u32[]{:S(2)}, u32[]{:S(2)}) collective-permute-start(bf16[9,8,1024]{2,1,0:T(8,128)(2,1)S(1)} %collective-permute-done.7.refs_10_.refs_12_), channel_id=1, source_target_pairs={{0,2},{1,3},{2,0},{3,1},{4,6},{5,7},{6,4},{7,5},{8,10},{9,11},{10,... | collective-permute-start | bytes 442376 | tf_op jit(solution)/shard_map/ppermute | solution.py:105
  14.6 0.0 collective-permute-done.refs_3_.refs_5_
  14.6 0.2 collective-permute-start.4
  14.8 0.0 collective-permute-done.5.refs_8_.refs_10_
  14.8 0.3 collective-permute-start.6
  15.1 2.7 %collective-permute-done.11.refs_16_ = bf16[9,8,1024]{2,1,0:T(8,128)(2,1)S(1)} collective-permute-done((bf16[9,8,1024]{2,1,0:T(8,128)(2,1)S(1)}, bf16[9,8,1024]{2,1,0:T(8,128)(2,1)S(1)}, u32[]{:S(2)}, u32[]{:S(2)}) %collective-permute-start.11) | collective-permute-done | bytes 147488 | tf_op jit(solution)/shard_map/ppermute | solution.py:105
  17.8 1.5 %collective-permute-start.13 = (bf16[9,8,1024]{2,1,0:T(8,128)(2,1)S(1)}, bf16[9,8,1024]{2,1,0:T(8,128)(2,1)S(1)}, u32[]{:S(2)}, u32[]{:S(2)}) collective-permute-start(bf16[9,8,1024]{2,1,0:T(8,128)(2,1)S(1)} %collective-permute-done.11.refs_16_), channel_id=1, source_target_pairs={{0,2},{1,3},{2,0},{3,1},{4,6},{5,7},{6,4},{7,5},{8,10},{9,11},{10,... | collective-permute-start | bytes 442376 | tf_op jit(solution)/shard_map/ppermute | solution.py:105
  19.3 0.0 collective-permute-done.2.refs_5_.refs_7_
  19.3 0.0 collective-permute-start.8
  19.3 0.4 collective-permute-done.9.refs_14_
  19.7 0.1 collective-permute-start.12
  19.8 0.0 collective-permute-done.4.refs_7_.refs_9_
  19.8 0.4 collective-permute-start.10
  20.3 0.0 collective-permute-done.6.refs_9_.refs_11_
  20.3 3.6 %attention_stage.1.refs_20_ = f32[128,8192]{1,0:T(8,128)S(1)} custom-call(bf16[128,4096]{1,0:T(8,128)(2,1)S(1)} %get-tuple-element.12.refs_0_, f32[1152,128]{1,0:T(8,128)S(1)} %get-tuple-element.13.refs_1_, bf16[9,8,1024]{2,1,0:T(8,128)(2,1)S(1)} %get-tuple-element.16.refs_2_.refs_4_, bf16[9,8,1024]{2,1,0:T(8,128)(2,1)S(1)} %collective-permute-done.refs_3_.refs_5_, ...), custom_call_target="tpu_custom_call" | custom-call | tf_op jit(solution)/shard_map/attention_stage/pallas_call | solution.py:331
  23.9 0.0 collective-permute-done.13.refs_18_
  23.9 0.1 collective-permute-start.14
  24.0 0.0 collective-permute-done.8.refs_13_
  24.0 0.0 collective-permute-done.12.refs_17_
  24.0 0.0 collective-permute-done.10.refs_15_
  24.0 1.3 %collective-permute-done.14.refs_19_ = bf16[9,8,1024]{2,1,0:T(8,128)(2,1)S(1)} collective-permute-done((bf16[9,8,1024]{2,1,0:T(8,128)(2,1)S(1)}, bf16[9,8,1024]{2,1,0:T(8,128)(2,1)S(1)}, u32[]{:S(2)}, u32[]{:S(2)}) %collective-permute-start.14) | collective-permute-done | bytes 147488 | tf_op jit(solution)/shard_map/ppermute | solution.py:105
  25.3 26.8 %attention_last.1 = bf16[128,4096]{1,0:T(8,128)(2,1)} custom-call(bf16[128,4096]{1,0:T(8,128)(2,1)S(1)} %get-tuple-element.12.refs_0_, f32[1152,128]{1,0:T(8,128)S(1)} %get-tuple-element.13.refs_1_, f32[128,128]{1,0:T(8,128)S(1)} %get-tuple-element.14.refs_2_, f32[1,1152]{1,0:T(1,128)S(1)} %get-tuple-element.15.refs_3_, ...), custom_call_target="tpu_custom_call" | custom-call | tf_op jit(solution)/shard_map/attention_last/pallas_call | solution.py:331
Async XLA Ops:
  0.0 9.6 %collective-permute-start.3 = (bf16[9,8,1024]{2,1,0:T(8,128)(2,1)}, bf16[9,8,1024]{2,1,0:T(8,128)(2,1)S(1)}, u32[]{:S(2)}, u32[]{:S(2)}) collective-permute-start(bf16[9,8,1024]{2,1,0:T(8,128)(2,1)} %shard_ref.1), channel_id=1, source_target_pairs={{0,4},{1,5},{2,6},{3,7},{4,0},{5,1},{6,2},{7,3},{8,12},{9,13},{10,... | collective-permute-start | bytes 442376 | tf_op jit(solution)/shard_map/ppermute | solution.py:105
  3.0 9.6 %collective-permute-start.7 = (bf16[9,8,1024]{2,1,0:T(8,128)(2,1)}, bf16[9,8,1024]{2,1,0:T(8,128)(2,1)S(1)}, u32[]{:S(2)}, u32[]{:S(2)}) collective-permute-start(bf16[9,8,1024]{2,1,0:T(8,128)(2,1)} %shard_ref.1), channel_id=1, source_target_pairs={{0,8},{1,9},{2,10},{3,11},{4,12},{5,13},{6,14},{7,15},{8,0},{9,1},... | collective-permute-start | bytes 442376 | tf_op jit(solution)/shard_map/ppermute | solution.py:105
  5.6 7.5 %collective-permute-start.1 = (bf16[9,8,1024]{2,1,0:T(8,128)(2,1)}, bf16[9,8,1024]{2,1,0:T(8,128)(2,1)S(1)}, u32[]{:S(2)}, u32[]{:S(2)}) collective-permute-start(bf16[9,8,1024]{2,1,0:T(8,128)(2,1)} %shard_ref.1), channel_id=1, source_target_pairs={{0,2},{1,3},{2,0},{3,1},{4,6},{5,7},{6,4},{7,5},{8,10},{9,11},{10,... | collective-permute-start | bytes 442376 | tf_op jit(solution)/shard_map/ppermute | solution.py:105
  7.1 7.5 %collective-permute-start = (bf16[9,8,1024]{2,1,0:T(8,128)(2,1)}, bf16[9,8,1024]{2,1,0:T(8,128)(2,1)S(1)}, u32[]{:S(2)}, u32[]{:S(2)}) collective-permute-start(bf16[9,8,1024]{2,1,0:T(8,128)(2,1)} %shard_ref.1), channel_id=1, source_target_pairs={{0,1},{1,0},{2,3},{3,2},{4,5},{5,4},{6,7},{7,6},{8,9},{9,8},{10,11... | collective-permute-start | bytes 442376 | tf_op jit(solution)/shard_map/ppermute | solution.py:105
  9.6 5.2 %collective-permute-start.5 = (bf16[9,8,1024]{2,1,0:T(8,128)(2,1)S(1)}, bf16[9,8,1024]{2,1,0:T(8,128)(2,1)S(1)}, u32[]{:S(2)}, u32[]{:S(2)}) collective-permute-start(bf16[9,8,1024]{2,1,0:T(8,128)(2,1)S(1)} %collective-permute-done.3.refs_6_.refs_8_), channel_id=1, source_target_pairs={{0,2},{1,3},{2,0},{3,1},{4,6},{5,7},{6,4},{7,5},{8,10},{9,11},{10,... | collective-permute-start | bytes 442376 | tf_op jit(solution)/shard_map/ppermute | solution.py:105
  12.7 5.1 %collective-permute-start.11 = (bf16[9,8,1024]{2,1,0:T(8,128)(2,1)S(1)}, bf16[9,8,1024]{2,1,0:T(8,128)(2,1)S(1)}, u32[]{:S(2)}, u32[]{:S(2)}) collective-permute-start(bf16[9,8,1024]{2,1,0:T(8,128)(2,1)S(1)} %collective-permute-done.7.refs_10_.refs_12_), channel_id=1, source_target_pairs={{0,4},{1,5},{2,6},{3,7},{4,0},{5,1},{6,2},{7,3},{8,12},{9,13},{10,... | collective-permute-start | bytes 442376 | tf_op jit(solution)/shard_map/ppermute | solution.py:105
  13.1 6.2 %collective-permute-start.2 = (bf16[9,8,1024]{2,1,0:T(8,128)(2,1)S(1)}, bf16[9,8,1024]{2,1,0:T(8,128)(2,1)S(1)}, u32[]{:S(2)}, u32[]{:S(2)}) collective-permute-start(bf16[9,8,1024]{2,1,0:T(8,128)(2,1)S(1)} %collective-permute-done.1.refs_4_.refs_6_), channel_id=1, source_target_pairs={{0,1},{1,0},{2,3},{3,2},{4,5},{5,4},{6,7},{7,6},{8,9},{9,8},{10,11... | collective-permute-start | bytes 442376 | tf_op jit(solution)/shard_map/ppermute | solution.py:105
  13.1 6.6 %collective-permute-start.9 = (bf16[9,8,1024]{2,1,0:T(8,128)(2,1)S(1)}, bf16[9,8,1024]{2,1,0:T(8,128)(2,1)S(1)}, u32[]{:S(2)}, u32[]{:S(2)}) collective-permute-start(bf16[9,8,1024]{2,1,0:T(8,128)(2,1)S(1)} %collective-permute-done.7.refs_10_.refs_12_), channel_id=1, source_target_pairs={{0,2},{1,3},{2,0},{3,1},{4,6},{5,7},{6,4},{7,5},{8,10},{9,11},{10,... | collective-permute-start | bytes 442376 | tf_op jit(solution)/shard_map/ppermute | solution.py:105
  14.6 5.2 %collective-permute-start.4 = (bf16[9,8,1024]{2,1,0:T(8,128)(2,1)S(1)}, bf16[9,8,1024]{2,1,0:T(8,128)(2,1)S(1)}, u32[]{:S(2)}, u32[]{:S(2)}) collective-permute-start(bf16[9,8,1024]{2,1,0:T(8,128)(2,1)S(1)} %collective-permute-done.3.refs_6_.refs_8_), channel_id=1, source_target_pairs={{0,1},{1,0},{2,3},{3,2},{4,5},{5,4},{6,7},{7,6},{8,9},{9,8},{10,11... | collective-permute-start | bytes 442376 | tf_op jit(solution)/shard_map/ppermute | solution.py:105
  14.8 5.4 %collective-permute-start.6 = (bf16[9,8,1024]{2,1,0:T(8,128)(2,1)S(1)}, bf16[9,8,1024]{2,1,0:T(8,128)(2,1)S(1)}, u32[]{:S(2)}, u32[]{:S(2)}) collective-permute-start(bf16[9,8,1024]{2,1,0:T(8,128)(2,1)S(1)} %collective-permute-done.5.refs_8_.refs_10_), channel_id=1, source_target_pairs={{0,1},{1,0},{2,3},{3,2},{4,5},{5,4},{6,7},{7,6},{8,9},{9,8},{10,11... | collective-permute-start | bytes 442376 | tf_op jit(solution)/shard_map/ppermute | solution.py:105
  17.8 6.1 %collective-permute-start.13 = (bf16[9,8,1024]{2,1,0:T(8,128)(2,1)S(1)}, bf16[9,8,1024]{2,1,0:T(8,128)(2,1)S(1)}, u32[]{:S(2)}, u32[]{:S(2)}) collective-permute-start(bf16[9,8,1024]{2,1,0:T(8,128)(2,1)S(1)} %collective-permute-done.11.refs_16_), channel_id=1, source_target_pairs={{0,2},{1,3},{2,0},{3,1},{4,6},{5,7},{6,4},{7,5},{8,10},{9,11},{10,... | collective-permute-start | bytes 442376 | tf_op jit(solution)/shard_map/ppermute | solution.py:105
  19.3 4.7 %collective-permute-start.8 = (bf16[9,8,1024]{2,1,0:T(8,128)(2,1)S(1)}, bf16[9,8,1024]{2,1,0:T(8,128)(2,1)S(1)}, u32[]{:S(2)}, u32[]{:S(2)}) collective-permute-start(bf16[9,8,1024]{2,1,0:T(8,128)(2,1)S(1)} %collective-permute-done.7.refs_10_.refs_12_), channel_id=1, source_target_pairs={{0,1},{1,0},{2,3},{3,2},{4,5},{5,4},{6,7},{7,6},{8,9},{9,8},{10,11... | collective-permute-start | bytes 442376 | tf_op jit(solution)/shard_map/ppermute | solution.py:105
  19.7 4.3 %collective-permute-start.12 = (bf16[9,8,1024]{2,1,0:T(8,128)(2,1)S(1)}, bf16[9,8,1024]{2,1,0:T(8,128)(2,1)S(1)}, u32[]{:S(2)}, u32[]{:S(2)}) collective-permute-start(bf16[9,8,1024]{2,1,0:T(8,128)(2,1)S(1)} %collective-permute-done.11.refs_16_), channel_id=1, source_target_pairs={{0,1},{1,0},{2,3},{3,2},{4,5},{5,4},{6,7},{7,6},{8,9},{9,8},{10,11... | collective-permute-start | bytes 442376 | tf_op jit(solution)/shard_map/ppermute | solution.py:105
  19.8 4.2 %collective-permute-start.10 = (bf16[9,8,1024]{2,1,0:T(8,128)(2,1)S(1)}, bf16[9,8,1024]{2,1,0:T(8,128)(2,1)S(1)}, u32[]{:S(2)}, u32[]{:S(2)}) collective-permute-start(bf16[9,8,1024]{2,1,0:T(8,128)(2,1)S(1)} %collective-permute-done.9.refs_14_), channel_id=1, source_target_pairs={{0,1},{1,0},{2,3},{3,2},{4,5},{5,4},{6,7},{7,6},{8,9},{9,8},{10,11... | collective-permute-start | bytes 442376 | tf_op jit(solution)/shard_map/ppermute | solution.py:105
  23.9 1.4 %collective-permute-start.14 = (bf16[9,8,1024]{2,1,0:T(8,128)(2,1)S(1)}, bf16[9,8,1024]{2,1,0:T(8,128)(2,1)S(1)}, u32[]{:S(2)}, u32[]{:S(2)}) collective-permute-start(bf16[9,8,1024]{2,1,0:T(8,128)(2,1)S(1)} %collective-permute-done.13.refs_18_), channel_id=1, source_target_pairs={{0,1},{1,0},{2,3},{3,2},{4,5},{5,4},{6,7},{7,6},{8,9},{9,8},{10,11... | collective-permute-start | bytes 442376 | tf_op jit(solution)/shard_map/ppermute | solution.py:105

commit v5 on v4

--- a/solution.py
+++ b/solution.py
@@ -85,7 +85,8 @@
     ("core", 0, ()),
     ("prepare", ()),
     ("x", 4, ("prepare",)),
-    ("z1", 8, ()),
+    ("attend", (0, 4), ()),
+    ("z1", 8, ("attend1",)),
     ("x", 8, ()),
     ("x", 12, ()),
     ("core", 2, ()),
@@ -94,8 +95,8 @@
     ("core", 8, ()),
     ("core", 10, ()),
     ("core", 12, ()),
-    ("attend", (0, 1, 2, 3, 4, 5, 6, 7, 8), ()),
-    ("core", 14, ("attend1",)),
+    ("attend", (1, 2, 3, 5, 6, 7, 8), ()),
+    ("core", 14, ("attend2",)),
     ("attend", (9, 10, 11, 12, 13, 14, 15), ()),
 )
 

time: 52.2 us -> 51.4 us (0.985)
  waiting for transfers between devices: 6.9 us -> 6.06 us
    ppermute x15, waiting for transfers between devices: 6.9 us -> 6.06 us  [permute(): return lax.ppermute(block, 'seq', pairs)]
    pallas_call x2 -> x3, Pallas kernels: 30.4 us -> 30.6 us  [attend_pieces(): pl.pallas_call(kernel, out_shape=out_shape, in_specs=[vmem] * len(operand...]
  transfers between devices with their start and end apart: 15 -> 15, of which waited for: 5 -> 5; matrix products, arithmetic and copies ran while one was open for 0% -> 0% of each run, Pallas kernels for 9% -> 10%
where the time goes in v5:
time: 51.4 us; the launch traced here: 51.2 us
  Pallas kernels  31.9 us (62%)
  starting transfers between devices  13.2 us (26%)
  waiting for transfers between devices  6.06 us (12%)
    pallas_call x3, Pallas kernels, attend_pieces(): pl.pallas_call(kernel, out_shape=out_shape, in_specs=[vmem] * len(operand...  30.6 us
    ppermute x15, starting transfers between devices, permute(): return lax.ppermute(block, 'seq', pairs)  13.2 us
    ppermute x15, waiting for transfers between devices, permute(): return lax.ppermute(block, 'seq', pairs)  6.06 us
    pallas_call x1, Pallas kernels, prepare(): pl.pallas_call(prepare_kernel, out_shape=shapes, in_specs=[pl.BlockSpec(m...  1.27 us
  transfers between devices with their start and end apart: 15, of which 5 were waited for; matrix products, arithmetic and copies ran while one was open for 0% of the time, Pallas kernels for 10%

profile of v5, /device:TPU:0, one launch (start us, length us, event | category | flops | bytes accessed | tf_op | source)
XLA Modules:
  0.0 51.2 jit_solution(11401979803658572230)
XLA Ops:
  0.0 3.0 %collective-permute-start.3 = (bf16[9,8,1024]{2,1,0:T(8,128)(2,1)}, bf16[9,8,1024]{2,1,0:T(8,128)(2,1)S(1)}, u32[]{:S(2)}, u32[]{:S(2)}) collective-permute-start(bf16[9,8,1024]{2,1,0:T(8,128)(2,1)} %shard_ref.1), channel_id=1, source_target_pairs={{0,4},{1,5},{2,6},{3,7},{4,0},{5,1},{6,2},{7,3},{8,12},{9,13},{10,... | collective-permute-start | bytes 442376 | tf_op jit(solution)/shard_map/ppermute | solution.py:106
  3.0 2.6 %collective-permute-start.7 = (bf16[9,8,1024]{2,1,0:T(8,128)(2,1)}, bf16[9,8,1024]{2,1,0:T(8,128)(2,1)S(1)}, u32[]{:S(2)}, u32[]{:S(2)}) collective-permute-start(bf16[9,8,1024]{2,1,0:T(8,128)(2,1)} %shard_ref.1), channel_id=1, source_target_pairs={{0,8},{1,9},{2,10},{3,11},{4,12},{5,13},{6,14},{7,15},{8,0},{9,1},... | collective-permute-start | bytes 442376 | tf_op jit(solution)/shard_map/ppermute | solution.py:106
  5.6 1.5 %collective-permute-start.1 = (bf16[9,8,1024]{2,1,0:T(8,128)(2,1)}, bf16[9,8,1024]{2,1,0:T(8,128)(2,1)S(1)}, u32[]{:S(2)}, u32[]{:S(2)}) collective-permute-start(bf16[9,8,1024]{2,1,0:T(8,128)(2,1)} %shard_ref.1), channel_id=1, source_target_pairs={{0,2},{1,3},{2,0},{3,1},{4,6},{5,7},{6,4},{7,5},{8,10},{9,11},{10,... | collective-permute-start | bytes 442376 | tf_op jit(solution)/shard_map/ppermute | solution.py:106
  7.1 0.0 collective-permute-start
  7.1 1.3 %prepare.1 = (bf16[128,4096]{1,0:T(8,128)(2,1)S(1)}, bf16[9,8,1024]{2,1,0:T(8,128)(2,1)S(1)}, f32[128,128]{1,0:T(8,128)S(1)}, f32[1152,128]{1,0:T(8,128)S(1)}, f32[1,1152]{1,0:T(1,128)S(1)}) custom-call(bf16[128,4096]{1,0:T(8,128)(2,1)} %q_ref.1, bf16[9,8,1024]{2,1,0:T(8,128)(2,1)} %shard_ref.1, s32[16]{0:T(128)} %lengths_in.1, s32[16]{0:T(128)} %owner_in.1, ...), custom_call_target="tpu_custom_call" | custom-call | tf_op jit(solution)/shard_map/prepare/pallas_call | solution.py:172
  8.4 1.2 %collective-permute-done.3.refs_3_.refs_8_ = bf16[9,8,1024]{2,1,0:T(8,128)(2,1)S(1)} collective-permute-done((bf16[9,8,1024]{2,1,0:T(8,128)(2,1)}, bf16[9,8,1024]{2,1,0:T(8,128)(2,1)S(1)}, u32[]{:S(2)}, u32[]{:S(2)}) %collective-permute-start.3) | collective-permute-done | bytes 147488 | tf_op jit(solution)/shard_map/ppermute | solution.py:106
  9.6 1.8 %collective-permute-start.5 = (bf16[9,8,1024]{2,1,0:T(8,128)(2,1)S(1)}, bf16[9,8,1024]{2,1,0:T(8,128)(2,1)S(1)}, u32[]{:S(2)}, u32[]{:S(2)}) collective-permute-start(bf16[9,8,1024]{2,1,0:T(8,128)(2,1)S(1)} %collective-permute-done.3.refs_3_.refs_8_), channel_id=1, source_target_pairs={{0,2},{1,3},{2,0},{3,1},{4,6},{5,7},{6,4},{7,5},{8,10},{9,11},{10,... | collective-permute-start | bytes 442376 | tf_op jit(solution)/shard_map/ppermute | solution.py:106
  11.4 1.4 %attention_stage.2.refs_9_ = f32[128,8192]{1,0:T(8,128)S(1)} custom-call(bf16[128,4096]{1,0:T(8,128)(2,1)S(1)} %get-tuple-element.13.refs_0_, f32[1152,128]{1,0:T(8,128)S(1)} %get-tuple-element.14.refs_1_, bf16[9,8,1024]{2,1,0:T(8,128)(2,1)S(1)} %get-tuple-element.17.refs_2_.refs_4_, bf16[9,8,1024]{2,1,0:T(8,128)(2,1)S(1)} %collective-permute-done.3.refs_3_.refs_8_), custom_call_target="tpu_custom_call" | custom-call | tf_op jit(solution)/shard_map/attention_stage/pallas_call | solution.py:332
  12.8 0.0 collective-permute-done.7.refs_8_.refs_12_
  12.8 0.3 collective-permute-start.11
  13.1 0.0 collective-permute-start.4
  13.1 0.0 collective-permute-done.1.refs_3_.refs_6_
  13.1 0.5 collective-permute-start.2
  13.6 0.0 collective-permute-done.refs_2_.refs_5_
  13.6 1.5 %collective-permute-start.9 = (bf16[9,8,1024]{2,1,0:T(8,128)(2,1)S(1)}, bf16[9,8,1024]{2,1,0:T(8,128)(2,1)S(1)}, u32[]{:S(2)}, u32[]{:S(2)}) collective-permute-start(bf16[9,8,1024]{2,1,0:T(8,128)(2,1)S(1)} %collective-permute-done.7.refs_8_.refs_12_), channel_id=1, source_target_pairs={{0,2},{1,3},{2,0},{3,1},{4,6},{5,7},{6,4},{7,5},{8,10},{9,11},{10,... | collective-permute-start | bytes 442376 | tf_op jit(solution)/shard_map/ppermute | solution.py:106
  15.1 0.0 collective-permute-done.5.refs_6_.refs_10_
  15.1 0.0 collective-permute-start.6
  15.1 2.9 %collective-permute-done.11.refs_16_ = bf16[9,8,1024]{2,1,0:T(8,128)(2,1)S(1)} collective-permute-done((bf16[9,8,1024]{2,1,0:T(8,128)(2,1)S(1)}, bf16[9,8,1024]{2,1,0:T(8,128)(2,1)S(1)}, u32[]{:S(2)}, u32[]{:S(2)}) %collective-permute-start.11) | collective-permute-done | bytes 147488 | tf_op jit(solution)/shard_map/ppermute | solution.py:106
  18.0 1.3 %collective-permute-start.13 = (bf16[9,8,1024]{2,1,0:T(8,128)(2,1)S(1)}, bf16[9,8,1024]{2,1,0:T(8,128)(2,1)S(1)}, u32[]{:S(2)}, u32[]{:S(2)}) collective-permute-start(bf16[9,8,1024]{2,1,0:T(8,128)(2,1)S(1)} %collective-permute-done.11.refs_16_), channel_id=1, source_target_pairs={{0,2},{1,3},{2,0},{3,1},{4,6},{5,7},{6,4},{7,5},{8,10},{9,11},{10,... | collective-permute-start | bytes 442376 | tf_op jit(solution)/shard_map/ppermute | solution.py:106
  19.3 0.0 collective-permute-done.4.refs_5_.refs_9_
  19.3 0.0 collective-permute-start.8
  19.3 0.0 collective-permute-done.2.refs_4_.refs_7_
  19.3 0.5 collective-permute-start.12
  19.8 0.5 collective-permute-done.9.refs_14_
  20.3 0.0 collective-permute-start.10
  20.3 0.0 collective-permute-done.6.refs_7_.refs_11_
  20.3 2.5 %attention_stage.3.refs_20_ = f32[128,8192]{1,0:T(8,128)S(1)} custom-call(bf16[128,4096]{1,0:T(8,128)(2,1)S(1)} %get-tuple-element.13.refs_0_, f32[1152,128]{1,0:T(8,128)S(1)} %get-tuple-element.14.refs_1_, bf16[9,8,1024]{2,1,0:T(8,128)(2,1)S(1)} %collective-permute-done.refs_2_.refs_5_, bf16[9,8,1024]{2,1,0:T(8,128)(2,1)S(1)} %collective-permute-done.1.refs_3_.refs_6_, ...), custom_call_target="tpu_custom_call" | custom-call | tf_op jit(solution)/shard_map/attention_stage/pallas_call | solution.py:332
  22.9 0.3 collective-permute-done.13.refs_18_
  23.2 0.3 collective-permute-start.14
  23.4 0.0 collective-permute-done.8.refs_13_
  23.4 0.0 collective-permute-done.12.refs_17_
  23.5 0.0 collective-permute-done.10.refs_15_
  23.5 1.1 %collective-permute-done.14.refs_19_ = bf16[9,8,1024]{2,1,0:T(8,128)(2,1)S(1)} collective-permute-done((bf16[9,8,1024]{2,1,0:T(8,128)(2,1)S(1)}, bf16[9,8,1024]{2,1,0:T(8,128)(2,1)S(1)}, u32[]{:S(2)}, u32[]{:S(2)}) %collective-permute-start.14) | collective-permute-done | bytes 147488 | tf_op jit(solution)/shard_map/ppermute | solution.py:106
  24.6 26.7 %attention_last.1 = bf16[128,4096]{1,0:T(8,128)(2,1)} custom-call(bf16[128,4096]{1,0:T(8,128)(2,1)S(1)} %get-tuple-element.13.refs_0_, f32[1152,128]{1,0:T(8,128)S(1)} %get-tuple-element.14.refs_1_, f32[128,128]{1,0:T(8,128)S(1)} %get-tuple-element.15.refs_2_, f32[1,1152]{1,0:T(1,128)S(1)} %get-tuple-element.16.refs_3_, ...), custom_call_target="tpu_custom_call" | custom-call | tf_op jit(solution)/shard_map/attention_last/pallas_call | solution.py:332
Async XLA Ops:
  0.0 9.6 %collective-permute-start.3 = (bf16[9,8,1024]{2,1,0:T(8,128)(2,1)}, bf16[9,8,1024]{2,1,0:T(8,128)(2,1)S(1)}, u32[]{:S(2)}, u32[]{:S(2)}) collective-permute-start(bf16[9,8,1024]{2,1,0:T(8,128)(2,1)} %shard_ref.1), channel_id=1, source_target_pairs={{0,4},{1,5},{2,6},{3,7},{4,0},{5,1},{6,2},{7,3},{8,12},{9,13},{10,... | collective-permute-start | bytes 442376 | tf_op jit(solution)/shard_map/ppermute | solution.py:106
  3.0 9.8 %collective-permute-start.7 = (bf16[9,8,1024]{2,1,0:T(8,128)(2,1)}, bf16[9,8,1024]{2,1,0:T(8,128)(2,1)S(1)}, u32[]{:S(2)}, u32[]{:S(2)}) collective-permute-start(bf16[9,8,1024]{2,1,0:T(8,128)(2,1)} %shard_ref.1), channel_id=1, source_target_pairs={{0,8},{1,9},{2,10},{3,11},{4,12},{5,13},{6,14},{7,15},{8,0},{9,1},... | collective-permute-start | bytes 442376 | tf_op jit(solution)/shard_map/ppermute | solution.py:106
  5.6 7.5 %collective-permute-start.1 = (bf16[9,8,1024]{2,1,0:T(8,128)(2,1)}, bf16[9,8,1024]{2,1,0:T(8,128)(2,1)S(1)}, u32[]{:S(2)}, u32[]{:S(2)}) collective-permute-start(bf16[9,8,1024]{2,1,0:T(8,128)(2,1)} %shard_ref.1), channel_id=1, source_target_pairs={{0,2},{1,3},{2,0},{3,1},{4,6},{5,7},{6,4},{7,5},{8,10},{9,11},{10,... | collective-permute-start | bytes 442376 | tf_op jit(solution)/shard_map/ppermute | solution.py:106
  7.1 6.5 %collective-permute-start = (bf16[9,8,1024]{2,1,0:T(8,128)(2,1)}, bf16[9,8,1024]{2,1,0:T(8,128)(2,1)S(1)}, u32[]{:S(2)}, u32[]{:S(2)}) collective-permute-start(bf16[9,8,1024]{2,1,0:T(8,128)(2,1)} %shard_ref.1), channel_id=1, source_target_pairs={{0,1},{1,0},{2,3},{3,2},{4,5},{5,4},{6,7},{7,6},{8,9},{9,8},{10,11... | collective-permute-start | bytes 442376 | tf_op jit(solution)/shard_map/ppermute | solution.py:106
  9.6 5.5 %collective-permute-start.5 = (bf16[9,8,1024]{2,1,0:T(8,128)(2,1)S(1)}, bf16[9,8,1024]{2,1,0:T(8,128)(2,1)S(1)}, u32[]{:S(2)}, u32[]{:S(2)}) collective-permute-start(bf16[9,8,1024]{2,1,0:T(8,128)(2,1)S(1)} %collective-permute-done.3.refs_3_.refs_8_), channel_id=1, source_target_pairs={{0,2},{1,3},{2,0},{3,1},{4,6},{5,7},{6,4},{7,5},{8,10},{9,11},{10,... | collective-permute-start | bytes 442376 | tf_op jit(solution)/shard_map/ppermute | solution.py:106
  12.8 5.2 %collective-permute-start.11 = (bf16[9,8,1024]{2,1,0:T(8,128)(2,1)S(1)}, bf16[9,8,1024]{2,1,0:T(8,128)(2,1)S(1)}, u32[]{:S(2)}, u32[]{:S(2)}) collective-permute-start(bf16[9,8,1024]{2,1,0:T(8,128)(2,1)S(1)} %collective-permute-done.7.refs_8_.refs_12_), channel_id=1, source_target_pairs={{0,4},{1,5},{2,6},{3,7},{4,0},{5,1},{6,2},{7,3},{8,12},{9,13},{10,... | collective-permute-start | bytes 442376 | tf_op jit(solution)/shard_map/ppermute | solution.py:106
  13.1 6.2 %collective-permute-start.4 = (bf16[9,8,1024]{2,1,0:T(8,128)(2,1)S(1)}, bf16[9,8,1024]{2,1,0:T(8,128)(2,1)S(1)}, u32[]{:S(2)}, u32[]{:S(2)}) collective-permute-start(bf16[9,8,1024]{2,1,0:T(8,128)(2,1)S(1)} %collective-permute-done.3.refs_3_.refs_8_), channel_id=1, source_target_pairs={{0,1},{1,0},{2,3},{3,2},{4,5},{5,4},{6,7},{7,6},{8,9},{9,8},{10,11... | collective-permute-start | bytes 442376 | tf_op jit(solution)/shard_map/ppermute | solution.py:106
  13.1 6.2 %collective-permute-start.2 = (bf16[9,8,1024]{2,1,0:T(8,128)(2,1)S(1)}, bf16[9,8,1024]{2,1,0:T(8,128)(2,1)S(1)}, u32[]{:S(2)}, u32[]{:S(2)}) collective-permute-start(bf16[9,8,1024]{2,1,0:T(8,128)(2,1)S(1)} %collective-permute-done.1.refs_3_.refs_6_), channel_id=1, source_target_pairs={{0,1},{1,0},{2,3},{3,2},{4,5},{5,4},{6,7},{7,6},{8,9},{9,8},{10,11... | collective-permute-start | bytes 442376 | tf_op jit(solution)/shard_map/ppermute | solution.py:106
  13.6 6.7 %collective-permute-start.9 = (bf16[9,8,1024]{2,1,0:T(8,128)(2,1)S(1)}, bf16[9,8,1024]{2,1,0:T(8,128)(2,1)S(1)}, u32[]{:S(2)}, u32[]{:S(2)}) collective-permute-start(bf16[9,8,1024]{2,1,0:T(8,128)(2,1)S(1)} %collective-permute-done.7.refs_8_.refs_12_), channel_id=1, source_target_pairs={{0,2},{1,3},{2,0},{3,1},{4,6},{5,7},{6,4},{7,5},{8,10},{9,11},{10,... | collective-permute-start | bytes 442376 | tf_op jit(solution)/shard_map/ppermute | solution.py:106
  15.1 5.2 %collective-permute-start.6 = (bf16[9,8,1024]{2,1,0:T(8,128)(2,1)S(1)}, bf16[9,8,1024]{2,1,0:T(8,128)(2,1)S(1)}, u32[]{:S(2)}, u32[]{:S(2)}) collective-permute-start(bf16[9,8,1024]{2,1,0:T(8,128)(2,1)S(1)} %collective-permute-done.5.refs_6_.refs_10_), channel_id=1, source_target_pairs={{0,1},{1,0},{2,3},{3,2},{4,5},{5,4},{6,7},{7,6},{8,9},{9,8},{10,11... | collective-permute-start | bytes 442376 | tf_op jit(solution)/shard_map/ppermute | solution.py:106
  18.0 5.1 %collective-permute-start.13 = (bf16[9,8,1024]{2,1,0:T(8,128)(2,1)S(1)}, bf16[9,8,1024]{2,1,0:T(8,128)(2,1)S(1)}, u32[]{:S(2)}, u32[]{:S(2)}) collective-permute-start(bf16[9,8,1024]{2,1,0:T(8,128)(2,1)S(1)} %collective-permute-done.11.refs_16_), channel_id=1, source_target_pairs={{0,2},{1,3},{2,0},{3,1},{4,6},{5,7},{6,4},{7,5},{8,10},{9,11},{10,... | collective-permute-start | bytes 442376 | tf_op jit(solution)/shard_map/ppermute | solution.py:106
  19.3 4.1 %collective-permute-start.8 = (bf16[9,8,1024]{2,1,0:T(8,128)(2,1)S(1)}, bf16[9,8,1024]{2,1,0:T(8,128)(2,1)S(1)}, u32[]{:S(2)}, u32[]{:S(2)}) collective-permute-start(bf16[9,8,1024]{2,1,0:T(8,128)(2,1)S(1)} %collective-permute-done.7.refs_8_.refs_12_), channel_id=1, source_target_pairs={{0,1},{1,0},{2,3},{3,2},{4,5},{5,4},{6,7},{7,6},{8,9},{9,8},{10,11... | collective-permute-start | bytes 442376 | tf_op jit(solution)/shard_map/ppermute | solution.py:106
  19.3 4.1 %collective-permute-start.12 = (bf16[9,8,1024]{2,1,0:T(8,128)(2,1)S(1)}, bf16[9,8,1024]{2,1,0:T(8,128)(2,1)S(1)}, u32[]{:S(2)}, u32[]{:S(2)}) collective-permute-start(bf16[9,8,1024]{2,1,0:T(8,128)(2,1)S(1)} %collective-permute-done.11.refs_16_), channel_id=1, source_target_pairs={{0,1},{1,0},{2,3},{3,2},{4,5},{5,4},{6,7},{7,6},{8,9},{9,8},{10,11... | collective-permute-start | bytes 442376 | tf_op jit(solution)/shard_map/ppermute | solution.py:106
  20.3 3.1 %collective-permute-start.10 = (bf16[9,8,1024]{2,1,0:T(8,128)(2,1)S(1)}, bf16[9,8,1024]{2,1,0:T(8,128)(2,1)S(1)}, u32[]{:S(2)}, u32[]{:S(2)}) collective-permute-start(bf16[9,8,1024]{2,1,0:T(8,128)(2,1)S(1)} %collective-permute-done.9.refs_14_), channel_id=1, source_target_pairs={{0,1},{1,0},{2,3},{3,2},{4,5},{5,4},{6,7},{7,6},{8,9},{9,8},{10,11... | collective-permute-start | bytes 442376 | tf_op jit(solution)/shard_map/ppermute | solution.py:106
  23.2 1.4 %collective-permute-start.14 = (bf16[9,8,1024]{2,1,0:T(8,128)(2,1)S(1)}, bf16[9,8,1024]{2,1,0:T(8,128)(2,1)S(1)}, u32[]{:S(2)}, u32[]{:S(2)}) collective-permute-start(bf16[9,8,1024]{2,1,0:T(8,128)(2,1)S(1)} %collective-permute-done.13.refs_18_), channel_id=1, source_target_pairs={{0,1},{1,0},{2,3},{3,2},{4,5},{5,4},{6,7},{7,6},{8,9},{9,8},{10,11... | collective-permute-start | bytes 442376 | tf_op jit(solution)/shard_map/ppermute | solution.py:106

commit v6 on v5

--- a/solution.py
+++ b/solution.py
@@ -97,7 +97,8 @@
     ("core", 12, ()),
     ("attend", (1, 2, 3, 5, 6, 7, 8), ()),
     ("core", 14, ("attend2",)),
-    ("attend", (9, 10, 11, 12, 13, 14, 15), ()),
+    ("attend", (9, 10, 12, (13, 0, 5)), (14,)),
+    ("attend", (11, (13, 5, 9), 14, 15), ()),
 )
 
 
@@ -181,26 +182,35 @@
     )(*inputs)
 
 
-def lay_out(piece_ref, h, keep):
-    piece_tokens = piece_ref.shape[0] * piece_ref.shape[1]
-    keys = piece_ref[:, :, h * HD : (h + 1) * HD].reshape(piece_tokens, HD)
-    values = piece_ref[:, :, (KVH + h) * HD : (KVH + h + 1) * HD].reshape(piece_tokens, HD)
+def part_of(entry, pages_dev):
+    return (entry, 0, pages_dev) if isinstance(entry, int) else entry
+
+
+def lay_out(piece_ref, begin, end, h, keep):
+    tokens = (end - begin) * piece_ref.shape[1]
+    keys = piece_ref[begin:end, :, h * HD : (h + 1) * HD].reshape(tokens, HD)
+    values = piece_ref[begin:end, :, (KVH + h) * HD : (KVH + h + 1) * HD].reshape(tokens, HD)
     return keys, values * keep, keep
 
 
 def stage_sums(q_ref, keep_ref, piece_refs, numbers, keys, values, old_sums, give):
     tokens = keys.shape[1]
-    piece_tokens = piece_refs[0].shape[0] * piece_refs[0].shape[1]
-    held = len(numbers) * piece_tokens
+    pages_dev, page_tokens = piece_refs[0].shape[:2]
+    parts = [part_of(entry, pages_dev) for entry in numbers]
+    held = sum(end - begin for _, begin, end in parts) * page_tokens
     if held < tokens:
         keys[:, held:, :] = jnp.zeros((KVH, tokens - held, HD), jnp.bfloat16)
         values[:, held:, :] = jnp.zeros((KVH, tokens - held, 2 * HD), jnp.bfloat16)
-    for i, number in enumerate(numbers):
-        keep = keep_ref[number * piece_tokens : (number + 1) * piece_tokens, :].astype(jnp.bfloat16)
-        span = slice(i * piece_tokens, (i + 1) * piece_tokens)
+    filled = 0
+    for i, (number, begin, end) in enumerate(parts):
+        first = (number * pages_dev + begin) * page_tokens
+        count = (end - begin) * page_tokens
+        keep = keep_ref[first : first + count, :].astype(jnp.bfloat16)
+        span = slice(filled, filled + count)
+        filled += count
         for h in range(KVH):
             keys[h, span, :], values[h, span, :HD], values[h, span, HD:] = lay_out(
-                piece_refs[i], h, keep
+                piece_refs[i], begin, end, h, keep
             )
     rows = q_ref.shape[0]
     for begin in range(0, QH, TOGETHER):
@@ -260,7 +270,8 @@
         if n % GROUP == GROUP - 1:
             copies[n // GROUP].start()
 
-    new_refs = [piece_refs[number] for number in numbers]
+    pages_dev = piece_refs[0].shape[0]
+    new_refs = [piece_refs[part_of(entry, pages_dev)[0]] for entry in numbers]
     stage_sums(q_ref, keep_ref, new_refs, numbers, keys, values, old_sums, give)
     fits = (added[0] <= 2.0**100) & (added[1] >= 2.0**-100)
     fits = jnp.min(jnp.where(fits, 1.0, 0.0).reshape(rows // 8, 8, HD), 0)
@@ -277,7 +288,7 @@
                 span = slice(number * piece_tokens, (number + 1) * piece_tokens)
                 keep = keep_ref[span, :].astype(jnp.bfloat16)
                 all_keys[span, :], all_values[span, :HD], all_values[span, HD:] = lay_out(
-                    piece_refs[number], h, keep
+                    piece_refs[number], 0, pages_dev, h, keep
                 )
 
             def one_head(g, unused):
@@ -305,8 +316,9 @@
 
 def attend_pieces(queries, keep, live, bias, pieces, numbers, state, last):
     rows, features = queries.shape
-    piece_tokens = pieces[numbers[0]].shape[0] * pieces[numbers[0]].shape[1]
-    held = len(numbers) * piece_tokens
+    pages_dev, page_tokens = pieces[0].shape[:2]
+    parts = [part_of(entry, pages_dev) for entry in numbers]
+    held = sum(end - begin for _, begin, end in parts) * page_tokens
     tokens = held + -held % HD
     vmem = pl.BlockSpec(memory_space=pltpu.VMEM)
     scratch = [
@@ -314,7 +326,7 @@
         pltpu.VMEM((KVH, tokens, 2 * HD), jnp.bfloat16),
     ]
     if last:
-        everything = GATHER_DEVICES * piece_tokens
+        everything = GATHER_DEVICES * pages_dev * page_tokens
         scratch += [
             pltpu.VMEM((rows, features), jnp.bfloat16),
             pltpu.VMEM((everything, HD), jnp.bfloat16),
@@ -326,7 +338,7 @@
         out_shape = jax.ShapeDtypeStruct((rows, features), jnp.bfloat16)
     else:
         kernel = functools.partial(stage_kernel, numbers=numbers, first=not state)
-        operands = [queries, keep] + [pieces[n] for n in numbers]
+        operands = [queries, keep] + [pieces[n] for n, _, _ in parts]
         out_shape = jax.ShapeDtypeStruct((rows, 2 * features), jnp.float32)
     operands += state
     return pl.pallas_call(

time: 51.4 us -> 50.7 us (0.986)
  waiting for transfers between devices: 6.06 us -> 5 us
    ppermute x15, waiting for transfers between devices: 6.06 us -> 5 us  [permute(): return lax.ppermute(block, 'seq', pairs)]
    pallas_call x3 -> x4, Pallas kernels: 30.6 us -> 31 us  [attend_pieces(): pl.pallas_call(kernel, out_shape=out_shape, in_specs=[vmem] * len(operand...]
  transfers between devices with their start and end apart: 15 -> 15, of which waited for: 5 -> 4; matrix products, arithmetic and copies ran while one was open for 0% -> 0% of each run, Pallas kernels for 10% -> 13%
where the time goes in v6:
time: 50.7 us; the launch traced here: 50.5 us
  Pallas kernels  32.2 us (64%)
  starting transfers between devices  13.2 us (26%)
  waiting for transfers between devices  5 us (10%)
    pallas_call x4, Pallas kernels, attend_pieces(): pl.pallas_call(kernel, out_shape=out_shape, in_specs=[vmem] * len(operand...  31 us
    ppermute x15, starting transfers between devices, permute(): return lax.ppermute(block, 'seq', pairs)  13.2 us
    ppermute x15, waiting for transfers between devices, permute(): return lax.ppermute(block, 'seq', pairs)  5 us
    pallas_call x1, Pallas kernels, prepare(): pl.pallas_call(prepare_kernel, out_shape=shapes, in_specs=[pl.BlockSpec(m...  1.27 us
  transfers between devices with their start and end apart: 15, of which 4 were waited for; matrix products, arithmetic and copies ran while one was open for 0% of the time, Pallas kernels for 13%

profile of v6, /device:TPU:0, one launch (start us, length us, event | category | flops | bytes accessed | tf_op | source)
XLA Modules:
  0.0 50.5 jit_solution(15145927663265456164)
XLA Ops:
  0.0 3.0 %collective-permute-start.3 = (bf16[9,8,1024]{2,1,0:T(8,128)(2,1)}, bf16[9,8,1024]{2,1,0:T(8,128)(2,1)S(1)}, u32[]{:S(2)}, u32[]{:S(2)}) collective-permute-start(bf16[9,8,1024]{2,1,0:T(8,128)(2,1)} %shard_ref.1), channel_id=1, source_target_pairs={{0,4},{1,5},{2,6},{3,7},{4,0},{5,1},{6,2},{7,3},{8,12},{9,13},{10,... | collective-permute-start | bytes 442376 | tf_op jit(solution)/shard_map/ppermute | solution.py:107
  3.0 2.6 %collective-permute-start.7 = (bf16[9,8,1024]{2,1,0:T(8,128)(2,1)}, bf16[9,8,1024]{2,1,0:T(8,128)(2,1)S(1)}, u32[]{:S(2)}, u32[]{:S(2)}) collective-permute-start(bf16[9,8,1024]{2,1,0:T(8,128)(2,1)} %shard_ref.1), channel_id=1, source_target_pairs={{0,8},{1,9},{2,10},{3,11},{4,12},{5,13},{6,14},{7,15},{8,0},{9,1},... | collective-permute-start | bytes 442376 | tf_op jit(solution)/shard_map/ppermute | solution.py:107
  5.6 1.5 %collective-permute-start.1 = (bf16[9,8,1024]{2,1,0:T(8,128)(2,1)}, bf16[9,8,1024]{2,1,0:T(8,128)(2,1)S(1)}, u32[]{:S(2)}, u32[]{:S(2)}) collective-permute-start(bf16[9,8,1024]{2,1,0:T(8,128)(2,1)} %shard_ref.1), channel_id=1, source_target_pairs={{0,2},{1,3},{2,0},{3,1},{4,6},{5,7},{6,4},{7,5},{8,10},{9,11},{10,... | collective-permute-start | bytes 442376 | tf_op jit(solution)/shard_map/ppermute | solution.py:107
  7.1 0.0 collective-permute-start
  7.1 1.3 %prepare.1 = (bf16[128,4096]{1,0:T(8,128)(2,1)S(1)}, bf16[9,8,1024]{2,1,0:T(8,128)(2,1)S(1)}, f32[128,128]{1,0:T(8,128)S(1)}, f32[1152,128]{1,0:T(8,128)S(1)}, f32[1,1152]{1,0:T(1,128)S(1)}) custom-call(bf16[128,4096]{1,0:T(8,128)(2,1)} %q_ref.1, bf16[9,8,1024]{2,1,0:T(8,128)(2,1)} %shard_ref.1, s32[16]{0:T(128)} %lengths_in.1, s32[16]{0:T(128)} %owner_in.1, ...), custom_call_target="tpu_custom_call" | custom-call | tf_op jit(solution)/shard_map/prepare/pallas_call | solution.py:173
  8.4 1.2 %collective-permute-done.3.refs_3_.refs_8_ = bf16[9,8,1024]{2,1,0:T(8,128)(2,1)S(1)} collective-permute-done((bf16[9,8,1024]{2,1,0:T(8,128)(2,1)}, bf16[9,8,1024]{2,1,0:T(8,128)(2,1)S(1)}, u32[]{:S(2)}, u32[]{:S(2)}) %collective-permute-start.3) | collective-permute-done | bytes 147488 | tf_op jit(solution)/shard_map/ppermute | solution.py:107
  9.6 1.8 %collective-permute-start.5 = (bf16[9,8,1024]{2,1,0:T(8,128)(2,1)S(1)}, bf16[9,8,1024]{2,1,0:T(8,128)(2,1)S(1)}, u32[]{:S(2)}, u32[]{:S(2)}) collective-permute-start(bf16[9,8,1024]{2,1,0:T(8,128)(2,1)S(1)} %collective-permute-done.3.refs_3_.refs_8_), channel_id=1, source_target_pairs={{0,2},{1,3},{2,0},{3,1},{4,6},{5,7},{6,4},{7,5},{8,10},{9,11},{10,... | collective-permute-start | bytes 442376 | tf_op jit(solution)/shard_map/ppermute | solution.py:107
  11.4 1.4 %attention_stage.3.refs_9_ = f32[128,8192]{1,0:T(8,128)S(1)} custom-call(bf16[128,4096]{1,0:T(8,128)(2,1)S(1)} %get-tuple-element.14.refs_0_, f32[1152,128]{1,0:T(8,128)S(1)} %get-tuple-element.22.refs_1_, bf16[9,8,1024]{2,1,0:T(8,128)(2,1)S(1)} %get-tuple-element.18.refs_2_.refs_4_, bf16[9,8,1024]{2,1,0:T(8,128)(2,1)S(1)} %collective-permute-done.3.refs_3_.refs_8_), custom_call_target="tpu_custom_call" | custom-call | tf_op jit(solution)/shard_map/attention_stage/pallas_call | solution.py:344
  12.8 0.0 collective-permute-done.7.refs_8_.refs_12_
  12.8 0.3 collective-permute-start.11
  13.1 0.0 collective-permute-start.4
  13.1 0.0 collective-permute-done.1.refs_3_.refs_6_
  13.1 0.5 %collective-permute-start.2 = (bf16[9,8,1024]{2,1,0:T(8,128)(2,1)S(1)}, bf16[9,8,1024]{2,1,0:T(8,128)(2,1)S(1)}, u32[]{:S(2)}, u32[]{:S(2)}) collective-permute-start(bf16[9,8,1024]{2,1,0:T(8,128)(2,1)S(1)} %collective-permute-done.1.refs_3_.refs_6_), channel_id=1, source_target_pairs={{0,1},{1,0},{2,3},{3,2},{4,5},{5,4},{6,7},{7,6},{8,9},{9,8},{10,11... | collective-permute-start | bytes 442376 | tf_op jit(solution)/shard_map/ppermute | solution.py:107
  13.6 0.0 collective-permute-done.refs_2_.refs_5_
  13.6 1.5 %collective-permute-start.9 = (bf16[9,8,1024]{2,1,0:T(8,128)(2,1)S(1)}, bf16[9,8,1024]{2,1,0:T(8,128)(2,1)S(1)}, u32[]{:S(2)}, u32[]{:S(2)}) collective-permute-start(bf16[9,8,1024]{2,1,0:T(8,128)(2,1)S(1)} %collective-permute-done.7.refs_8_.refs_12_), channel_id=1, source_target_pairs={{0,2},{1,3},{2,0},{3,1},{4,6},{5,7},{6,4},{7,5},{8,10},{9,11},{10,... | collective-permute-start | bytes 442376 | tf_op jit(solution)/shard_map/ppermute | solution.py:107
  15.1 0.0 collective-permute-done.5.refs_6_.refs_10_
  15.1 0.0 collective-permute-start.6
  15.1 2.9 %collective-permute-done.11.refs_4_.refs_16_ = bf16[9,8,1024]{2,1,0:T(8,128)(2,1)S(1)} collective-permute-done((bf16[9,8,1024]{2,1,0:T(8,128)(2,1)S(1)}, bf16[9,8,1024]{2,1,0:T(8,128)(2,1)S(1)}, u32[]{:S(2)}, u32[]{:S(2)}) %collective-permute-start.11) | collective-permute-done | bytes 147488 | tf_op jit(solution)/shard_map/ppermute | solution.py:107
  18.0 1.3 %collective-permute-start.13 = (bf16[9,8,1024]{2,1,0:T(8,128)(2,1)S(1)}, bf16[9,8,1024]{2,1,0:T(8,128)(2,1)S(1)}, u32[]{:S(2)}, u32[]{:S(2)}) collective-permute-start(bf16[9,8,1024]{2,1,0:T(8,128)(2,1)S(1)} %collective-permute-done.11.refs_4_.refs_16_), channel_id=1, source_target_pairs={{0,2},{1,3},{2,0},{3,1},{4,6},{5,7},{6,4},{7,5},{8,10},{9,11},{10,... | collective-permute-start | bytes 442376 | tf_op jit(solution)/shard_map/ppermute | solution.py:107
  19.3 0.0 collective-permute-done.4.refs_5_.refs_9_
  19.3 0.0 collective-permute-start.8
  19.3 0.0 collective-permute-done.2.refs_4_.refs_7_
  19.3 0.5 %collective-permute-start.12 = (bf16[9,8,1024]{2,1,0:T(8,128)(2,1)S(1)}, bf16[9,8,1024]{2,1,0:T(8,128)(2,1)S(1)}, u32[]{:S(2)}, u32[]{:S(2)}) collective-permute-start(bf16[9,8,1024]{2,1,0:T(8,128)(2,1)S(1)} %collective-permute-done.11.refs_4_.refs_16_), channel_id=1, source_target_pairs={{0,1},{1,0},{2,3},{3,2},{4,5},{5,4},{6,7},{7,6},{8,9},{9,8},{10,11... | collective-permute-start | bytes 442376 | tf_op jit(solution)/shard_map/ppermute | solution.py:107
  19.8 0.5 collective-permute-done.9.refs_3_.refs_14_
  20.3 0.0 collective-permute-start.10
  20.3 0.0 collective-permute-done.6.refs_7_.refs_11_
  20.3 2.5 %attention_stage.4.refs_6_ = f32[128,8192]{1,0:T(8,128)S(1)} custom-call(bf16[128,4096]{1,0:T(8,128)(2,1)S(1)} %get-tuple-element.14.refs_0_, f32[1152,128]{1,0:T(8,128)S(1)} %get-tuple-element.22.refs_1_, bf16[9,8,1024]{2,1,0:T(8,128)(2,1)S(1)} %collective-permute-done.refs_2_.refs_5_, bf16[9,8,1024]{2,1,0:T(8,128)(2,1)S(1)} %collective-permute-done.1.refs_3_.refs_6_, ...), custom_call_target="tpu_custom_call" | custom-call | tf_op jit(solution)/shard_map/attention_stage/pallas_call | solution.py:344
  22.8 0.3 collective-permute-done.13.refs_18_
  23.2 0.2 collective-permute-start.14
  23.4 0.0 collective-permute-done.8.refs_2_.refs_13_
  23.4 0.0 collective-permute-done.12.refs_5_.refs_17_
  23.4 1.4 %attention_stage.5.refs_20_ = f32[128,8192]{1,0:T(8,128)S(1)} custom-call(bf16[128,4096]{1,0:T(8,128)(2,1)S(1)} %get-tuple-element.14.refs_0_, f32[1152,128]{1,0:T(8,128)S(1)} %get-tuple-element.22.refs_1_, bf16[9,8,1024]{2,1,0:T(8,128)(2,1)S(1)} %collective-permute-done.8.refs_2_.refs_13_, bf16[9,8,1024]{2,1,0:T(8,128)(2,1)S(1)} %collective-permute-done.9.refs_3_.refs_14_, ...), custom_call_target="tpu_custom_call" | custom-call | tf_op jit(solution)/shard_map/attention_stage/pallas_call | solution.py:344
  24.8 0.0 collective-permute-done.10.refs_15_
  24.8 0.0 collective-permute-done.14.refs_19_
  24.8 25.7 %attention_last.1 = bf16[128,4096]{1,0:T(8,128)(2,1)} custom-call(bf16[128,4096]{1,0:T(8,128)(2,1)S(1)} %get-tuple-element.14.refs_0_, f32[1152,128]{1,0:T(8,128)S(1)} %get-tuple-element.22.refs_1_, f32[128,128]{1,0:T(8,128)S(1)} %get-tuple-element.16.refs_2_, f32[1,1152]{1,0:T(1,128)S(1)} %get-tuple-element.17.refs_3_, ...), custom_call_target="tpu_custom_call" | custom-call | tf_op jit(solution)/shard_map/attention_last/pallas_call | solution.py:344
Async XLA Ops:
  0.0 9.6 %collective-permute-start.3 = (bf16[9,8,1024]{2,1,0:T(8,128)(2,1)}, bf16[9,8,1024]{2,1,0:T(8,128)(2,1)S(1)}, u32[]{:S(2)}, u32[]{:S(2)}) collective-permute-start(bf16[9,8,1024]{2,1,0:T(8,128)(2,1)} %shard_ref.1), channel_id=1, source_target_pairs={{0,4},{1,5},{2,6},{3,7},{4,0},{5,1},{6,2},{7,3},{8,12},{9,13},{10,... | collective-permute-start | bytes 442376 | tf_op jit(solution)/shard_map/ppermute | solution.py:107
  3.0 9.8 %collective-permute-start.7 = (bf16[9,8,1024]{2,1,0:T(8,128)(2,1)}, bf16[9,8,1024]{2,1,0:T(8,128)(2,1)S(1)}, u32[]{:S(2)}, u32[]{:S(2)}) collective-permute-start(bf16[9,8,1024]{2,1,0:T(8,128)(2,1)} %shard_ref.1), channel_id=1, source_target_pairs={{0,8},{1,9},{2,10},{3,11},{4,12},{5,13},{6,14},{7,15},{8,0},{9,1},... | collective-permute-start | bytes 442376 | tf_op jit(solution)/shard_map/ppermute | solution.py:107
  5.6 7.5 %collective-permute-start.1 = (bf16[9,8,1024]{2,1,0:T(8,128)(2,1)}, bf16[9,8,1024]{2,1,0:T(8,128)(2,1)S(1)}, u32[]{:S(2)}, u32[]{:S(2)}) collective-permute-start(bf16[9,8,1024]{2,1,0:T(8,128)(2,1)} %shard_ref.1), channel_id=1, source_target_pairs={{0,2},{1,3},{2,0},{3,1},{4,6},{5,7},{6,4},{7,5},{8,10},{9,11},{10,... | collective-permute-start | bytes 442376 | tf_op jit(solution)/shard_map/ppermute | solution.py:107
  7.1 6.5 %collective-permute-start = (bf16[9,8,1024]{2,1,0:T(8,128)(2,1)}, bf16[9,8,1024]{2,1,0:T(8,128)(2,1)S(1)}, u32[]{:S(2)}, u32[]{:S(2)}) collective-permute-start(bf16[9,8,1024]{2,1,0:T(8,128)(2,1)} %shard_ref.1), channel_id=1, source_target_pairs={{0,1},{1,0},{2,3},{3,2},{4,5},{5,4},{6,7},{7,6},{8,9},{9,8},{10,11... | collective-permute-start | bytes 442376 | tf_op jit(solution)/shard_map/ppermute | solution.py:107
  9.6 5.5 %collective-permute-start.5 = (bf16[9,8,1024]{2,1,0:T(8,128)(2,1)S(1)}, bf16[9,8,1024]{2,1,0:T(8,128)(2,1)S(1)}, u32[]{:S(2)}, u32[]{:S(2)}) collective-permute-start(bf16[9,8,1024]{2,1,0:T(8,128)(2,1)S(1)} %collective-permute-done.3.refs_3_.refs_8_), channel_id=1, source_target_pairs={{0,2},{1,3},{2,0},{3,1},{4,6},{5,7},{6,4},{7,5},{8,10},{9,11},{10,... | collective-permute-start | bytes 442376 | tf_op jit(solution)/shard_map/ppermute | solution.py:107
  12.8 5.2 %collective-permute-start.11 = (bf16[9,8,1024]{2,1,0:T(8,128)(2,1)S(1)}, bf16[9,8,1024]{2,1,0:T(8,128)(2,1)S(1)}, u32[]{:S(2)}, u32[]{:S(2)}) collective-permute-start(bf16[9,8,1024]{2,1,0:T(8,128)(2,1)S(1)} %collective-permute-done.7.refs_8_.refs_12_), channel_id=1, source_target_pairs={{0,4},{1,5},{2,6},{3,7},{4,0},{5,1},{6,2},{7,3},{8,12},{9,13},{10,... | collective-permute-start | bytes 442376 | tf_op jit(solution)/shard_map/ppermute | solution.py:107
  13.1 6.2 %collective-permute-start.4 = (bf16[9,8,1024]{2,1,0:T(8,128)(2,1)S(1)}, bf16[9,8,1024]{2,1,0:T(8,128)(2,1)S(1)}, u32[]{:S(2)}, u32[]{:S(2)}) collective-permute-start(bf16[9,8,1024]{2,1,0:T(8,128)(2,1)S(1)} %collective-permute-done.3.refs_3_.refs_8_), channel_id=1, source_target_pairs={{0,1},{1,0},{2,3},{3,2},{4,5},{5,4},{6,7},{7,6},{8,9},{9,8},{10,11... | collective-permute-start | bytes 442376 | tf_op jit(solution)/shard_map/ppermute | solution.py:107
  13.1 6.2 %collective-permute-start.2 = (bf16[9,8,1024]{2,1,0:T(8,128)(2,1)S(1)}, bf16[9,8,1024]{2,1,0:T(8,128)(2,1)S(1)}, u32[]{:S(2)}, u32[]{:S(2)}) collective-permute-start(bf16[9,8,1024]{2,1,0:T(8,128)(2,1)S(1)} %collective-permute-done.1.refs_3_.refs_6_), channel_id=1, source_target_pairs={{0,1},{1,0},{2,3},{3,2},{4,5},{5,4},{6,7},{7,6},{8,9},{9,8},{10,11... | collective-permute-start | bytes 442376 | tf_op jit(solution)/shard_map/ppermute | solution.py:107
  13.6 6.7 %collective-permute-start.9 = (bf16[9,8,1024]{2,1,0:T(8,128)(2,1)S(1)}, bf16[9,8,1024]{2,1,0:T(8,128)(2,1)S(1)}, u32[]{:S(2)}, u32[]{:S(2)}) collective-permute-start(bf16[9,8,1024]{2,1,0:T(8,128)(2,1)S(1)} %collective-permute-done.7.refs_8_.refs_12_), channel_id=1, source_target_pairs={{0,2},{1,3},{2,0},{3,1},{4,6},{5,7},{6,4},{7,5},{8,10},{9,11},{10,... | collective-permute-start | bytes 442376 | tf_op jit(solution)/shard_map/ppermute | solution.py:107
  15.1 5.2 %collective-permute-start.6 = (bf16[9,8,1024]{2,1,0:T(8,128)(2,1)S(1)}, bf16[9,8,1024]{2,1,0:T(8,128)(2,1)S(1)}, u32[]{:S(2)}, u32[]{:S(2)}) collective-permute-start(bf16[9,8,1024]{2,1,0:T(8,128)(2,1)S(1)} %collective-permute-done.5.refs_6_.refs_10_), channel_id=1, source_target_pairs={{0,1},{1,0},{2,3},{3,2},{4,5},{5,4},{6,7},{7,6},{8,9},{9,8},{10,11... | collective-permute-start | bytes 442376 | tf_op jit(solution)/shard_map/ppermute | solution.py:107
  18.0 5.1 %collective-permute-start.13 = (bf16[9,8,1024]{2,1,0:T(8,128)(2,1)S(1)}, bf16[9,8,1024]{2,1,0:T(8,128)(2,1)S(1)}, u32[]{:S(2)}, u32[]{:S(2)}) collective-permute-start(bf16[9,8,1024]{2,1,0:T(8,128)(2,1)S(1)} %collective-permute-done.11.refs_4_.refs_16_), channel_id=1, source_target_pairs={{0,2},{1,3},{2,0},{3,1},{4,6},{5,7},{6,4},{7,5},{8,10},{9,11},{10,... | collective-permute-start | bytes 442376 | tf_op jit(solution)/shard_map/ppermute | solution.py:107
  19.3 4.1 %collective-permute-start.8 = (bf16[9,8,1024]{2,1,0:T(8,128)(2,1)S(1)}, bf16[9,8,1024]{2,1,0:T(8,128)(2,1)S(1)}, u32[]{:S(2)}, u32[]{:S(2)}) collective-permute-start(bf16[9,8,1024]{2,1,0:T(8,128)(2,1)S(1)} %collective-permute-done.7.refs_8_.refs_12_), channel_id=1, source_target_pairs={{0,1},{1,0},{2,3},{3,2},{4,5},{5,4},{6,7},{7,6},{8,9},{9,8},{10,11... | collective-permute-start | bytes 442376 | tf_op jit(solution)/shard_map/ppermute | solution.py:107
  19.3 4.1 %collective-permute-start.12 = (bf16[9,8,1024]{2,1,0:T(8,128)(2,1)S(1)}, bf16[9,8,1024]{2,1,0:T(8,128)(2,1)S(1)}, u32[]{:S(2)}, u32[]{:S(2)}) collective-permute-start(bf16[9,8,1024]{2,1,0:T(8,128)(2,1)S(1)} %collective-permute-done.11.refs_4_.refs_16_), channel_id=1, source_target_pairs={{0,1},{1,0},{2,3},{3,2},{4,5},{5,4},{6,7},{7,6},{8,9},{9,8},{10,11... | collective-permute-start | bytes 442376 | tf_op jit(solution)/shard_map/ppermute | solution.py:107
  20.3 4.5 %collective-permute-start.10 = (bf16[9,8,1024]{2,1,0:T(8,128)(2,1)S(1)}, bf16[9,8,1024]{2,1,0:T(8,128)(2,1)S(1)}, u32[]{:S(2)}, u32[]{:S(2)}) collective-permute-start(bf16[9,8,1024]{2,1,0:T(8,128)(2,1)S(1)} %collective-permute-done.9.refs_3_.refs_14_), channel_id=1, source_target_pairs={{0,1},{1,0},{2,3},{3,2},{4,5},{5,4},{6,7},{7,6},{8,9},{9,8},{10,11... | collective-permute-start | bytes 442376 | tf_op jit(solution)/shard_map/ppermute | solution.py:107
  23.2 1.7 %collective-permute-start.14 = (bf16[9,8,1024]{2,1,0:T(8,128)(2,1)S(1)}, bf16[9,8,1024]{2,1,0:T(8,128)(2,1)S(1)}, u32[]{:S(2)}, u32[]{:S(2)}) collective-permute-start(bf16[9,8,1024]{2,1,0:T(8,128)(2,1)S(1)} %collective-permute-done.13.refs_18_), channel_id=1, source_target_pairs={{0,1},{1,0},{2,3},{3,2},{4,5},{5,4},{6,7},{7,6},{8,9},{9,8},{10,11... | collective-permute-start | bytes 442376 | tf_op jit(solution)/shard_map/ppermute | solution.py:107
